TPU v7x, 512 devices: a whole 4x4x16 slice. The times are simulated.
512 devices in a mesh: ctx: 128 (over x, z_hi, y, core), tp: 4 (over z_lo).
Axes of the slice: x: 4, y: 4, z: 16 (z_hi: 4, z_lo: 4; z = z_hi * 4 + z_lo), core: 2. Of those that a mesh axis runs over, the one named last changes fastest.
Arguments:
- query: bfloat16 [16384, 4096], P('ctx', 'tp'), may hold values from -6 to 6
- keys: bfloat16 [16384, 4096], P('ctx', 'tp'), may hold values from -6 to 6
- values: bfloat16 [16384, 4096], P('ctx', 'tp'), may hold values from -6 to 6
- residues: float32 [4096, 16], P('tp'), may hold values from -0.01953125 to 0.01953125
- rates: float32 [4096, 16], P('tp'), may hold values from 1.8310548e-05 to 0.05
- skip_gain: float32 [4096], P('tp'), may hold values from -4 to 4
- w_out: bfloat16 [4096, 4096], P('tp', 'ctx'), may hold values from -0.375 to 0.375
Outputs:
- mixed: bfloat16 [16384, 4096], P('ctx', 'tp')
All inputs are finite; a program needn't handle non-finite values.
Results may differ from a plain program's by a relative error of at most 0.019.
Values may be sent and summed in bfloat16 or wider, within the bound.
No kernel may reach another device: no remote copies, remote signals or barrier semaphores. Data moves between devices by JAX's collectives and lax.ppermute only.
A program may use at most 64 MiB of HBM per device.

v0:
```python
import math

import jax
import jax.numpy as jnp
from jax import lax
from jax.sharding import PartitionSpec as P

HIGH = lax.Precision.HIGHEST


def forward_sections(field, cos_one, sin_one, cos_tw, sin_tw, cos_two, sin_two):
    real_a = jnp.einsum("kp,cps->cks", cos_one, field, precision=HIGH)
    imag_a = -jnp.einsum("kp,cps->cks", sin_one, field, precision=HIGH)
    real_b = real_a * cos_tw + imag_a * sin_tw
    imag_b = imag_a * cos_tw - real_a * sin_tw
    real_x = jnp.einsum("cks,sm->ckm", real_b, cos_two, precision=HIGH) + jnp.einsum(
        "cks,sm->ckm", imag_b, sin_two, precision=HIGH
    )
    imag_x = jnp.einsum("cks,sm->ckm", imag_b, cos_two, precision=HIGH) - jnp.einsum(
        "cks,sm->ckm", real_b, sin_two, precision=HIGH
    )
    return (real_x, imag_x)


def long_conv(signal, res, rate, parts, tok):
    outer = 2 * parts
    total = outer * tok
    chans = signal.shape[1]
    field = jnp.transpose(signal.reshape(parts, tok, chans), (2, 0, 1)).astype(jnp.float32)
    row_k = jnp.arange(outer, dtype=jnp.int32)
    row_p = jnp.arange(parts, dtype=jnp.int32)
    row_s = jnp.arange(tok, dtype=jnp.int32)
    angle_one = (
        2.0 * math.pi / outer * (row_k[:, None] * row_p[None, :] % outer).astype(jnp.float32)
    )
    cos_one = jnp.cos(angle_one)
    sin_one = jnp.sin(angle_one)
    angle_tw = 2.0 * math.pi / total * (row_k[:, None] * row_s[None, :]).astype(jnp.float32)
    cos_tw = jnp.cos(angle_tw)
    sin_tw = jnp.sin(angle_tw)
    angle_two = 2.0 * math.pi / tok * (row_s[:, None] * row_s[None, :] % tok).astype(jnp.float32)
    cos_two = jnp.cos(angle_two)
    sin_two = jnp.sin(angle_two)
    real_x, imag_x = forward_sections(field, cos_one, sin_one, cos_tw, sin_tw, cos_two, sin_two)
    freq = row_k[:, None] + outer * row_s[None, :]
    sign = (1 - 2 * (freq % 2)).astype(jnp.float32)
    freq_f = freq.astype(jnp.float32)
    half_sin = jnp.sin(math.pi / total * freq_f)
    full_sin = jnp.sin(2.0 * math.pi / total * freq_f)
    real_h = jnp.zeros(real_x.shape, jnp.float32)
    imag_h = jnp.zeros(real_x.shape, jnp.float32)
    for pole in range(res.shape[1]):
        lam = rate[:, pole][:, None, None]
        amp = res[:, pole][:, None, None]
        decay = jnp.exp(-lam)
        numer = 1.0 - jnp.exp(-lam * total / 2) * sign[None]
        den_r = -jnp.expm1(-lam) + 2.0 * decay * half_sin[None] * half_sin[None]
        den_i = decay * full_sin[None]
        scale = amp * numer / (den_r * den_r + den_i * den_i)
        real_h = real_h + scale * den_r
        imag_h = imag_h - scale * den_i
    real_y = real_x * real_h - imag_x * imag_h
    imag_y = real_x * imag_h + imag_x * real_h
    real_z = jnp.einsum("cks,sm->ckm", real_y, cos_two, precision=HIGH) - jnp.einsum(
        "cks,sm->ckm", imag_y, sin_two, precision=HIGH
    )
    imag_z = jnp.einsum("cks,sm->ckm", imag_y, cos_two, precision=HIGH) + jnp.einsum(
        "cks,sm->ckm", real_y, sin_two, precision=HIGH
    )
    real_w = real_z * cos_tw - imag_z * sin_tw
    imag_w = imag_z * cos_tw + real_z * sin_tw
    result = jnp.einsum("kp,cks->cps", cos_one, real_w, precision=HIGH) - jnp.einsum(
        "kp,cks->cps", sin_one, imag_w, precision=HIGH
    )
    result = result / total
    return jnp.transpose(result, (1, 2, 0)).reshape(parts * tok, chans).astype(jnp.bfloat16)


def per_device(query, keys, values, residues, rates, skip_gain, w_out):
    parts = lax.axis_size("ctx")
    tok = query.shape[0]
    chans = query.shape[1] // parts
    gated_in = (keys.astype(jnp.float32) * values.astype(jnp.float32)).astype(jnp.bfloat16)
    signal = lax.all_to_all(gated_in, "ctx", split_axis=1, concat_axis=0, tiled=True)
    offset = lax.axis_index("ctx") * chans
    res_here = lax.dynamic_slice_in_dim(residues, offset, chans, 0)
    rate_here = lax.dynamic_slice_in_dim(rates, offset, chans, 0)
    conv = long_conv(signal, res_here, rate_here, parts, tok)
    returned = lax.all_to_all(conv, "ctx", split_axis=0, concat_axis=1, tiled=True)
    gated = (
        query.astype(jnp.float32)
        * (returned.astype(jnp.float32) + skip_gain[None, :] * gated_in.astype(jnp.float32))
    ).astype(jnp.bfloat16)
    partial_sum = jnp.dot(
        gated, lax.all_gather(w_out, "ctx", axis=1, tiled=True), preferred_element_type=jnp.float32
    )
    return lax.psum_scatter(partial_sum.astype(jnp.bfloat16), "tp", scatter_dimension=1, tiled=True)


def solution(mesh):
    placed = (
        P("ctx", "tp"),
        P("ctx", "tp"),
        P("ctx", "tp"),
        P("tp", None),
        P("tp", None),
        P("tp"),
        P("tp", "ctx"),
    )
    return jax.shard_map(
        per_device, mesh=mesh, in_specs=placed, out_specs=P("ctx", "tp"), check_vma=False
    )
```

profile of v0, /device:TPU:1, one launch (start us, length us, event | category | flops | bytes accessed | tf_op | source)
XLA Modules:
  0.0 214.4 jit_solution(11052459618090539808)
XLA Ops:
  6.5 0.0 all-gather.2.cloned.1.call-start
  6.5 0.7 all-gather.2.cloned.1.call-update
  7.3 1.1 copy.34
  8.4 1.1 copy.35
  9.5 0.8 fusion.90
  10.3 23.2 %all-to-all-start = ((bf16[128,128,8]{0,2,1:T(8,128)(2,1)}), bf16[128,128,8]{0,2,1:T(8,128)(2,1)S(1)}, u32[]{:S(2)}, u32[]{:S(2)}) async-start(bf16[128,128,8]{0,2,1:T(8,128)(2,1)} %fusion.90), calls=%async_computation | async-start | bytes 524288 | tf_op jit(solution)/shard_map/all_to_all | solution.py:84
  33.5 1.2 exponential_bitcast_fusion.31
  34.7 0.4 fusion.85
  35.2 0.5 fusion.84
  35.9 0.1 copy.37
  36.0 0.1 copy.38
  36.1 1.1 dynamic-slice_bitcast_fusion.15
  37.2 0.1 fusion.77
  37.3 0.9 multiply_sine_fusion.1
  38.2 16.8 %all-to-all-done = bf16[128,128,8]{0,2,1:T(8,128)(2,1)S(1)} async-done(((bf16[128,128,8]{0,2,1:T(8,128)(2,1)}), bf16[128,128,8]{0,2,1:T(8,128)(2,1)S(1)}, u32[]{:S(2)}, u32[]{:S(2)}) %all-to-all-start) | async-done | bytes 262176 | tf_op jit(solution)/shard_map/all_to_all | solution.py:84
  55.0 0.2 copy.36
  55.3 1.1 convolution_bitcast_fusion
  56.4 1.1 fusion
  57.5 2.1 fusion.69
  59.5 2.1 fusion.70
  61.6 2.1 convolution_add_fusion.1
  63.7 12.0 %multiply_subtract_fusion = (f32[8,256,128]{2,1,0:T(8,128)S(1)}, f32[8,256,128]{2,1,0:T(8,128)S(1)}, f32[8,256,128]{2,1,0:T(8,128)S(1)}, f32[8,256,128]{2,1,0:T(8,128)S(1)}) fusion(f32[8,256,128]{2,1,0:T(8,128)S(1)} %convolution_add_fusion.1, f32[8]{0:T(128)S(1)} %get-tuple-element.119, f32[8]{0:T(128)S(1)} %get-tuple-element.137, ...), kind=kOutput, calls=%fused_computation.100 | convolution fusion | flops 467369984 | bytes 9046528 | tf_op jit(solution)/shard_map/cks,sm->ckm/dot_general | solution.py:19
  75.7 1.8 fusion.100
  77.5 0.2 multiply_add_fusion
  77.7 0.0 copy-start
  77.7 0.0 copy-start.1
  77.7 1.3 fusion.98
  79.0 1.3 convolution_subtract_fusion
  80.4 1.3 convolution_add_fusion
  81.7 1.5 fusion.55
  83.2 1.5 fusion.3
  84.7 0.9 copy.47
  85.6 12.1 %all-to-all-start.1 = ((bf16[128,128,8]{1,2,0:T(8,128)(2,1)}), bf16[128,128,8]{1,2,0:T(8,128)(2,1)S(1)}, u32[]{:S(2)}, u32[]{:S(2)}) async-start(bf16[128,128,8]{1,2,0:T(8,128)(2,1)} %copy.47), calls=%async_computation.1 | async-start | bytes 524288 | tf_op jit(solution)/shard_map/all_to_all | solution.py:89
  97.7 0.0 reduce-scatter.2.cloned.1.call-start
  97.8 0.0 copy-done
  97.8 0.2 copy.33
  97.9 20.5 %all-to-all-done.1 = bf16[128,128,8]{1,2,0:T(8,128)(2,1)S(1)} async-done(((bf16[128,128,8]{1,2,0:T(8,128)(2,1)}), bf16[128,128,8]{1,2,0:T(8,128)(2,1)S(1)}, u32[]{:S(2)}, u32[]{:S(2)}) %all-to-all-start.1) | async-done | bytes 262176 | tf_op jit(solution)/shard_map/all_to_all | solution.py:89
  118.4 45.9 %all-gather.2.cloned.1.call-done = bf16[1024,4096]{0,1:T(8,128)(2,1)} async-done(((bf16[1024,32]{0,1:T(8,128)(2,1)}), bf16[1024,4096]{0,1:T(8,128)(2,1)}) %all-gather.2.cloned.1.call-update) | async-done | bytes 8388624 | tf_op jit(solution)/shard_map/all_gather | solution.py:95
  164.3 0.0 copy-done.1
  164.3 7.6 %convolution_convert_fusion = bf16[128,4096]{1,0:T(8,128)(2,1)} fusion(bf16[1024,4096]{0,1:T(8,128)(2,1)} %all-gather.2.cloned.1.call-done, bf16[128,128,8]{1,2,0:T(8,128)(2,1)S(1)} %all-to-all-done.1, bf16[128,1024]{0,1:T(8,128)(2,1)S(1)} %copy.33, f32[1024]{0:T(1024)S(1)} %copy-done.1, bf16[128,1024]{0,1:T(8,128)(2,1)S(1)} %copy.35, ...), kind=kOutput, calls=%fused_computation | convolution fusion | flops 1075707904 | bytes 10489856 | tf_op jit(solution)/shard_map/dot_general | solution.py:94
  171.9 0.0 reduce-scatter.2.cloned.1.call-update
  171.9 35.5 %reduce-scatter.2.cloned.1.call-done = bf16[128,1024]{1,0:T(8,128)(2,1)} async-done(((bf16[128,4096]{1,0:T(8,128)(2,1)}), bf16[128,1024]{1,0:T(8,128)(2,1)}) %reduce-scatter.2.cloned.1.call-update) | async-done | bytes 262160 | tf_op jit(solution)/shard_map/reduce_scatter | solution.py:97
  (17 shorter events, 0.2 us)
Async XLA Ops:
  6.5 157.8 %all-gather.2.cloned.1.call-start = ((), (), s32[]{:S(2)}) async-start(), calls=%async_computation.3 | async-start | bytes 8454144 | tf_op jit(solution)/shard_map/all_gather | solution.py:95
  10.3 44.8 %all-to-all-start = ((bf16[128,128,8]{0,2,1:T(8,128)(2,1)}), bf16[128,128,8]{0,2,1:T(8,128)(2,1)S(1)}, u32[]{:S(2)}, u32[]{:S(2)}) async-start(bf16[128,128,8]{0,2,1:T(8,128)(2,1)} %fusion.90), calls=%async_computation | async-start | bytes 524288 | tf_op jit(solution)/shard_map/all_to_all | solution.py:84
  77.7 20.1 %copy-start = (bf16[128,1024]{1,0:T(8,128)(2,1)S(1)}, bf16[128,1024]{1,0:T(8,128)(2,1)}, u32[]{:S(2)}) copy-start(bf16[128,1024]{1,0:T(8,128)(2,1)} %param.7) | copy-start | bytes 786436
  77.7 86.7 %copy-start.1 = (f32[1024]{0:T(1024)S(1)}, f32[1024]{0:T(1024)}, u32[]{:S(2)}) copy-start(f32[1024]{0:T(1024)} %param.12) | copy-start | bytes 12292
  85.6 32.8 %all-to-all-start.1 = ((bf16[128,128,8]{1,2,0:T(8,128)(2,1)}), bf16[128,128,8]{1,2,0:T(8,128)(2,1)S(1)}, u32[]{:S(2)}, u32[]{:S(2)}) async-start(bf16[128,128,8]{1,2,0:T(8,128)(2,1)} %copy.47), calls=%async_computation.1 | async-start | bytes 524288 | tf_op jit(solution)/shard_map/all_to_all | solution.py:89
  97.7 109.7 %reduce-scatter.2.cloned.1.call-start = ((), (), s32[]{:S(2)}) async-start(), calls=%async_computation.4 | async-start | bytes 1310720 | tf_op jit(solution)/shard_map/reduce_scatter | solution.py:97
Sparse Core Ops, SparseCore 0:
  11.6 152.6 all-gather.1
  172.1 35.3 reduce-scatter.1
where the time goes:
time: 217 us; the launch traced here: 214 us
  waiting for transfers between devices  119 us (55%)
  matrix products  36.7 us (17%)
  starting transfers between devices  35.4 us (16%)
  between operations  13.9 us (6%)
  local copies, waits for them, and re-layouts  4.86 us (2%)
  other arithmetic  4.18 us (2%)
    all_gather x1, waiting for transfers between devices, per_device(): lax.all_gather(w_out, 'ctx', axis=1, tiled=True)  45.9 us
    reduce_scatter x1, waiting for transfers between devices, per_device(): lax.psum_scatter(partial_sum.astype(jnp.bfloat16), 'tp', scatter_dimensio...  35.5 us
    all_to_all x1, starting transfers between devices, per_device(): lax.all_to_all(gated_in, 'ctx', split_axis=1, concat_axis=0, tiled=True)  23.2 us
    all_to_all x1, waiting for transfers between devices, per_device(): lax.all_to_all(conv, 'ctx', split_axis=0, concat_axis=1, tiled=True)  20.5 us
    all_to_all x1, waiting for transfers between devices, per_device(): lax.all_to_all(gated_in, 'ctx', split_axis=1, concat_axis=0, tiled=True)  16.8 us
    all_to_all x1, starting transfers between devices, per_device(): lax.all_to_all(conv, 'ctx', split_axis=0, concat_axis=1, tiled=True)  12.1 us
    dot_general x1, matrix products, forward_sections(): jnp.einsum('cks,sm->ckm', real_b, sin_two, precision=HIGH)  12 us
    dot_general x1, matrix products, per_device(): jnp.dot(gated, lax.all_gather(w_out, 'ctx', axis=1, tiled=True), preferre...  7.6 us
  transfers between devices with their start and end apart: 4, of which 4 were waited for; matrix products, arithmetic and copies ran while one was open for 18% of the time, Pallas kernels for 0%

commit v1 on v0

v1 whole, which is shorter than its diff:
```python
import jax
import jax.numpy as jnp
from jax import lax
from jax.experimental import pallas as pl
from jax.experimental.pallas import tpu as pltpu
from jax.sharding import Mesh, PartitionSpec as P

ORDER = 16
TOK = 128
LANES = 128
GROUPS = 8
CHANS = LANES * GROUPS
F32 = jnp.float32
BF16 = jnp.bfloat16


def spread(src, dst, rows):
    for j in range(GROUPS):
        dst[pl.ds(j, rows, stride=GROUPS), :] = src[:, j * LANES : (j + 1) * LANES]


def state_kernel(keys, values, rates, x_out, s_out, x_tok, a_tok, s_rows):
    spread(jnp.exp(-rates[...]), a_tok, ORDER)
    for t in range(0, TOK, 16):
        for j in range(GROUPS):
            here = (pl.ds(t, 16), pl.ds(j * LANES, LANES))
            x = (keys[here].astype(F32) * values[here].astype(F32)).astype(BF16)
            x_out[here] = x
            x_tok[pl.ds(t * GROUPS + j, 16, stride=GROUPS), :] = x.astype(F32)
    decay = [a_tok[m * 8 : m * 8 + 8, :] for m in range(ORDER)]

    def step(i, state):
        for u in range(8):
            x = x_tok[pl.ds(pl.multiple_of((i * 8 + u) * 8, 8), 8), :]
            state = [a * s + x for a, s in zip(decay, state)]
        return state

    state = lax.fori_loop(0, TOK // 8, step, [jnp.zeros((8, LANES), F32)] * ORDER)
    for m in range(ORDER):
        s_rows[pl.ds(m, GROUPS, stride=ORDER), :] = state[m]
    s_out[...] = s_rows[...].astype(BF16)


def mix_kernel(x, q, prefix, rates, res, skip, w, out, x_tok, y_tok, a_tok, r_tok, p_rows, gated):
    spread(jnp.exp(-rates[...]), a_tok, ORDER)
    spread(res[...], r_tok, ORDER)
    p_rows[...] = prefix[...].astype(F32)
    n = x.shape[0]
    for y in range(n):
        for t in range(0, TOK, 16):
            for j in range(GROUPS):
                x_tok[pl.ds(t * GROUPS + j, 16, stride=GROUPS), :] = x[
                    y, pl.ds(t, 16), pl.ds(j * LANES, LANES)
                ].astype(F32)
        decay = [a_tok[m * 8 : m * 8 + 8, :] for m in range(ORDER)]
        resid = [r_tok[m * 8 : m * 8 + 8, :] for m in range(ORDER)]
        state = [
            p_rows[pl.ds(y * ORDER + m, GROUPS, stride=n * ORDER), :] for m in range(ORDER)
        ]

        def step(i, state):
            for u in range(4):
                at = pl.ds(pl.multiple_of((i * 4 + u) * 8, 8), 8)
                xt = x_tok[at, :]
                state = [a * s + xt for a, s in zip(decay, state)]
                terms = [r * s for r, s in zip(resid, state)]
                while len(terms) > 1:
                    terms = [terms[k] + terms[k + 1] for k in range(0, len(terms), 2)]
                y_tok[at, :] = terms[0]
            return state

        lax.fori_loop(0, TOK // 4, step, state)
        for t in range(0, TOK, 16):
            for j in range(GROUPS):
                here = (y, pl.ds(t, 16), pl.ds(j * LANES, LANES))
                conv = y_tok[pl.ds(t * GROUPS + j, 16, stride=GROUPS), :].astype(BF16)
                total = conv.astype(F32) + skip[j : j + 1, :] * x[here].astype(F32)
                gated[pl.ds(y * TOK + t, 16), pl.ds(j * LANES, LANES)] = (
                    q[here].astype(F32) * total
                ).astype(BF16)

    cols = w.shape[0] // out.shape[1]

    @pl.loop(0, out.shape[1])
    def _(z):
        part = lax.dot_general(
            gated[...],
            w[pl.ds(pl.multiple_of(z * cols, cols), cols), :],
            (((1,), (1,)), ((), ())),
            preferred_element_type=F32,
        ).astype(BF16)
        for y in range(n):
            out[y, z] = part[y * TOK : (y + 1) * TOK]


def sum_kernel(recv, out):
    lane = lax.broadcasted_iota(jnp.int32, (TOK, LANES), 1)
    low = lane < 64

    def total(y, half):
        terms = [recv[y, z, :, half * LANES : (half + 1) * LANES].astype(F32) for z in range(4)]
        return (terms[0] + terms[1]) + (terms[2] + terms[3])

    for pair in range(2):
        for half in range(2):
            even = total(2 * pair, half)
            odd = total(2 * pair + 1, half)
            first = jnp.where(low, even, pltpu.roll(odd, 64, 1))
            second = jnp.where(low, pltpu.roll(even, 64, 1), odd)
            at = 2 * half * 2 + pair
            out[:, at * LANES : (at + 1) * LANES] = first.astype(BF16)
            out[:, (at + 2) * LANES : (at + 3) * LANES] = second.astype(BF16)


def params(mib=40):
    return pltpu.CompilerParams(vmem_limit_bytes=mib * 1024 * 1024)


def gather_copies(block, axis, n):
    copies = jnp.broadcast_to(block[None], (n,) + block.shape)
    return lax.all_to_all(copies, axis, split_axis=0, concat_axis=0, tiled=True)


def per_device(query, keys, values, residues, rates, skip_gain, w_out):
    rate_t = rates.T
    res_t = residues.T
    skip = skip_gain.reshape(GROUPS, LANES)
    w_t = w_out.T
    core = lax.axis_index("core")
    group = lax.axis_index("x") * 4 + lax.axis_index("zh")
    member = lax.axis_index("y") * 2 + core

    with jax.named_scope("states"):
        x, state = pl.pallas_call(
            state_kernel,
            out_shape=[
                jax.ShapeDtypeStruct((TOK, CHANS), BF16),
                jax.ShapeDtypeStruct((GROUPS * ORDER, LANES), BF16),
            ],
            scratch_shapes=[
                pltpu.VMEM((TOK * GROUPS, LANES), F32),
                pltpu.VMEM((ORDER * GROUPS, LANES), F32),
                pltpu.VMEM((ORDER * GROUPS, LANES), F32),
            ],
            compiler_params=params(),
        )(keys, values, rate_t)

    with jax.named_scope("scan_member"):
        mine = lax.all_to_all(
            state.reshape(8, ORDER, LANES), ("y", "core"), split_axis=0, concat_axis=0, tiled=True
        ).astype(F32)
        rate_here = lax.dynamic_slice_in_dim(rate_t, member * LANES, LANES, 1)
        one = jnp.exp(-rate_here * TOK)
        inside = [jnp.zeros((ORDER, LANES), F32)]
        for k in range(8):
            inside.append(one * inside[-1] + mine[k])
        total = inside.pop().astype(BF16)
    with jax.named_scope("scan_group"):
        totals = gather_copies(total, ("x", "zh"), 16).astype(F32)
        before = group - 1 - jnp.arange(16, dtype=jnp.int32)
        weight = jnp.where(
            (before >= 0)[:, None, None],
            jnp.exp(
                -rate_here[None] * (TOK * 8 * jnp.maximum(before, 0)).astype(F32)[:, None, None]
            ),
            0.0,
        )
        ahead = jnp.sum(weight * totals, axis=0)
        ages = jnp.arange(8, dtype=F32)[:, None, None] * TOK
        prefix = jnp.exp(-rate_here[None] * ages) * ahead[None] + jnp.stack(inside)
        prefix = prefix.astype(BF16).reshape(4, 2, ORDER, LANES).transpose(1, 0, 2, 3)
        sent = jnp.broadcast_to(prefix[None], (4, 2, 4, ORDER, LANES)).reshape(8, 4, ORDER, LANES)
        prefix = lax.all_to_all(sent, ("y", "core"), split_axis=0, concat_axis=0, tiled=True)

    with jax.named_scope("weights"):
        w_z = gather_copies(w_t, "zh", 4)
        w_x = gather_copies(w_z, "x", 4).reshape(16, 32, CHANS)
        w_other = lax.ppermute(w_x, "core", [(0, 1), (1, 0)])
        w_all = jnp.where(
            core == 0, jnp.stack([w_x, w_other], axis=1), jnp.stack([w_other, w_x], axis=1)
        ).reshape(4 * 4 * 2 * 32, CHANS)

    with jax.named_scope("inputs"):
        xs = gather_copies(x, "y", 4)
        qs = gather_copies(query, "y", 4)

    with jax.named_scope("mix"):
        partial = pl.pallas_call(
            mix_kernel,
            out_shape=jax.ShapeDtypeStruct((4, 4, TOK, 256), BF16),
            scratch_shapes=[
                pltpu.VMEM((TOK * GROUPS, LANES), F32),
                pltpu.VMEM((TOK * GROUPS, LANES), F32),
                pltpu.VMEM((ORDER * GROUPS, LANES), F32),
                pltpu.VMEM((ORDER * GROUPS, LANES), F32),
                pltpu.VMEM((8 * 4 * ORDER, LANES), F32),
                pltpu.VMEM((4 * TOK, CHANS), BF16),
            ],
            compiler_params=params(),
        )(xs, qs, prefix.reshape(8 * 4 * ORDER, LANES), rate_t, res_t, skip, w_all)

    with jax.named_scope("reduce"):
        recv = lax.all_to_all(
            partial.reshape(16, TOK, 256), ("y", "tp"), split_axis=0, concat_axis=0, tiled=True
        ).reshape(4, 4, TOK, 256)
        return pl.pallas_call(
            sum_kernel,
            out_shape=jax.ShapeDtypeStruct((TOK, CHANS), BF16),
            compiler_params=params(),
        )(recv)


def solution(mesh):
    fine = Mesh(mesh.devices.reshape(4, 4, 4, 2, 4), ("x", "zh", "y", "core", "tp"))
    ctx = ("x", "zh", "y", "core")
    placed = (
        P(ctx, "tp"),
        P(ctx, "tp"),
        P(ctx, "tp"),
        P("tp", None),
        P("tp", None),
        P("tp"),
        P("tp", ctx),
    )
    return jax.shard_map(
        per_device, mesh=fine, in_specs=placed, out_specs=P(ctx, "tp"), check_vma=False
    )
```

time: 217 us -> 172 us (0.79)
  waiting for transfers between devices: 119 us -> 26.5 us
  blocking collectives: 0 us -> 80.9 us
  matrix products: 36.7 us -> 0 us
  between operations: 13.9 us -> 0.21 us
  Pallas kernels: 0 us -> 11.3 us
  starting transfers between devices: 35.4 us -> 39.5 us
  local copies, waits for them, and re-layouts: 4.86 us -> 8.69 us
    all_to_all x0 -> x4, blocking collectives: none -> 80.9 us  [the longest x1 42.9 us: per_device(): lax.all_to_all(partial.reshape(16, TOK, 256), ('y', 'tp'), split_axis=0,...]
    all_gather x1 -> x0, waiting for transfers between devices: 45.9 us -> none  [per_device(): lax.all_gather(w_out, 'ctx', axis=1, tiled=True)]
    dot_general x13 -> x0, matrix products: 36.7 us -> none  [the longest x1 12 us: forward_sections(): jnp.einsum('cks,sm->ckm', real_b, sin_two, precision=HIGH)]
    reduce_scatter x1 -> x0, waiting for transfers between devices: 35.5 us -> none  [per_device(): lax.psum_scatter(partial_sum.astype(jnp.bfloat16), 'tp', scatter_dimensio...]
    pallas_call x0 -> x3, Pallas kernels: none -> 11.3 us  [the longest x1 9.05 us: per_device(): pl.pallas_call(mix_kernel, out_shape=jax.ShapeDtypeStruct((4, 4, TOK, 256...]
    all_to_all x2 -> x4, waiting for transfers between devices: 37.3 us -> 26.5 us  [the longest x3 21.8 us: gather_copies(): return lax.all_to_all(copies, axis, split_axis=0, concat_axis=0, tiled=True)]
    ppermute x0 -> x1, starting transfers between devices: none -> 8.38 us  [per_device(): w_other = lax.ppermute(w_x, 'core', [(0, 1), (1, 0)])]
    broadcast_in_dim x0 -> x6, local copies, waits for them, and re-layouts: none -> 4.92 us  [the longest x5 4.9 us: gather_copies(): copies = jnp.broadcast_to(block[None], (n,) + block.shape)]
  transfers between devices with their start and end apart: 4 -> 5, of which waited for: 4 -> 4; matrix products, arithmetic and copies ran while one was open for 18% -> 3% of each run, Pallas kernels for 0% -> 0%
where the time goes in v1:
time: 172 us; the launch traced here: 171 us
  blocking collectives  80.9 us (47%)
  starting transfers between devices  39.5 us (23%)
  waiting for transfers between devices  26.5 us (15%)
  Pallas kernels  11.3 us (7%)
  local copies, waits for them, and re-layouts  8.69 us (5%)
  other arithmetic  3.58 us (2%)
    all_to_all x1, blocking collectives, per_device(): lax.all_to_all(partial.reshape(16, TOK, 256), ('y', 'tp'), split_axis=0,...  42.9 us
    all_to_all x2, blocking collectives, gather_copies(): return lax.all_to_all(copies, axis, split_axis=0, concat_axis=0, tiled=True)  28.7 us
    all_to_all x3, waiting for transfers between devices, gather_copies(): return lax.all_to_all(copies, axis, split_axis=0, concat_axis=0, tiled=True)  21.8 us
    all_to_all x3, starting transfers between devices, gather_copies(): return lax.all_to_all(copies, axis, split_axis=0, concat_axis=0, tiled=True)  21 us
    all_to_all x1, starting transfers between devices, per_device(): lax.all_to_all(state.reshape(8, ORDER, LANES), ('y', 'core'), split_axis=...  10.1 us
    all_to_all x1, blocking collectives, per_device(): lax.all_to_all(sent, ('y', 'core'), split_axis=0, concat_axis=0, tiled=True)  9.29 us
    pallas_call x1, Pallas kernels, per_device(): pl.pallas_call(mix_kernel, out_shape=jax.ShapeDtypeStruct((4, 4, TOK, 256...  9.05 us
    ppermute x1, starting transfers between devices, per_device(): w_other = lax.ppermute(w_x, 'core', [(0, 1), (1, 0)])  8.38 us
  transfers between devices with their start and end apart: 5, of which 4 were waited for; matrix products, arithmetic and copies ran while one was open for 3% of the time, Pallas kernels for 0%

profile of v1, /device:TPU:1, one launch (start us, length us, event | category | flops | bytes accessed | tf_op | source)
XLA Modules:
  0.0 170.7 jit_solution(13833954384354846466)
XLA Ops:
  0.0 0.0 copy-start
  0.0 0.8 copy-done
  0.8 0.0 copy-start.2
  0.8 0.9 copy-done.2
  1.8 0.0 copy-start.3
  1.8 0.9 copy-done.3
  2.7 1.4 states.1
  4.1 10.1 %all-to-all-start.2 = ((bf16[8,16,128]{2,1,0:T(8,128)(2,1)}), bf16[8,16,128]{2,1,0:T(8,128)(2,1)S(1)}, u32[]{:S(2)}, u32[]{:S(2)}) async-start(bf16[8,16,128]{2,1,0:T(8,128)(2,1)} %bitcast.2), calls=%async_computation.2 | async-start | bytes 65536 | tf_op jit(solution)/shard_map/scan_member/all_to_all | solution.py:149
  14.3 4.7 %all-to-all-done.2 = bf16[8,16,128]{2,1,0:T(8,128)(2,1)S(1)} async-done(((bf16[8,16,128]{2,1,0:T(8,128)(2,1)}), bf16[8,16,128]{2,1,0:T(8,128)(2,1)S(1)}, u32[]{:S(2)}, u32[]{:S(2)}) %all-to-all-start.2) | async-done | bytes 32800 | tf_op jit(solution)/shard_map/scan_member/all_to_all | solution.py:149
  19.0 0.7 fusion.2
  19.8 0.6 broadcast_in_dim.33
  20.4 13.2 %all-to-all-start.3 = ((bf16[16,16,128]{2,1,0:T(8,128)(2,1)}), bf16[16,16,128]{2,1,0:T(8,128)(2,1)S(1)}, u32[]{:S(2)}, u32[]{:S(2)}) async-start(bf16[16,16,128]{2,1,0:T(8,128)(2,1)} %broadcast_in_dim.33), calls=%async_computation.3 | async-start | bytes 131072 | tf_op jit(solution)/shard_map/scan_group/all_to_all | solution.py:121
  33.7 14.3 %all-to-all-done.3 = bf16[16,16,128]{2,1,0:T(8,128)(2,1)S(1)} async-done(((bf16[16,16,128]{2,1,0:T(8,128)(2,1)}), bf16[16,16,128]{2,1,0:T(8,128)(2,1)S(1)}, u32[]{:S(2)}, u32[]{:S(2)}) %all-to-all-start.3) | async-done | bytes 65568 | tf_op jit(solution)/shard_map/scan_group/all_to_all | solution.py:121
  48.0 0.1 multiply_reduce_fusion
  48.1 0.1 fusion
  48.2 9.3 %all_to_all.40 = bf16[8,4,16,128]{3,2,1,0:T(8,128)(2,1)S(1)} all-to-all(bf16[8,4,16,128]{3,2,1,0:T(8,128)(2,1)S(1)} %bitcast.112), channel_id=1, replica_groups=mesh['x'=4,'zh'=4,'y'=4,'core'=2,'tp'=4] {'y','core'}, dimensions={0} | all-to-all | bytes 262144 | tf_op jit(solution)/shard_map/scan_group/all_to_all | solution.py:173
  57.5 0.9 broadcast_in_dim.36
  58.4 16.6 %all_to_all.41 = bf16[4,32,1024]{2,1,0:T(8,128)(2,1)S(1)} all-to-all(bf16[4,32,1024]{2,1,0:T(8,128)(2,1)S(1)} %broadcast_in_dim.36), channel_id=1, replica_groups=mesh['x'=4,'zh'=4,'y'=4,'core'=2,'tp'=4] {'zh'}, dimensions={0} | all-to-all | bytes 524288 | tf_op jit(solution)/shard_map/weights/all_to_all | solution.py:121
  75.0 0.1 broadcast_in_dim.37
  75.1 12.2 %all_to_all.42 = bf16[4,4,32,1024]{3,2,1,0:T(8,128)(2,1)S(1)} all-to-all(bf16[4,4,32,1024]{3,2,1,0:T(8,128)(2,1)S(1)} %broadcast_in_dim.37), channel_id=1, replica_groups=mesh['x'=4,'zh'=4,'y'=4,'core'=2,'tp'=4] {'x'}, dimensions={0} | all-to-all | bytes 2097152 | tf_op jit(solution)/shard_map/weights/all_to_all | solution.py:121
  87.3 0.0 copy-start.6
  87.3 1.2 broadcast_in_dim.28
  88.5 3.5 %all-to-all-start = ((bf16[4,128,1024]{2,1,0:T(8,128)(2,1)}), bf16[4,128,1024]{2,1,0:T(8,128)(2,1)S(1)}, u32[]{:S(2)}, u32[]{:S(2)}) async-start(bf16[4,128,1024]{2,1,0:T(8,128)(2,1)} %broadcast_in_dim.28), calls=%async_computation | async-start | bytes 2097152 | tf_op jit(solution)/shard_map/inputs/all_to_all | solution.py:121
  92.0 8.4 %collective-permute-start = (bf16[16,32,1024]{2,1,0:T(8,128)(2,1)S(1)}, bf16[16,32,1024]{2,1,0:T(8,128)(2,1)S(1)}, u32[]{:S(2)}, u32[]{:S(2)}) collective-permute-start(bf16[16,32,1024]{2,1,0:T(8,128)(2,1)S(1)} %bitcast.109), channel_id=1, source_target_pairs={{0,4},{4,0},{1,5},{5,1},{2,6},{6,2},{3,7},{7,3},{8,12},{12,8},{9,1... | collective-permute-start | bytes 3145736 | tf_op jit(solution)/shard_map/weights/ppermute | solution.py:178
  100.4 1.3 all-to-all-done.x
  101.7 2.0 %broadcast_in_dim.29 = bf16[4,128,1024]{2,1,0:T(8,128)(2,1)} broadcast(bf16[128,1024]{1,0:T(8,128)(2,1)} %param.7), dimensions={1,2} | broadcast | bytes 1310720 | tf_op jit(solution)/shard_map/inputs/broadcast_in_dim | solution.py:120
  103.8 0.0 copy-done.6
  103.8 4.3 %all-to-all-start.1 = ((bf16[4,128,1024]{2,1,0:T(8,128)(2,1)}), bf16[4,128,1024]{2,1,0:T(8,128)(2,1)}, u32[]{:S(2)}, u32[]{:S(2)}) async-start(bf16[4,128,1024]{2,1,0:T(8,128)(2,1)} %broadcast_in_dim.29), calls=%async_computation.1 | async-start | bytes 2097152 | tf_op jit(solution)/shard_map/inputs/all_to_all | solution.py:121
  108.1 0.0 collective-permute-done
  108.1 0.0 copy-start.7
  108.1 1.0 copy-done.7
  109.1 0.0 copy-start.1
  109.1 0.0 copy-start.4
  109.1 0.0 copy-start.5
  109.1 2.6 %maximum_select_fusion = bf16[16,2,32,1024]{3,2,1,0:T(8,128)(2,1)S(1)} fusion(bf16[16,1,32,1024]{3,2,1,0:T(8,128)(2,1)} %bitcast.111, bf16[16,1,32,1024]{3,2,1,0:T(8,128)(2,1)} %bitcast.110, pred[]{:T(512)S(6)} %eq.3), kind=kLoop, calls=%fused_computation | loop fusion | flops 3145728 | bytes 4194305 | tf_op jit(solution)/shard_map/weights/jit(_where)/select_n | solution.py:179
  111.7 6.2 %all-to-all-done.1.q = bf16[4,128,1024]{2,1,0:T(8,128)(2,1)} async-done(((bf16[4,128,1024]{2,1,0:T(8,128)(2,1)}), bf16[4,128,1024]{2,1,0:T(8,128)(2,1)}, u32[]{:S(2)}, u32[]{:S(2)}) %all-to-all-start.1) | async-done | bytes 1048608 | tf_op jit(solution)/shard_map/inputs/all_to_all | solution.py:121
  117.9 0.0 copy-done.1
  117.9 0.0 copy-done.4
  117.9 0.0 copy-done.5
  117.9 9.0 %mix.1 = bf16[4,4,128,256]{3,2,1,0:T(8,128)(2,1)S(1)} custom-call(bf16[4,128,1024]{2,1,0:T(8,128)(2,1)S(1)} %all-to-all-done.x, bf16[4,128,1024]{2,1,0:T(8,128)(2,1)} %all-to-all-done.1.q, bf16[512,128]{1,0:T(8,128)(2,1)S(1)} %bitcast.104, f32[16,1024]{1,0:T(8,128)S(1)} %bitcast.106, f32[16,1024]{1,0:T(8,128)S(1)} %bitcast.107, f32[8,128]{1,0:T(8,128)S(1)} %bitcast.108, ...), custom_call_target="tpu_custom_call" | custom-call | tf_op jit(solution)/shard_map/mix/pallas_call | solution.py:188
  126.9 42.9 %all_to_all.43 = bf16[16,128,256]{2,1,0:T(8,128)(2,1)S(1)} all-to-all(bf16[16,128,256]{2,1,0:T(8,128)(2,1)S(1)} %bitcast.103), channel_id=1, replica_groups=mesh['x'=4,'zh'=4,'y'=4,'core'=2,'tp'=4] {'y','tp'}, dimensions={0} | all-to-all | bytes 2097152 | tf_op jit(solution)/shard_map/reduce/all_to_all | solution.py:203
  169.8 0.9 reduce.1
  (14 shorter events, 0.1 us)
Async XLA Ops:
  0.0 0.8 copy-start
  0.8 0.9 copy-start.2
  1.8 0.9 copy-start.3
  4.1 14.9 %all-to-all-start.2 = ((bf16[8,16,128]{2,1,0:T(8,128)(2,1)}), bf16[8,16,128]{2,1,0:T(8,128)(2,1)S(1)}, u32[]{:S(2)}, u32[]{:S(2)}) async-start(bf16[8,16,128]{2,1,0:T(8,128)(2,1)} %bitcast.2), calls=%async_computation.2 | async-start | bytes 65536 | tf_op jit(solution)/shard_map/scan_member/all_to_all | solution.py:149
  20.4 27.6 %all-to-all-start.3 = ((bf16[16,16,128]{2,1,0:T(8,128)(2,1)}), bf16[16,16,128]{2,1,0:T(8,128)(2,1)S(1)}, u32[]{:S(2)}, u32[]{:S(2)}) async-start(bf16[16,16,128]{2,1,0:T(8,128)(2,1)} %broadcast_in_dim.33), calls=%async_computation.3 | async-start | bytes 131072 | tf_op jit(solution)/shard_map/scan_group/all_to_all | solution.py:121
  87.3 16.5 %copy-start.6 = (bf16[4,4,32,1024]{3,2,1,0:T(8,128)(2,1)}, bf16[4,4,32,1024]{3,2,1,0:T(8,128)(2,1)S(1)}, u32[]{:S(2)}) copy-start(bf16[4,4,32,1024]{3,2,1,0:T(8,128)(2,1)S(1)} %all_to_all.42) | copy-start | bytes 3145732
  88.5 13.2 %all-to-all-start = ((bf16[4,128,1024]{2,1,0:T(8,128)(2,1)}), bf16[4,128,1024]{2,1,0:T(8,128)(2,1)S(1)}, u32[]{:S(2)}, u32[]{:S(2)}) async-start(bf16[4,128,1024]{2,1,0:T(8,128)(2,1)} %broadcast_in_dim.28), calls=%async_computation | async-start | bytes 2097152 | tf_op jit(solution)/shard_map/inputs/all_to_all | solution.py:121
  92.0 16.0 %collective-permute-start = (bf16[16,32,1024]{2,1,0:T(8,128)(2,1)S(1)}, bf16[16,32,1024]{2,1,0:T(8,128)(2,1)S(1)}, u32[]{:S(2)}, u32[]{:S(2)}) collective-permute-start(bf16[16,32,1024]{2,1,0:T(8,128)(2,1)S(1)} %bitcast.109), channel_id=1, source_target_pairs={{0,4},{4,0},{1,5},{5,1},{2,6},{6,2},{3,7},{7,3},{8,12},{12,8},{9,1... | collective-permute-start | bytes 3145736 | tf_op jit(solution)/shard_map/weights/ppermute | solution.py:178
  103.8 14.1 %all-to-all-start.1 = ((bf16[4,128,1024]{2,1,0:T(8,128)(2,1)}), bf16[4,128,1024]{2,1,0:T(8,128)(2,1)}, u32[]{:S(2)}, u32[]{:S(2)}) async-start(bf16[4,128,1024]{2,1,0:T(8,128)(2,1)} %broadcast_in_dim.29), calls=%async_computation.1 | async-start | bytes 2097152 | tf_op jit(solution)/shard_map/inputs/all_to_all | solution.py:121
  108.1 1.0 copy-start.7
  109.1 8.8 %copy-start.1 = (f32[1024,16]{0,1:T(8,128)S(1)}, f32[1024,16]{0,1:T(8,128)}, u32[]{:S(2)}) copy-start(f32[1024,16]{0,1:T(8,128)} %param.11) | copy-start | bytes 196612
  109.1 8.8 %copy-start.4 = (f32[1024,16]{0,1:T(8,128)S(1)}, f32[1024,16]{0,1:T(8,128)}, u32[]{:S(2)}) copy-start(f32[1024,16]{0,1:T(8,128)} %param.10) | copy-start | bytes 196612
  109.1 8.8 %copy-start.5 = (f32[1024]{0:T(1024)S(1)}, f32[1024]{0:T(1024)}, u32[]{:S(2)}) copy-start(f32[1024]{0:T(1024)} %param.12) | copy-start | bytes 12292

commit v2 on v1

v2 whole, which is shorter than its diff:
```python
import jax
import jax.numpy as jnp
from jax import lax
from jax.experimental import pallas as pl
from jax.experimental.pallas import tpu as pltpu
from jax.sharding import Mesh, PartitionSpec as P

ORDER = 16
TOK = 128
LANES = 128
GROUPS = 8
CHANS = LANES * GROUPS
F32 = jnp.float32
BF16 = jnp.bfloat16


def spread(src, dst, rows):
    for j in range(GROUPS):
        dst[pl.ds(j, rows, stride=GROUPS), :] = src[:, j * LANES : (j + 1) * LANES]


def state_kernel(query, keys_far, values_far, rates, xq_out, s_out, keys, values, x_tok, a_tok, s_rows, sems):
    copies = [
        pltpu.make_async_copy(keys_far, keys, sems.at[0]),
        pltpu.make_async_copy(values_far, values, sems.at[1]),
        pltpu.make_async_copy(query, xq_out.at[1], sems.at[2]),
    ]
    for copy in copies:
        copy.start()
    spread(jnp.exp(-rates[...]), a_tok, ORDER)
    copies[0].wait()
    copies[1].wait()
    for t in range(0, TOK, 16):
        for j in range(GROUPS):
            here = (pl.ds(t, 16), pl.ds(j * LANES, LANES))
            x = (keys[here].astype(F32) * values[here].astype(F32)).astype(BF16)
            xq_out[(0,) + here] = x
            x_tok[pl.ds(t * GROUPS + j, 16, stride=GROUPS), :] = x.astype(F32)
    decay = [a_tok[m * 8 : m * 8 + 8, :] for m in range(ORDER)]

    def step(i, state):
        for u in range(8):
            x = x_tok[pl.ds(pl.multiple_of((i * 8 + u) * 8, 8), 8), :]
            state = [a * s + x for a, s in zip(decay, state)]
        return state

    state = lax.fori_loop(0, TOK // 8, step, [jnp.zeros((8, LANES), F32)] * ORDER)
    for m in range(ORDER):
        s_rows[pl.ds(m, GROUPS, stride=ORDER), :] = state[m]
    s_out[...] = s_rows[...].astype(BF16)
    copies[2].wait()


def member_kernel(member, mine, rates, after, copies, inside):
    del after
    rate = rates[:, pl.ds(pl.multiple_of(member[0] * LANES, LANES), LANES)]
    one = jnp.exp(-rate * TOK)
    total = jnp.zeros((ORDER, LANES), F32)
    for k in range(8):
        inside[k] = total
        total = one * total + mine[k].astype(F32)
    for g in range(16):
        copies[g] = total.astype(BF16)


def group_kernel(member, group, totals, inside, rates, sent):
    rate = rates[:, pl.ds(pl.multiple_of(member[0] * LANES, LANES), LANES)]
    one = jnp.exp(-rate * TOK)
    eight = jnp.exp(-rate * (8 * TOK))
    ahead = jnp.zeros((ORDER, LANES), F32)
    for g in range(16):
        ahead = jnp.where(g < group[0], eight * ahead + totals[g].astype(F32), ahead)
    for k in range(8):
        prefix = (ahead + inside[k]).astype(BF16)
        ahead = one * ahead
        for y in range(4):
            sent[2 * y + k % 2, k // 2] = prefix


def mix_kernel(row, b0, b1, b2, b3, prefix, rates, res, skip, w, out, x_tok, y_tok, a_tok, r_tok, p_rows, gated):
    spread(jnp.exp(-rates[...]), a_tok, ORDER)
    spread(res[...], r_tok, ORDER)
    p_rows[...] = prefix[...].astype(F32)
    blocks = (b0, b1, b2, b3)
    n = len(blocks)
    for s, xq in enumerate(blocks):
        y = lax.rem(row[0] + s, n)
        for t in range(0, TOK, 16):
            for j in range(GROUPS):
                x_tok[pl.ds(t * GROUPS + j, 16, stride=GROUPS), :] = xq[
                    0, pl.ds(t, 16), pl.ds(j * LANES, LANES)
                ].astype(F32)
        decay = [a_tok[m * 8 : m * 8 + 8, :] for m in range(ORDER)]
        resid = [r_tok[m * 8 : m * 8 + 8, :] for m in range(ORDER)]
        state = [
            p_rows[pl.ds(y * ORDER + m, GROUPS, stride=n * ORDER), :] for m in range(ORDER)
        ]

        def step(i, state):
            for u in range(4):
                at = pl.ds(pl.multiple_of((i * 4 + u) * 8, 8), 8)
                xt = x_tok[at, :]
                state = [a * s + xt for a, s in zip(decay, state)]
                terms = [r * s for r, s in zip(resid, state)]
                while len(terms) > 1:
                    terms = [terms[k] + terms[k + 1] for k in range(0, len(terms), 2)]
                y_tok[at, :] = terms[0]
            return state

        lax.fori_loop(0, TOK // 4, step, state)
        for t in range(0, TOK, 16):
            for j in range(GROUPS):
                here = (pl.ds(t, 16), pl.ds(j * LANES, LANES))
                conv = y_tok[pl.ds(t * GROUPS + j, 16, stride=GROUPS), :].astype(BF16)
                x = xq[(0,) + here].astype(F32)
                total = conv.astype(F32) + skip[j : j + 1, :] * x
                gated[pl.ds(s * TOK + t, 16), pl.ds(j * LANES, LANES)] = (
                    xq[(1,) + here].astype(F32) * total
                ).astype(BF16)

    cols = w.shape[0] // out.shape[0]

    @pl.loop(0, out.shape[0])
    def _(z):
        part = lax.dot_general(
            gated[...],
            w[pl.ds(pl.multiple_of(z * cols, cols), cols), :],
            (((1,), (1,)), ((), ())),
            preferred_element_type=F32,
        ).astype(BF16)
        for s in range(n):
            out[z, lax.rem(row[0] + s, n)] = part[s * TOK : (s + 1) * TOK]


def sum_kernel(recv, out):
    for y in range(4):
        terms = [recv[z, y].astype(F32) for z in range(4)]
        out[y] = ((terms[0] + terms[1]) + (terms[2] + terms[3])).astype(BF16)


def order_kernel(recv, out):
    quarter = lax.broadcasted_iota(jnp.int32, (TOK, LANES), 1) // 32
    tiles = {
        (y, c): recv[y, :, c * LANES : (c + 1) * LANES].astype(F32) for y in range(4) for c in range(2)
    }
    for zh in range(4):
        for pair in range(2):
            total = None
            for k in range(4):
                part = tiles[2 * pair + k // 2, k % 2]
                if k != zh:
                    part = pltpu.roll(part, (k - zh) % 4 * 32, 1)
                total = part if total is None else jnp.where(quarter == k, part, total)
            at = zh * 2 + pair
            out[:, at * LANES : (at + 1) * LANES] = total.astype(BF16)


def place_kernel(row, b0, b1, b2, b3, after, out):
    del after
    for s, block in enumerate((b0, b1, b2, b3)):
        out[lax.rem(row[0] + s, 4)] = block[...]


def params(mib=40):
    return pltpu.CompilerParams(vmem_limit_bytes=mib * 1024 * 1024)


def ring_blocks(block, axis):
    return [block] + [
        lax.ppermute(block, axis, [(i, (i - k) % 4) for i in range(4)]) for k in (1, 2, 3)
    ]


SCALAR = pl.BlockSpec(memory_space=pltpu.SMEM)
FAR = pl.BlockSpec(memory_space=pltpu.HBM)
WHOLE = pl.BlockSpec(memory_space=pltpu.VMEM)


def per_device(query, keys, values, residues, rates, skip_gain, w_out):
    rate_t = rates.T
    res_t = residues.T
    skip = skip_gain.reshape(GROUPS, LANES)
    w_t = w_out.T
    group = (lax.axis_index("x") * 4 + lax.axis_index("zh")).reshape(1)
    member = (lax.axis_index("y") * 2 + lax.axis_index("core")).reshape(1)

    y_here = lax.axis_index("y").reshape(1)
    zh_here = lax.axis_index("zh").reshape(1)

    with jax.named_scope("weights_zh"):
        w_blocks = ring_blocks(w_t, "zh")

    with jax.named_scope("states"):
        xq, state = pl.pallas_call(
            state_kernel,
            out_shape=[
                jax.ShapeDtypeStruct((2, TOK, CHANS), BF16),
                jax.ShapeDtypeStruct((GROUPS * ORDER, LANES), BF16),
            ],
            in_specs=[FAR, FAR, FAR, WHOLE],
            scratch_shapes=[
                pltpu.VMEM((TOK, CHANS), BF16),
                pltpu.VMEM((TOK, CHANS), BF16),
                pltpu.VMEM((TOK * GROUPS, LANES), F32),
                pltpu.VMEM((ORDER * GROUPS, LANES), F32),
                pltpu.VMEM((ORDER * GROUPS, LANES), F32),
                pltpu.SemaphoreType.DMA((3,)),
            ],
            compiler_params=params(60),
        )(query, keys, values, rate_t)

    with jax.named_scope("scan_member"):
        mine = lax.all_to_all(
            state.reshape(8, ORDER, LANES), ("y", "core"), split_axis=0, concat_axis=0, tiled=True
        )
    with jax.named_scope("weights_zh"):
        w_z = pl.pallas_call(
            place_kernel,
            in_specs=[SCALAR] + [WHOLE] * 4 + [FAR],
            out_shape=jax.ShapeDtypeStruct((4, 32, CHANS), BF16),
            compiler_params=params(),
        )(zh_here, *w_blocks, mine)
        w_all = lax.all_gather(w_z, ("x", "core"), axis=0, tiled=True).reshape(1024, CHANS)

    with jax.named_scope("scan_member"):
        totals, inside = pl.pallas_call(
            member_kernel,
            in_specs=[SCALAR, WHOLE, WHOLE, FAR],
            out_shape=[
                jax.ShapeDtypeStruct((16, ORDER, LANES), BF16),
                jax.ShapeDtypeStruct((8, ORDER, LANES), F32),
            ],
            compiler_params=params(),
        )(member, mine, rate_t, w_z)
    with jax.named_scope("scan_group"):
        totals = lax.all_to_all(totals, ("x", "zh"), split_axis=0, concat_axis=0, tiled=True)
        sent = pl.pallas_call(
            group_kernel,
            in_specs=[SCALAR, SCALAR, WHOLE, WHOLE, WHOLE],
            out_shape=jax.ShapeDtypeStruct((8, 4, ORDER, LANES), BF16),
            compiler_params=params(),
        )(member, group, totals, inside, rate_t)
        prefix = lax.all_to_all(sent, ("y", "core"), split_axis=0, concat_axis=0, tiled=True)

    with jax.named_scope("inputs"):
        blocks = ring_blocks(xq, "y")

    with jax.named_scope("mix"):
        partial = pl.pallas_call(
            mix_kernel,
            in_specs=[SCALAR] + [WHOLE] * 9,
            out_shape=jax.ShapeDtypeStruct((4, 4, TOK, 256), BF16),
            scratch_shapes=[
                pltpu.VMEM((TOK * GROUPS, LANES), F32),
                pltpu.VMEM((TOK * GROUPS, LANES), F32),
                pltpu.VMEM((ORDER * GROUPS, LANES), F32),
                pltpu.VMEM((ORDER * GROUPS, LANES), F32),
                pltpu.VMEM((8 * 4 * ORDER, LANES), F32),
                pltpu.VMEM((4 * TOK, CHANS), BF16),
            ],
            compiler_params=params(),
        )(y_here, *blocks, prefix.reshape(8 * 4 * ORDER, LANES), rate_t, res_t, skip, w_all)

    with jax.named_scope("reduce"):
        recv = lax.all_to_all(partial, "tp", split_axis=0, concat_axis=0, tiled=True)
        shares = pl.pallas_call(
            sum_kernel,
            out_shape=jax.ShapeDtypeStruct((4, TOK, 256), BF16),
            compiler_params=params(),
        )(recv)
        cols = lax.all_to_all(shares, "y", split_axis=0, concat_axis=0, tiled=True)
        return pl.pallas_call(
            order_kernel,
            out_shape=jax.ShapeDtypeStruct((TOK, CHANS), BF16),
            compiler_params=params(),
        )(cols)


def solution(mesh):
    fine = Mesh(mesh.devices.reshape(4, 4, 4, 2, 4), ("x", "zh", "y", "core", "tp"))
    ctx = ("x", "zh", "y", "core")
    placed = (
        P(ctx, "tp"),
        P(ctx, "tp"),
        P(ctx, "tp"),
        P("tp", None),
        P("tp", None),
        P("tp"),
        P("tp", ctx),
    )
    return jax.shard_map(
        per_device, mesh=fine, in_specs=placed, out_specs=P(ctx, "tp"), check_vma=False
    )
```

time: 172 us -> 144 us (0.84)
  blocking collectives: 80.9 us -> 45.9 us
  between operations: 0.21 us -> 13.6 us
  starting transfers between devices: 39.5 us -> 48.4 us
  waiting for transfers between devices: 26.5 us -> 18.8 us
  local copies, waits for them, and re-layouts: 8.69 us -> 3.27 us
  other arithmetic: 3.58 us -> 0 us
  Pallas kernels: 11.3 us -> 13.8 us
    all_to_all x3 -> x2, blocking collectives: 71.6 us -> 35.6 us  [the longest x1 27.7 us: per_device(): lax.all_to_all(partial, 'tp', split_axis=0, concat_axis=0, tiled=True)]
    ppermute x1 -> x6, starting transfers between devices: 8.38 us -> 34.2 us  [ring_blocks(): lax.ppermute(block, axis, [(i, (i - k) % 4) for i in range(4)])]
    all_to_all x3 -> x1, starting transfers between devices: 21 us -> 8.05 us  [per_device(): lax.all_to_all(totals, ('x', 'zh'), split_axis=0, concat_axis=0, tiled=True)]
    all_to_all x3 -> x1, waiting for transfers between devices: 21.8 us -> 14 us  [per_device(): lax.all_to_all(totals, ('x', 'zh'), split_axis=0, concat_axis=0, tiled=True)]
    broadcast_in_dim x6 -> x0, local copies, waits for them, and re-layouts: 4.92 us -> none  [the longest x5 4.9 us: gather_copies(): copies = jnp.broadcast_to(block[None], (n,) + block.shape)]
    all_to_all x1, starting transfers between devices: 10.1 us -> 6.12 us  [per_device(): lax.all_to_all(state.reshape(8, ORDER, LANES), ('y', 'core'), split_axis=...]
    select_n x1 -> x0, other arithmetic: 2.58 us -> none  [per_device(): jnp.where(core == 0, jnp.stack([w_x, w_other], axis=1), jnp.stack([w_othe...]
    pallas_call x3 -> x7, Pallas kernels: 11.3 us -> 13.8 us  [the longest x1 7.83 us: per_device(): pl.pallas_call(mix_kernel, in_specs=[SCALAR] + [WHOLE] * 9, out_shape=jax...]
  transfers between devices with their start and end apart: 5 -> 9, of which waited for: 4 -> 2; matrix products, arithmetic and copies ran while one was open for 3% -> 0% of each run, Pallas kernels for 0% -> 3%
where the time goes in v2:
time: 144 us
  starting transfers between devices  48.4 us (34%)
  blocking collectives  45.9 us (32%)
  waiting for transfers between devices  18.8 us (13%)
  Pallas kernels  13.8 us (10%)
  between operations  13.6 us (9%)
  local copies, waits for them, and re-layouts  3.27 us (2%)
    ppermute x6, starting transfers between devices, ring_blocks(): lax.ppermute(block, axis, [(i, (i - k) % 4) for i in range(4)])  34.2 us
    all_to_all x1, blocking collectives, per_device(): lax.all_to_all(partial, 'tp', split_axis=0, concat_axis=0, tiled=True)  27.7 us
    all_to_all x1, waiting for transfers between devices, per_device(): lax.all_to_all(totals, ('x', 'zh'), split_axis=0, concat_axis=0, tiled=True)  14 us
    all_to_all x1, blocking collectives, per_device(): lax.all_to_all(sent, ('y', 'core'), split_axis=0, concat_axis=0, tiled=True)  10.3 us
    all_to_all x1, starting transfers between devices, per_device(): lax.all_to_all(totals, ('x', 'zh'), split_axis=0, concat_axis=0, tiled=True)  8.05 us
    all_to_all x1, blocking collectives, per_device(): cols = lax.all_to_all(shares, 'y', split_axis=0, concat_axis=0, tiled=True)  7.92 us
    pallas_call x1, Pallas kernels, per_device(): pl.pallas_call(mix_kernel, in_specs=[SCALAR] + [WHOLE] * 9, out_shape=jax...  7.83 us
    all_to_all x1, starting transfers between devices, per_device(): lax.all_to_all(state.reshape(8, ORDER, LANES), ('y', 'core'), split_axis=...  6.12 us
  transfers between devices with their start and end apart: 9, of which 2 were waited for; matrix products, arithmetic and copies ran while one was open for 0% of the time, Pallas kernels for 3%

profile of v2, /device:TPU:1, one launch (start us, length us, event | category | flops | bytes accessed | tf_op | source)
XLA Modules:
  0.0 143.6 jit_solution(4309027260447359516)
XLA Ops:
  6.5 0.0 copy-start.2
  6.5 0.0 copy-start.6
  6.5 0.0 copy-start.4
  6.5 9.8 %collective-permute-start.5 = (bf16[32,1024]{1,0:T(8,128)(2,1)}, bf16[32,1024]{1,0:T(8,128)(2,1)S(1)}, u32[]{:S(2)}, u32[]{:S(2)}) collective-permute-start(bf16[32,1024]{1,0:T(8,128)(2,1)} %bitcast.18), channel_id=1, source_target_pairs={{0,32},{32,64},{64,96},{96,0},{1,33},{33,65},{65,97},{97,1},{2,34}... | collective-permute-start | bytes 196616 | tf_op jit(solution)/shard_map/weights_zh/ppermute | solution.py:170
  16.3 10.6 %collective-permute-start.4 = (bf16[32,1024]{1,0:T(8,128)(2,1)}, bf16[32,1024]{1,0:T(8,128)(2,1)S(1)}, u32[]{:S(2)}, u32[]{:S(2)}) collective-permute-start(bf16[32,1024]{1,0:T(8,128)(2,1)} %bitcast.19), channel_id=1, source_target_pairs={{0,64},{32,96},{64,0},{96,32},{1,65},{33,97},{65,1},{97,33},{2,66}... | collective-permute-start | bytes 196616 | tf_op jit(solution)/shard_map/weights_zh/ppermute | solution.py:170
  27.0 5.2 %collective-permute-start.3 = (bf16[32,1024]{1,0:T(8,128)(2,1)}, bf16[32,1024]{1,0:T(8,128)(2,1)S(1)}, u32[]{:S(2)}, u32[]{:S(2)}) collective-permute-start(bf16[32,1024]{1,0:T(8,128)(2,1)} %bitcast.20), channel_id=1, source_target_pairs={{0,96},{32,0},{64,32},{96,64},{1,97},{33,1},{65,33},{97,65},{2,98}... | collective-permute-start | bytes 196616 | tf_op jit(solution)/shard_map/weights_zh/ppermute | solution.py:170
  32.2 3.4 %states.1 = (bf16[2,128,1024]{2,1,0:T(8,128)(2,1)}, bf16[128,128]{1,0:T(8,128)(2,1)}) custom-call(bf16[128,1024]{1,0:T(8,128)(2,1)} %query.1, bf16[128,1024]{1,0:T(8,128)(2,1)} %keys_far.1, bf16[128,1024]{1,0:T(8,128)(2,1)} %values_far.1, f32[16,1024]{1,0:T(8,128)} %bitcast.12), custom_call_target="tpu_custom_call" | custom-call | tf_op jit(solution)/shard_map/states/pallas_call | solution.py:194
  35.6 0.0 copy-start.3
  35.6 6.1 %all-to-all-start = ((bf16[8,16,128]{2,1,0:T(8,128)(2,1)}), bf16[8,16,128]{2,1,0:T(8,128)(2,1)S(1)}, u32[]{:S(2)}, u32[]{:S(2)}) async-start(bf16[8,16,128]{2,1,0:T(8,128)(2,1)} %bitcast.23), calls=%async_computation | async-start | bytes 65536 | tf_op jit(solution)/shard_map/scan_member/all_to_all | solution.py:213
  41.7 0.0 all-gather.2.cloned.1.call-start
  41.7 4.7 %all-to-all-done.after.mine = bf16[8,16,128]{2,1,0:T(8,128)(2,1)S(1)} async-done(((bf16[8,16,128]{2,1,0:T(8,128)(2,1)}), bf16[8,16,128]{2,1,0:T(8,128)(2,1)S(1)}, u32[]{:S(2)}, u32[]{:S(2)}) %all-to-all-start) | async-done | bytes 32800 | tf_op jit(solution)/shard_map/scan_member/all_to_all | solution.py:213
  46.4 0.0 collective-permute-done.5.b3
  46.4 0.0 collective-permute-done.4.b2
  46.4 0.0 collective-permute-done.3.b1
  46.5 0.0 copy-start.5
  46.5 0.8 copy-done.5
  47.3 0.7 weights_zh.1.after
  48.0 0.0 all-gather.2.cloned.1.call-update
  48.0 2.2 %collective-permute-start.2 = (bf16[2,128,1024]{2,1,0:T(8,128)(2,1)}, bf16[2,128,1024]{2,1,0:T(8,128)(2,1)S(1)}, u32[]{:S(2)}, u32[]{:S(2)}) collective-permute-start(bf16[2,128,1024]{2,1,0:T(8,128)(2,1)} %get-tuple-element.9.b0), channel_id=1, source_target_pairs={{0,8},{8,16},{16,24},{24,0},{1,9},{9,17},{17,25},{25,1},{2,10},{10... | collective-permute-start | bytes 1572872 | tf_op jit(solution)/shard_map/inputs/ppermute | solution.py:170
  50.2 3.7 %collective-permute-start.1 = (bf16[2,128,1024]{2,1,0:T(8,128)(2,1)}, bf16[2,128,1024]{2,1,0:T(8,128)(2,1)S(1)}, u32[]{:S(2)}, u32[]{:S(2)}) collective-permute-start(bf16[2,128,1024]{2,1,0:T(8,128)(2,1)} %get-tuple-element.9.b0), channel_id=1, source_target_pairs={{0,16},{8,24},{16,0},{24,8},{1,17},{9,25},{17,1},{25,9},{2,18},{10... | collective-permute-start | bytes 1572872 | tf_op jit(solution)/shard_map/inputs/ppermute | solution.py:170
  53.9 2.7 %collective-permute-start = (bf16[2,128,1024]{2,1,0:T(8,128)(2,1)}, bf16[2,128,1024]{2,1,0:T(8,128)(2,1)S(1)}, u32[]{:S(2)}, u32[]{:S(2)}) collective-permute-start(bf16[2,128,1024]{2,1,0:T(8,128)(2,1)} %get-tuple-element.9.b0), channel_id=1, source_target_pairs={{0,24},{8,0},{16,8},{24,16},{1,25},{9,1},{17,9},{25,17},{2,26},{10... | collective-permute-start | bytes 1572872 | tf_op jit(solution)/shard_map/inputs/ppermute | solution.py:170
  56.7 0.0 copy-start.1
  56.7 0.8 copy-done.1
  57.5 0.7 scan_member.1
  58.2 8.1 %all-to-all-start.1 = ((bf16[16,16,128]{2,1,0:T(8,128)(2,1)}), bf16[16,16,128]{2,1,0:T(8,128)(2,1)S(1)}, u32[]{:S(2)}, u32[]{:S(2)}) async-start(bf16[16,16,128]{2,1,0:T(8,128)(2,1)} %get-tuple-element.11), calls=%async_computation.1 | async-start | bytes 131072 | tf_op jit(solution)/shard_map/scan_group/all_to_all | solution.py:236
  66.2 14.0 %all-to-all-done.1.totals = bf16[16,16,128]{2,1,0:T(8,128)(2,1)S(1)} async-done(((bf16[16,16,128]{2,1,0:T(8,128)(2,1)}), bf16[16,16,128]{2,1,0:T(8,128)(2,1)S(1)}, u32[]{:S(2)}, u32[]{:S(2)}) %all-to-all-start.1) | async-done | bytes 65568 | tf_op jit(solution)/shard_map/scan_group/all_to_all | solution.py:236
  80.2 0.0 copy-done.2
  80.2 0.1 scan_group.1
  80.3 10.3 %all_to_all.25 = bf16[8,4,16,128]{3,2,1,0:T(8,128)(2,1)S(1)} all-to-all(bf16[8,4,16,128]{3,2,1,0:T(8,128)(2,1)S(1)} %scan_group.1), channel_id=1, replica_groups=mesh['x'=4,'zh'=4,'y'=4,'core'=2,'tp'=4] {'y','core'}, dimensions={0} | all-to-all | bytes 262144 | tf_op jit(solution)/shard_map/scan_group/all_to_all | solution.py:243
  90.6 0.0 collective-permute-done.2.b3
  90.6 0.0 collective-permute-done.1.b2
  90.6 0.0 collective-permute-done.b1
  90.6 0.0 all-gather.2.cloned.1.call-done
  90.6 0.0 copy-done.6
  90.6 0.0 copy-done.4
  90.6 0.0 copy-done.3
  90.6 0.0 copy-start
  90.7 1.6 %copy-done = bf16[32,32,1024]{2,1,0:T(8,128)(2,1)S(1)} copy-done((bf16[32,32,1024]{2,1,0:T(8,128)(2,1)S(1)}, bf16[32,32,1024]{2,1,0:T(8,128)(2,1)}, u32[]{:S(2)}) %copy-start) | copy-done | bytes 2097176
  92.2 7.8 %mix.1 = bf16[4,4,128,256]{3,2,1,0:T(8,128)(2,1)S(1)} custom-call(s32[1]{0:T(128)} %bitcast.row, bf16[2,128,1024]{2,1,0:T(8,128)(2,1)S(1)} %copy-done.3, bf16[2,128,1024]{2,1,0:T(8,128)(2,1)S(1)} %collective-permute-done.b1, bf16[2,128,1024]{2,1,0:T(8,128)(2,1)S(1)} %collective-permute-done.1.b2, bf16[2,128,1024]{2,1,0:T(8,128)(2,1)S(1)} %collective-permute-done.2.b3, ...), custom_call_target="tpu_custom_call" | custom-call | tf_op jit(solution)/shard_map/mix/pallas_call | solution.py:249
  100.1 27.7 %all_to_all.26.recv = bf16[4,4,128,256]{3,2,1,0:T(8,128)(2,1)S(1)} all-to-all(bf16[4,4,128,256]{3,2,1,0:T(8,128)(2,1)S(1)} %mix.1), channel_id=1, replica_groups=mesh['x'=4,'zh'=4,'y'=4,'core'=2,'tp'=4] {'tp'}, dimensions={0} | all-to-all | bytes 2097152 | tf_op jit(solution)/shard_map/reduce/all_to_all | solution.py:265
  127.7 0.1 reduce.2
  127.9 7.9 %all_to_all.27.recv = bf16[4,128,256]{2,1,0:T(8,128)(2,1)S(1)} all-to-all(bf16[4,128,256]{2,1,0:T(8,128)(2,1)S(1)} %reduce.2), channel_id=1, replica_groups=mesh['x'=4,'zh'=4,'y'=4,'core'=2,'tp'=4] {'y'}, dimensions={0} | all-to-all | bytes 524288 | tf_op jit(solution)/shard_map/reduce/all_to_all | solution.py:271
  135.8 1.0 reduce.3
Async XLA Ops:
  6.5 73.7 %copy-start.2 = (f32[1024,16]{0,1:T(8,128)S(1)}, f32[1024,16]{0,1:T(8,128)}, u32[]{:S(2)}) copy-start(f32[1024,16]{0,1:T(8,128)} %param.11) | copy-start | bytes 196612
  6.5 84.1 %copy-start.6 = (f32[1024]{0:T(1024)S(1)}, f32[1024]{0:T(1024)}, u32[]{:S(2)}) copy-start(f32[1024]{0:T(1024)} %param.12) | copy-start | bytes 12292
  6.5 84.1 %copy-start.4 = (f32[1024,16]{0,1:T(8,128)S(1)}, f32[1024,16]{0,1:T(8,128)}, u32[]{:S(2)}) copy-start(f32[1024,16]{0,1:T(8,128)} %param.10) | copy-start | bytes 196612
  6.5 39.9 %collective-permute-start.5 = (bf16[32,1024]{1,0:T(8,128)(2,1)}, bf16[32,1024]{1,0:T(8,128)(2,1)S(1)}, u32[]{:S(2)}, u32[]{:S(2)}) collective-permute-start(bf16[32,1024]{1,0:T(8,128)(2,1)} %bitcast.18), channel_id=1, source_target_pairs={{0,32},{32,64},{64,96},{96,0},{1,33},{33,65},{65,97},{97,1},{2,34}... | collective-permute-start | bytes 196616 | tf_op jit(solution)/shard_map/weights_zh/ppermute | solution.py:170
  16.3 30.1 %collective-permute-start.4 = (bf16[32,1024]{1,0:T(8,128)(2,1)}, bf16[32,1024]{1,0:T(8,128)(2,1)S(1)}, u32[]{:S(2)}, u32[]{:S(2)}) collective-permute-start(bf16[32,1024]{1,0:T(8,128)(2,1)} %bitcast.19), channel_id=1, source_target_pairs={{0,64},{32,96},{64,0},{96,32},{1,65},{33,97},{65,1},{97,33},{2,66}... | collective-permute-start | bytes 196616 | tf_op jit(solution)/shard_map/weights_zh/ppermute | solution.py:170
  27.0 19.5 %collective-permute-start.3 = (bf16[32,1024]{1,0:T(8,128)(2,1)}, bf16[32,1024]{1,0:T(8,128)(2,1)S(1)}, u32[]{:S(2)}, u32[]{:S(2)}) collective-permute-start(bf16[32,1024]{1,0:T(8,128)(2,1)} %bitcast.20), channel_id=1, source_target_pairs={{0,96},{32,0},{64,32},{96,64},{1,97},{33,1},{65,33},{97,65},{2,98}... | collective-permute-start | bytes 196616 | tf_op jit(solution)/shard_map/weights_zh/ppermute | solution.py:170
  35.6 55.1 %copy-start.3 = (bf16[2,128,1024]{2,1,0:T(8,128)(2,1)S(1)}, bf16[2,128,1024]{2,1,0:T(8,128)(2,1)}, u32[]{:S(2)}) copy-start(bf16[2,128,1024]{2,1,0:T(8,128)(2,1)} %get-tuple-element.9.b0) | copy-start | bytes 1572868
  35.6 10.8 %all-to-all-start = ((bf16[8,16,128]{2,1,0:T(8,128)(2,1)}), bf16[8,16,128]{2,1,0:T(8,128)(2,1)S(1)}, u32[]{:S(2)}, u32[]{:S(2)}) async-start(bf16[8,16,128]{2,1,0:T(8,128)(2,1)} %bitcast.23), calls=%async_computation | async-start | bytes 65536 | tf_op jit(solution)/shard_map/scan_member/all_to_all | solution.py:213
  41.7 48.9 %all-gather.2.cloned.1.call-start = ((), (), s32[]{:S(2)}) async-start(), calls=%async_computation.5 | async-start | bytes 2359296 | tf_op jit(solution)/shard_map/weights_zh/all_gather | solution.py:223
  46.5 0.8 copy-start.5
  48.0 42.5 %collective-permute-start.2 = (bf16[2,128,1024]{2,1,0:T(8,128)(2,1)}, bf16[2,128,1024]{2,1,0:T(8,128)(2,1)S(1)}, u32[]{:S(2)}, u32[]{:S(2)}) collective-permute-start(bf16[2,128,1024]{2,1,0:T(8,128)(2,1)} %get-tuple-element.9.b0), channel_id=1, source_target_pairs={{0,8},{8,16},{16,24},{24,0},{1,9},{9,17},{17,25},{25,1},{2,10},{10... | collective-permute-start | bytes 1572872 | tf_op jit(solution)/shard_map/inputs/ppermute | solution.py:170
  50.2 40.3 %collective-permute-start.1 = (bf16[2,128,1024]{2,1,0:T(8,128)(2,1)}, bf16[2,128,1024]{2,1,0:T(8,128)(2,1)S(1)}, u32[]{:S(2)}, u32[]{:S(2)}) collective-permute-start(bf16[2,128,1024]{2,1,0:T(8,128)(2,1)} %get-tuple-element.9.b0), channel_id=1, source_target_pairs={{0,16},{8,24},{16,0},{24,8},{1,17},{9,25},{17,1},{25,9},{2,18},{10... | collective-permute-start | bytes 1572872 | tf_op jit(solution)/shard_map/inputs/ppermute | solution.py:170
  53.9 36.6 %collective-permute-start = (bf16[2,128,1024]{2,1,0:T(8,128)(2,1)}, bf16[2,128,1024]{2,1,0:T(8,128)(2,1)S(1)}, u32[]{:S(2)}, u32[]{:S(2)}) collective-permute-start(bf16[2,128,1024]{2,1,0:T(8,128)(2,1)} %get-tuple-element.9.b0), channel_id=1, source_target_pairs={{0,24},{8,0},{16,8},{24,16},{1,25},{9,1},{17,9},{25,17},{2,26},{10... | collective-permute-start | bytes 1572872 | tf_op jit(solution)/shard_map/inputs/ppermute | solution.py:170
  56.7 0.8 copy-start.1
  58.2 22.1 %all-to-all-start.1 = ((bf16[16,16,128]{2,1,0:T(8,128)(2,1)}), bf16[16,16,128]{2,1,0:T(8,128)(2,1)S(1)}, u32[]{:S(2)}, u32[]{:S(2)}) async-start(bf16[16,16,128]{2,1,0:T(8,128)(2,1)} %get-tuple-element.11), calls=%async_computation.1 | async-start | bytes 131072 | tf_op jit(solution)/shard_map/scan_group/all_to_all | solution.py:236
  90.6 1.6 %copy-start = (bf16[32,32,1024]{2,1,0:T(8,128)(2,1)S(1)}, bf16[32,32,1024]{2,1,0:T(8,128)(2,1)}, u32[]{:S(2)}) copy-start(bf16[32,32,1024]{2,1,0:T(8,128)(2,1)} %all-gather.2.cloned.1.call-done) | copy-start | bytes 6291460
Sparse Core Ops, SparseCore 0:
  48.2 26.1 all-gather.1

commit v3 on v2

v3 whole, which is shorter than its diff:
```python
import jax
import jax.numpy as jnp
from jax import lax
from jax.experimental import pallas as pl
from jax.experimental.pallas import tpu as pltpu
from jax.sharding import Mesh, PartitionSpec as P

ORDER = 16
TOK = 128
LANES = 128
GROUPS = 8
CHANS = LANES * GROUPS
COLS = 32
W_ROWS = GROUPS * COLS
PACK = W_ROWS + ORDER
F32 = jnp.float32
BF16 = jnp.bfloat16

SCALAR = pl.BlockSpec(memory_space=pltpu.SMEM)
WHOLE = pl.BlockSpec(memory_space=pltpu.VMEM)
FAR = pl.BlockSpec(memory_space=pltpu.HBM)


def params(mib=40):
    return pltpu.CompilerParams(vmem_limit_bytes=mib * 1024 * 1024)


def spread(src, dst, rows):
    for j in range(GROUPS):
        dst[pl.ds(j, rows, stride=GROUPS), :] = src[:, j * LANES : (j + 1) * LANES]


def per_pole(ref):
    return [ref[m * GROUPS : (m + 1) * GROUPS, :] for m in range(ORDER)]


def tree_sum(terms):
    while len(terms) > 1:
        terms = [terms[k] + terms[k + 1] for k in range(0, len(terms), 2)]
    return terms[0]


def token_rows(t):
    return pl.ds(pl.multiple_of(t * GROUPS, GROUPS), GROUPS)


def state_kernel(keys_far, values_far, rates, x_out, tok_out, s_out, keys, values, a_tok, s_rows, sems):
    copies = [
        pltpu.make_async_copy(keys_far, keys, sems.at[0]),
        pltpu.make_async_copy(values_far, values, sems.at[1]),
    ]
    for copy in copies:
        copy.start()
    spread(jnp.exp(-rates[...]), a_tok, ORDER)
    for copy in copies:
        copy.wait()
    for t in range(0, TOK, 16):
        for j in range(GROUPS):
            here = (pl.ds(t, 16), pl.ds(j * LANES, LANES))
            x = (keys[here].astype(F32) * values[here].astype(F32)).astype(BF16)
            x_out[here] = x
            tok_out[pl.ds(t * GROUPS + j, 16, stride=GROUPS), :] = x.astype(F32)
    decay = per_pole(a_tok)

    def step(i, state):
        for u in range(8):
            x = tok_out[token_rows(i * 8 + u), :]
            state = [a * s + x for a, s in zip(decay, state)]
        return state

    state = lax.fori_loop(0, TOK // 8, step, [jnp.zeros((GROUPS, LANES), F32)] * ORDER)
    for m in range(ORDER):
        s_rows[pl.ds(m, GROUPS, stride=ORDER), :] = state[m]
    s_out[...] = s_rows[...].astype(BF16)


def local_kernel(x_tok, rates, res, y_tok, a_tok, r_tok):
    spread(jnp.exp(-rates[...]), a_tok, ORDER)
    spread(res[...], r_tok, ORDER)
    decay = per_pole(a_tok)
    resid = per_pole(r_tok)

    def step(i, state):
        for u in range(4):
            x = x_tok[token_rows(i * 4 + u), :]
            state = [a * s + x for a, s in zip(decay, state)]
            y_tok[token_rows(i * 4 + u), :] = tree_sum([r * s for r, s in zip(resid, state)])
        return state

    lax.fori_loop(0, TOK // 4, step, [jnp.zeros((GROUPS, LANES), F32)] * ORDER)


def member_kernel(member, mine, rates, w_t, packed, inside):
    rate = rates[:, pl.ds(pl.multiple_of(member[0] * LANES, LANES), LANES)]
    one = jnp.exp(-rate * TOK)
    total = jnp.zeros((ORDER, LANES), F32)
    for k in range(8):
        inside[k] = total
        total = one * total + mine[k].astype(F32)
    total = total.astype(BF16)
    for d in range(4):
        for j in range(GROUPS):
            packed[d, j * COLS : (j + 1) * COLS, :] = w_t[:, j * LANES : (j + 1) * LANES]
        packed[d, W_ROWS:, :] = total


def group_kernel(member, group, packs, inside, rates, sent):
    rate = rates[:, pl.ds(pl.multiple_of(member[0] * LANES, LANES), LANES)]
    one = jnp.exp(-rate * TOK)
    eight = jnp.exp(-rate * (8 * TOK))
    ahead = jnp.zeros((ORDER, LANES), F32)
    for g in range(16):
        total = packs[g // 4, g % 4, W_ROWS:, :].astype(F32)
        ahead = jnp.where(g < group[0], eight * ahead + total, ahead)
    for k in range(8):
        sent[k] = (ahead + inside[k]).astype(BF16)
        ahead = one * ahead


def join_kernel(core, own, other, w):
    for half, packs in enumerate((own, other)):
        side = lax.rem(core[0] + half, 2)
        for x in range(4):
            for zh in range(4):
                rows = pl.ds(pl.multiple_of(side * 128 + zh * COLS, COLS), COLS)
                for j in range(GROUPS):
                    w[x, rows, j * LANES : (j + 1) * LANES] = packs[
                        x, zh, j * COLS : (j + 1) * COLS, :
                    ]


def carry_kernel(y_tok, prefix, x, q, rates, res, skip, out, c_tok, a_tok, r_tok, p_rows):
    spread(jnp.exp(-rates[...]), a_tok, ORDER)
    spread(res[...], r_tok, ORDER)
    p_rows[...] = prefix[...].astype(F32)
    decay = per_pole(a_tok)
    state = [
        r * p_rows[pl.ds(m, GROUPS, stride=ORDER), :] for m, r in enumerate(per_pole(r_tok))
    ]

    def step(i, state):
        for u in range(4):
            at = token_rows(i * 4 + u)
            state = [a * s for a, s in zip(decay, state)]
            c_tok[at, :] = y_tok[at, :] + tree_sum(state)
        return state

    lax.fori_loop(0, TOK // 4, step, state)
    for t in range(0, TOK, 16):
        for j in range(GROUPS):
            here = (pl.ds(t, 16), pl.ds(j * LANES, LANES))
            conv = c_tok[pl.ds(t * GROUPS + j, 16, stride=GROUPS), :].astype(BF16)
            total = conv.astype(F32) + skip[j : j + 1, :] * x[here].astype(F32)
            gated = (q[here].astype(F32) * total).astype(BF16)
            for d in range(4):
                out[(d,) + here] = gated


def dot_kernel(gated, w, out):
    @pl.loop(0, 4)
    def _(x):
        rhs = w[x]
        for y in range(4):
            out[x, y] = lax.dot_general(
                gated[y], rhs, (((1,), (1,)), ((), ())), preferred_element_type=F32
            ).astype(BF16)


def sum_kernel(recv, out):
    for y in range(4):
        terms = [recv[z, y].astype(F32) for z in range(4)]
        out[y] = ((terms[0] + terms[1]) + (terms[2] + terms[3])).astype(BF16)


def order_kernel(recv, out):
    quarter = lax.broadcasted_iota(jnp.int32, (TOK, LANES), 1) // 32
    tiles = {
        (y, c): recv[y, :, c * LANES : (c + 1) * LANES].astype(F32)
        for y in range(4)
        for c in range(2)
    }
    for zh in range(4):
        for pair in range(2):
            total = None
            for k in range(4):
                part = tiles[2 * pair + k // 2, k % 2]
                if k != zh:
                    part = pltpu.roll(part, (k - zh) % 4 * 32, 1)
                total = part if total is None else jnp.where(quarter == k, part, total)
            at = zh * 2 + pair
            out[:, at * LANES : (at + 1) * LANES] = total.astype(BF16)


def exchange(blocks, axis):
    return lax.all_to_all(blocks, axis, split_axis=0, concat_axis=0, tiled=True)


def call(kernel, out_shape, scratch=(), specs=None, mib=40):
    extra = {} if specs is None else {"in_specs": specs}
    return pl.pallas_call(
        kernel, out_shape=out_shape, scratch_shapes=list(scratch), compiler_params=params(mib), **extra
    )


def per_device(query, keys, values, residues, rates, skip_gain, w_out):
    rate_t = rates.T
    res_t = residues.T
    skip = skip_gain.reshape(GROUPS, LANES)
    w_t = w_out.T
    group = (lax.axis_index("x") * 4 + lax.axis_index("zh")).reshape(1)
    core = lax.axis_index("core").reshape(1)
    member = lax.axis_index("y").reshape(1) * 2 + core
    poles = pltpu.VMEM((ORDER * GROUPS, LANES), F32)
    by_token = jax.ShapeDtypeStruct((TOK * GROUPS, LANES), F32)

    with jax.named_scope("states"):
        x, x_tok, state = call(
            state_kernel,
            [
                jax.ShapeDtypeStruct((TOK, CHANS), BF16),
                by_token,
                jax.ShapeDtypeStruct((GROUPS * ORDER, LANES), BF16),
            ],
            [
                pltpu.VMEM((TOK, CHANS), BF16),
                pltpu.VMEM((TOK, CHANS), BF16),
                poles,
                poles,
                pltpu.SemaphoreType.DMA((2,)),
            ],
            [FAR, FAR, WHOLE],
            60,
        )(keys, values, rate_t)
    with jax.named_scope("local"):
        y_tok = call(local_kernel, by_token, [poles, poles])(x_tok, rate_t, res_t)
    with jax.named_scope("scan_member"):
        mine = exchange(state.reshape(8, ORDER, LANES), ("y", "core"))
        packed, inside = call(
            member_kernel,
            [
                jax.ShapeDtypeStruct((4, PACK, LANES), BF16),
                jax.ShapeDtypeStruct((8, ORDER, LANES), F32),
            ],
            specs=[SCALAR, WHOLE, WHOLE, WHOLE],
        )(member, mine, rate_t, w_t)
    with jax.named_scope("scan_group"):
        packed = exchange(packed, "zh")
        packed = exchange(jnp.broadcast_to(packed[None], (4, 4, PACK, LANES)), "x")
        sent = call(
            group_kernel,
            jax.ShapeDtypeStruct((8, ORDER, LANES), BF16),
            specs=[SCALAR, SCALAR, WHOLE, WHOLE, WHOLE],
        )(member, group, packed, inside, rate_t)
        prefix = exchange(sent, ("y", "core")).reshape(GROUPS * ORDER, LANES)
    with jax.named_scope("weights"):
        other = lax.ppermute(packed, "core", [(0, 1), (1, 0)])
        w = call(
            join_kernel,
            jax.ShapeDtypeStruct((4, 8 * COLS, CHANS), BF16),
            specs=[SCALAR, WHOLE, WHOLE],
        )(core, packed, other)
    with jax.named_scope("gate"):
        gated = call(
            carry_kernel,
            jax.ShapeDtypeStruct((4, TOK, CHANS), BF16),
            [pltpu.VMEM((TOK * GROUPS, LANES), F32), poles, poles, poles],
        )(y_tok, prefix, x, query, rate_t, res_t, skip)
        gated = exchange(gated, "y")
    with jax.named_scope("project"):
        partial = call(dot_kernel, jax.ShapeDtypeStruct((4, 4, TOK, 256), BF16))(gated, w)
    with jax.named_scope("reduce"):
        shares = call(sum_kernel, jax.ShapeDtypeStruct((4, TOK, 256), BF16))(
            exchange(partial, "tp")
        )
        return call(order_kernel, jax.ShapeDtypeStruct((TOK, CHANS), BF16))(
            exchange(shares, "y")
        )


def solution(mesh):
    fine = Mesh(mesh.devices.reshape(4, 4, 4, 2, 4), ("x", "zh", "y", "core", "tp"))
    ctx = ("x", "zh", "y", "core")
    placed = (
        P(ctx, "tp"),
        P(ctx, "tp"),
        P(ctx, "tp"),
        P("tp", None),
        P("tp", None),
        P("tp"),
        P("tp", ctx),
    )
    return jax.shard_map(
        per_device, mesh=fine, in_specs=placed, out_specs=P(ctx, "tp"), check_vma=False
    )
```

time: 144 us -> 148 us (1.028)
  blocking collectives: 45.9 us -> 79.1 us
  starting transfers between devices: 48.4 us -> 28.1 us
  between operations: 13.6 us -> 0.13 us
  local copies, waits for them, and re-layouts: 3.27 us -> 6 us
    all_to_all x3 -> x4, blocking collectives: 45.9 us -> 79.1 us  [exchange(): return lax.all_to_all(blocks, axis, split_axis=0, concat_axis=0, tiled=True)]
    ppermute x6 -> x1, starting transfers between devices: 34.2 us -> 10.4 us  [per_device(): other = lax.ppermute(packed, 'core', [(0, 1), (1, 0)])]
    all_to_all x2 -> x3, starting transfers between devices: 14.2 us -> 17.6 us  [exchange(): return lax.all_to_all(blocks, axis, split_axis=0, concat_axis=0, tiled=True)]
    unnamed x14 -> x20, local copies, waits for them, and re-layouts: 3.27 us -> 5.86 us
    all_to_all x2 -> x3, waiting for transfers between devices: 18.7 us -> 20 us  [exchange(): return lax.all_to_all(blocks, axis, split_axis=0, concat_axis=0, tiled=True)]
    pallas_call x7 -> x9, Pallas kernels: 13.8 us -> 13.2 us  [the longest x1 4.42 us: per_device(): call(dot_kernel, jax.ShapeDtypeStruct((4, 4, TOK, 256), BF16))(gated, w)]
  transfers between devices with their start and end apart: 9 -> 4, of which waited for: 2 -> 3; matrix products, arithmetic and copies ran while one was open for 0% -> 0% of each run, Pallas kernels for 3% -> 3%
where the time goes in v3:
time: 148 us; the launch traced here: 147 us
  blocking collectives  79.1 us (53%)
  starting transfers between devices  28.1 us (19%)
  waiting for transfers between devices  20 us (14%)
  Pallas kernels  13.2 us (9%)
  local copies, waits for them, and re-layouts  6 us (4%)
    all_to_all x4, blocking collectives, exchange(): return lax.all_to_all(blocks, axis, split_axis=0, concat_axis=0, tiled=True)  79.1 us
    all_to_all x3, waiting for transfers between devices, exchange(): return lax.all_to_all(blocks, axis, split_axis=0, concat_axis=0, tiled=True)  20 us
    all_to_all x3, starting transfers between devices, exchange(): return lax.all_to_all(blocks, axis, split_axis=0, concat_axis=0, tiled=True)  17.6 us
    ppermute x1, starting transfers between devices, per_device(): other = lax.ppermute(packed, 'core', [(0, 1), (1, 0)])  10.4 us
    unnamed x20, local copies, waits for them, and re-layouts  5.86 us
    pallas_call x1, Pallas kernels, per_device(): call(dot_kernel, jax.ShapeDtypeStruct((4, 4, TOK, 256), BF16))(gated, w)  4.42 us
    pallas_call x1, Pallas kernels, per_device(): call(state_kernel, [jax.ShapeDtypeStruct((TOK, CHANS), BF16), by_token, j...  3.45 us
  transfers between devices with their start and end apart: 4, of which 3 were waited for; matrix products, arithmetic and copies ran while one was open for 0% of the time, Pallas kernels for 3%

profile of v3, /device:TPU:1, one launch (start us, length us, event | category | flops | bytes accessed | tf_op | source)
XLA Modules:
  0.0 146.6 jit_solution(938373344022051050)
XLA Ops:
  0.0 3.5 %states.1 = (bf16[128,1024]{1,0:T(8,128)(2,1)}, f32[1024,128]{1,0:T(8,128)}, bf16[128,128]{1,0:T(8,128)(2,1)}) custom-call(bf16[128,1024]{1,0:T(8,128)(2,1)} %keys_far.1, bf16[128,1024]{1,0:T(8,128)(2,1)} %values_far.1, f32[16,1024]{1,0:T(8,128)} %bitcast.9), custom_call_target="tpu_custom_call" | custom-call | tf_op jit(solution)/shard_map/states/pallas_call | solution.py:217
  3.5 10.1 %all-to-all-start = ((bf16[8,16,128]{2,1,0:T(8,128)(2,1)}), bf16[8,16,128]{2,1,0:T(8,128)(2,1)S(1)}, u32[]{:S(2)}, u32[]{:S(2)}) async-start(bf16[8,16,128]{2,1,0:T(8,128)(2,1)} %bitcast.19), calls=%async_computation | async-start | bytes 65536 | tf_op jit(solution)/shard_map/scan_member/all_to_all | solution.py:195
  13.6 4.7 %all-to-all-done.mine = bf16[8,16,128]{2,1,0:T(8,128)(2,1)S(1)} async-done(((bf16[8,16,128]{2,1,0:T(8,128)(2,1)}), bf16[8,16,128]{2,1,0:T(8,128)(2,1)S(1)}, u32[]{:S(2)}, u32[]{:S(2)}) %all-to-all-start) | async-done | bytes 32800 | tf_op jit(solution)/shard_map/scan_member/all_to_all | solution.py:195
  18.3 0.0 copy-start
  18.3 0.8 copy-done
  19.2 0.0 copy-start.8
  19.2 0.8 copy-done.8
  20.0 24.7 %all_to_all.35 = bf16[4,272,128]{2,1,0:T(8,128)(2,1)S(1)} all-to-all(bf16[4,272,128]{2,1,0:T(8,128)(2,1)S(1)} %get-tuple-element.12), channel_id=1, replica_groups=mesh['x'=4,'zh'=4,'y'=4,'core'=2,'tp'=4] {'zh'}, dimensions={0} | all-to-all | bytes 557056 | tf_op jit(solution)/shard_map/scan_group/all_to_all | solution.py:195
  44.8 0.1 broadcast_in_dim.2
  44.9 0.0 copy-start.1
  44.9 14.0 %all_to_all.36.packs.own = bf16[4,4,272,128]{3,2,1,0:T(8,128)(2,1)S(1)} all-to-all(bf16[4,4,272,128]{3,2,1,0:T(8,128)(2,1)S(1)} %broadcast_in_dim.2), channel_id=1, replica_groups=mesh['x'=4,'zh'=4,'y'=4,'core'=2,'tp'=4] {'x'}, dimensions={0} | all-to-all | bytes 2228224 | tf_op jit(solution)/shard_map/scan_group/all_to_all | solution.py:195
  59.0 0.0 copy-start.4
  59.0 0.0 copy-start.7
  59.0 10.4 %collective-permute-start = (bf16[4,4,272,128]{3,2,1,0:T(8,128)(2,1)S(1)}, bf16[4,4,272,128]{3,2,1,0:T(8,128)(2,1)S(1)}, u32[]{:S(2)}, u32[]{:S(2)}) collective-permute-start(bf16[4,4,272,128]{3,2,1,0:T(8,128)(2,1)S(1)} %all_to_all.36.packs.own), channel_id=1, source_target_pairs={{0,4},{4,0},{1,5},{5,1},{2,6},{6,2},{3,7},{7,3},{8,12},{12,8},{9,1... | collective-permute-start | bytes 3342344 | tf_op jit(solution)/shard_map/weights/ppermute | solution.py:256
  69.4 0.0 copy-done.1
  69.5 0.0 copy-start.9
  69.5 0.7 scan_group.1
  70.1 3.3 %all-to-all-start.3 = ((bf16[8,16,128]{2,1,0:T(8,128)(2,1)}), bf16[8,16,128]{2,1,0:T(8,128)(2,1)S(1)}, u32[]{:S(2)}, u32[]{:S(2)}) async-start(bf16[8,16,128]{2,1,0:T(8,128)(2,1)} %scan_group.1), calls=%async_computation.3 | async-start | bytes 65536 | tf_op jit(solution)/shard_map/scan_group/all_to_all | solution.py:195
  73.4 0.0 copy-done.4
  73.4 0.0 copy-done.7
  73.5 1.2 local.1.y_tok
  74.7 3.5 %all-to-all-done.3 = bf16[8,16,128]{2,1,0:T(8,128)(2,1)S(1)} async-done(((bf16[8,16,128]{2,1,0:T(8,128)(2,1)}), bf16[8,16,128]{2,1,0:T(8,128)(2,1)S(1)}, u32[]{:S(2)}, u32[]{:S(2)}) %all-to-all-start.3) | async-done | bytes 32800 | tf_op jit(solution)/shard_map/scan_group/all_to_all | solution.py:195
  78.1 0.0 copy-done.9
  78.1 0.0 copy-start.5
  78.1 0.9 copy-done.5
  79.1 0.0 copy-start.6
  79.1 0.9 copy-done.6
  80.0 2.0 %gate.1 = bf16[4,128,1024]{2,1,0:T(8,128)(2,1)} custom-call(f32[1024,128]{1,0:T(8,128)S(1)} %local.1.y_tok, bf16[128,128]{1,0:T(8,128)(2,1)S(1)} %bitcast.16, bf16[128,1024]{1,0:T(8,128)(2,1)S(1)} %copy-done.6, bf16[128,1024]{1,0:T(8,128)(2,1)S(1)} %copy-done.5, f32[16,1024]{1,0:T(8,128)S(1)} %bitcast.13, f32[16,1024]{1,0:T(8,128)S(1)} %bitcast.15, ...), custom_call_target="tpu_custom_call" | custom-call | tf_op jit(solution)/shard_map/gate/pallas_call | solution.py:263
  82.0 4.2 %all-to-all-start.4 = ((bf16[4,128,1024]{2,1,0:T(8,128)(2,1)}), bf16[4,128,1024]{2,1,0:T(8,128)(2,1)}, u32[]{:S(2)}, u32[]{:S(2)}) async-start(bf16[4,128,1024]{2,1,0:T(8,128)(2,1)} %gate.1), calls=%async_computation.4 | async-start | bytes 2097152 | tf_op jit(solution)/shard_map/gate/all_to_all | solution.py:195
  86.2 0.0 collective-permute-done.other
  86.3 0.0 copy-start.2
  86.3 1.0 copy-done.2
  87.3 0.0 copy-start.3
  87.3 1.2 copy-done.3
  88.5 0.4 weights.1.w
  88.9 11.8 %all-to-all-done.4.gated = bf16[4,128,1024]{2,1,0:T(8,128)(2,1)} async-done(((bf16[4,128,1024]{2,1,0:T(8,128)(2,1)}), bf16[4,128,1024]{2,1,0:T(8,128)(2,1)}, u32[]{:S(2)}, u32[]{:S(2)}) %all-to-all-start.4) | async-done | bytes 1048608 | tf_op jit(solution)/shard_map/gate/all_to_all | solution.py:195
  100.7 4.4 %project.1 = bf16[4,4,128,256]{3,2,1,0:T(8,128)(2,1)S(1)} custom-call(bf16[4,128,1024]{2,1,0:T(8,128)(2,1)} %all-to-all-done.4.gated, bf16[4,256,1024]{2,1,0:T(8,128)(2,1)S(1)} %weights.1.w), custom_call_target="tpu_custom_call" | custom-call | tf_op jit(solution)/shard_map/project/pallas_call | solution.py:270
  105.2 32.4 %all_to_all.37.recv = bf16[4,4,128,256]{3,2,1,0:T(8,128)(2,1)S(1)} all-to-all(bf16[4,4,128,256]{3,2,1,0:T(8,128)(2,1)S(1)} %project.1), channel_id=1, replica_groups=mesh['x'=4,'zh'=4,'y'=4,'core'=2,'tp'=4] {'tp'}, dimensions={0} | all-to-all | bytes 2097152 | tf_op jit(solution)/shard_map/reduce/all_to_all | solution.py:195
  137.6 0.1 reduce.2
  137.7 7.9 %all_to_all.38.recv = bf16[4,128,256]{2,1,0:T(8,128)(2,1)S(1)} all-to-all(bf16[4,128,256]{2,1,0:T(8,128)(2,1)S(1)} %reduce.2), channel_id=1, replica_groups=mesh['x'=4,'zh'=4,'y'=4,'core'=2,'tp'=4] {'y'}, dimensions={0} | all-to-all | bytes 524288 | tf_op jit(solution)/shard_map/reduce/all_to_all | solution.py:195
  145.6 1.0 reduce.3
  (1 shorter events, 0.0 us)
Async XLA Ops:
  3.5 14.9 %all-to-all-start = ((bf16[8,16,128]{2,1,0:T(8,128)(2,1)}), bf16[8,16,128]{2,1,0:T(8,128)(2,1)S(1)}, u32[]{:S(2)}, u32[]{:S(2)}) async-start(bf16[8,16,128]{2,1,0:T(8,128)(2,1)} %bitcast.19), calls=%async_computation | async-start | bytes 65536 | tf_op jit(solution)/shard_map/scan_member/all_to_all | solution.py:195
  18.3 0.8 copy-start
  19.2 0.8 copy-start.8
  44.9 24.5 %copy-start.1 = (f32[1024,16]{0,1:T(8,128)S(1)}, f32[1024,16]{0,1:T(8,128)}, u32[]{:S(2)}) copy-start(f32[1024,16]{0,1:T(8,128)} %param.11) | copy-start | bytes 196612
  59.0 14.5 %copy-start.4 = (f32[1024,128]{1,0:T(8,128)S(1)}, f32[1024,128]{1,0:T(8,128)}, u32[]{:S(2)}) copy-start(f32[1024,128]{1,0:T(8,128)} %get-tuple-element.10.x_tok) | copy-start | bytes 1572868
  59.0 14.5 %copy-start.7 = (f32[1024,16]{0,1:T(8,128)S(1)}, f32[1024,16]{0,1:T(8,128)}, u32[]{:S(2)}) copy-start(f32[1024,16]{0,1:T(8,128)} %param.10) | copy-start | bytes 196612
  59.0 27.3 %collective-permute-start = (bf16[4,4,272,128]{3,2,1,0:T(8,128)(2,1)S(1)}, bf16[4,4,272,128]{3,2,1,0:T(8,128)(2,1)S(1)}, u32[]{:S(2)}, u32[]{:S(2)}) collective-permute-start(bf16[4,4,272,128]{3,2,1,0:T(8,128)(2,1)S(1)} %all_to_all.36.packs.own), channel_id=1, source_target_pairs={{0,4},{4,0},{1,5},{5,1},{2,6},{6,2},{3,7},{7,3},{8,12},{12,8},{9,1... | collective-permute-start | bytes 3342344 | tf_op jit(solution)/shard_map/weights/ppermute | solution.py:256
  69.5 8.7 %copy-start.9 = (f32[1024]{0:T(1024)S(1)}, f32[1024]{0:T(1024)}, u32[]{:S(2)}) copy-start(f32[1024]{0:T(1024)} %param.12) | copy-start | bytes 12292
  70.1 8.0 %all-to-all-start.3 = ((bf16[8,16,128]{2,1,0:T(8,128)(2,1)}), bf16[8,16,128]{2,1,0:T(8,128)(2,1)S(1)}, u32[]{:S(2)}, u32[]{:S(2)}) async-start(bf16[8,16,128]{2,1,0:T(8,128)(2,1)} %scan_group.1), calls=%async_computation.3 | async-start | bytes 65536 | tf_op jit(solution)/shard_map/scan_group/all_to_all | solution.py:195
  78.1 1.0 copy-start.5
  79.1 0.9 copy-start.6
  82.0 18.7 %all-to-all-start.4 = ((bf16[4,128,1024]{2,1,0:T(8,128)(2,1)}), bf16[4,128,1024]{2,1,0:T(8,128)(2,1)}, u32[]{:S(2)}, u32[]{:S(2)}) async-start(bf16[4,128,1024]{2,1,0:T(8,128)(2,1)} %gate.1), calls=%async_computation.4 | async-start | bytes 2097152 | tf_op jit(solution)/shard_map/gate/all_to_all | solution.py:195
  86.3 1.0 copy-start.2
  87.3 1.2 copy-start.3

commit v4 on v3

v4 whole, which is shorter than its diff:
```python
import jax
import jax.numpy as jnp
from jax import lax
from jax.experimental import pallas as pl
from jax.experimental.pallas import tpu as pltpu
from jax.sharding import Mesh, PartitionSpec as P

ORDER = 16
TOK = 128
LANES = 128
GROUPS = 8
CHANS = LANES * GROUPS
COLS = 32
W_ROWS = GROUPS * COLS
PACK = W_ROWS + ORDER
F32 = jnp.float32
BF16 = jnp.bfloat16

SCALAR = pl.BlockSpec(memory_space=pltpu.SMEM)
WHOLE = pl.BlockSpec(memory_space=pltpu.VMEM)
FAR = pl.BlockSpec(memory_space=pltpu.HBM)


def params(mib=40):
    return pltpu.CompilerParams(vmem_limit_bytes=mib * 1024 * 1024)


def tree_sum(terms):
    while len(terms) > 1:
        terms = [terms[k] + terms[k + 1] for k in range(0, len(terms), 2)]
    return terms[0]


def token_rows(t):
    return pl.ds(pl.multiple_of(t * GROUPS, GROUPS), GROUPS)


def prepare_kernel(keys_far, values_far, query_far, out, keys, values, query, sems):
    pairs = ((keys_far, keys), (values_far, values), (query_far, query))
    copies = [pltpu.make_async_copy(a, b, sems.at[i]) for i, (a, b) in enumerate(pairs)]
    for copy in copies:
        copy.start()
    copies[0].wait()
    copies[1].wait()
    for j in range(GROUPS):
        lanes = slice(j * LANES, (j + 1) * LANES)
        out[j, 0] = (keys[:, lanes].astype(F32) * values[:, lanes].astype(F32)).astype(BF16)
    copies[2].wait()
    for j in range(GROUPS):
        out[j, 1] = query[:, j * LANES : (j + 1) * LANES]


def own_channels(member, ref):
    return ref[:, pl.ds(pl.multiple_of(member[0] * LANES, LANES), LANES)]


def per_pole(block):
    return [jnp.broadcast_to(block[m : m + 1], (GROUPS, LANES)) for m in range(ORDER)]


def by_token(blocks, x_tok):
    for k in range(GROUPS):
        x_tok[pl.ds(k, TOK, stride=GROUPS), :] = blocks[k, 0].astype(F32)


def state_kernel(member, blocks, rates, w_far, packed, inside, x_tok, s_rows, w_t, sem):
    copy = pltpu.make_async_copy(w_far, w_t, sem)
    copy.start()
    rate = own_channels(member, rates)
    decay = per_pole(jnp.exp(-rate))
    by_token(blocks, x_tok)

    def step(i, state):
        for u in range(8):
            x = x_tok[token_rows(i * 8 + u), :]
            state = [a * s + x for a, s in zip(decay, state)]
        return state

    state = lax.fori_loop(0, TOK // 8, step, [jnp.zeros((GROUPS, LANES), F32)] * ORDER)
    for m in range(ORDER):
        s_rows[pl.ds(m, GROUPS, stride=ORDER), :] = state[m]
    one = jnp.exp(-rate * TOK)
    total = jnp.zeros((ORDER, LANES), F32)
    for k in range(GROUPS):
        inside[k] = total
        total = one * total + s_rows[k * ORDER : (k + 1) * ORDER, :]
    total = total.astype(BF16)
    copy.wait()
    for d in range(4):
        packed[d, W_ROWS:, :] = total
        for j in range(GROUPS):
            packed[d, j * COLS : (j + 1) * COLS, :] = w_t[:, j * LANES : (j + 1) * LANES]


def local_kernel(member, blocks, rates, res, y_tok, x_tok):
    decay = per_pole(jnp.exp(-own_channels(member, rates)))
    resid = per_pole(own_channels(member, res))
    by_token(blocks, x_tok)

    def step(i, state):
        for u in range(4):
            x = x_tok[token_rows(i * 4 + u), :]
            state = [a * s + x for a, s in zip(decay, state)]
            y_tok[token_rows(i * 4 + u), :] = tree_sum([r * s for r, s in zip(resid, state)])
        return state

    lax.fori_loop(0, TOK // 4, step, [jnp.zeros((GROUPS, LANES), F32)] * ORDER)


def carry_kernel(
    member, group, packs, inside, y_tok, blocks, rates, res, skips, out, c_tok, p_rows
):
    rate = own_channels(member, rates)
    one = jnp.exp(-rate * TOK)
    eight = jnp.exp(-rate * (8 * TOK))
    ahead = jnp.zeros((ORDER, LANES), F32)
    for g in range(16):
        total = packs[g // 4, g % 4].astype(F32)
        ahead = jnp.where(g < group[0], eight * ahead + total, ahead)
    for k in range(GROUPS):
        p_rows[k * ORDER : (k + 1) * ORDER, :] = ahead + inside[k]
        ahead = one * ahead
    decay = per_pole(jnp.exp(-rate))
    resid = per_pole(own_channels(member, res))
    state = [r * p_rows[pl.ds(m, GROUPS, stride=ORDER), :] for m, r in enumerate(resid)]

    def step(i, state):
        for u in range(4):
            at = token_rows(i * 4 + u)
            state = [a * s for a, s in zip(decay, state)]
            c_tok[at, :] = y_tok[at, :] + tree_sum(state)
        return state

    lax.fori_loop(0, TOK // 4, step, state)
    skip = skips[pl.ds(member[0], 1), :]
    for k in range(GROUPS):
        conv = c_tok[pl.ds(k, TOK, stride=GROUPS), :].astype(BF16).astype(F32)
        total = conv + skip * blocks[k, 0].astype(F32)
        gated = (blocks[k, 1].astype(F32) * total).astype(BF16)
        for y in range(4):
            for t0 in range(2):
                out[2 * (2 * y + k % 2) + t0, k // 2] = gated


def copies_kernel(packed, after, out):
    del after
    for d in range(4):
        out[d] = packed[...]


def join_kernel(core, own, other, w):
    first = core[0] == 0
    for x in range(4):
        for j in range(GROUPS):
            rows = slice(j * COLS, (j + 1) * COLS)
            mine = own[x, :, rows, :].reshape(4 * COLS, LANES)
            theirs = other[x, :, rows, :].reshape(4 * COLS, LANES)
            at = slice(x % 2 * CHANS + j * LANES, x % 2 * CHANS + (j + 1) * LANES)
            w[x // 2, at, :LANES] = jnp.where(first, mine, theirs).T
            w[x // 2, at, LANES:] = jnp.where(first, theirs, mine).T


def dot_kernel(gated, w, out, lhs):
    for y in range(4):
        for j in range(GROUPS):
            for t0 in range(2):
                at = t0 * CHANS + j * LANES
                lhs[y * TOK : (y + 1) * TOK, at : at + LANES] = gated[2 * j + t0, y]

    @pl.loop(0, 2)
    def _(t1):
        part = jnp.dot(lhs[...], w[t1], preferred_element_type=F32).astype(BF16)
        for y in range(4):
            out[y, t1] = part[y * TOK : (y + 1) * TOK]


def order_kernel(recv, out):
    quarter = lax.broadcasted_iota(jnp.int32, (TOK, LANES), 1) // 32
    tiles = {
        (y, c): recv[y, 0, :, c * LANES : (c + 1) * LANES].astype(F32)
        + recv[y, 1, :, c * LANES : (c + 1) * LANES].astype(F32)
        for y in range(4)
        for c in range(2)
    }
    for zh in range(4):
        for pair in range(2):
            total = None
            for k in range(4):
                part = tiles[2 * pair + k // 2, k % 2]
                if k != zh:
                    part = pltpu.roll(part, (k - zh) % 4 * 32, 1)
                total = part if total is None else jnp.where(quarter == k, part, total)
            at = zh * 2 + pair
            out[:, at * LANES : (at + 1) * LANES] = total.astype(BF16)


def exchange(blocks, axis):
    return lax.all_to_all(blocks, axis, split_axis=0, concat_axis=0, tiled=True)


def call(kernel, out_shape, scratch=(), specs=None, mib=24):
    extra = {} if specs is None else {"in_specs": specs}
    return pl.pallas_call(
        kernel, out_shape=out_shape, scratch_shapes=list(scratch), compiler_params=params(mib), **extra
    )


def per_device(query, keys, values, residues, rates, skip_gain, w_out):
    rate_t = rates.T
    res_t = residues.T
    skip = skip_gain.reshape(GROUPS, LANES)
    w_t = w_out.T
    group = (lax.axis_index("x") * 4 + lax.axis_index("zh")).reshape(1)
    core = lax.axis_index("core").reshape(1)
    member = lax.axis_index("y").reshape(1) * 2 + core
    tokens = pltpu.VMEM((TOK * GROUPS, LANES), F32)
    rows = pltpu.VMEM((GROUPS * ORDER, LANES), F32)
    members = ("y", "core")

    with jax.named_scope("prepare"):
        half = pltpu.VMEM((TOK, CHANS), BF16)
        blocks = call(
            prepare_kernel,
            jax.ShapeDtypeStruct((GROUPS, 2, TOK, LANES), BF16),
            [half, half, half, pltpu.SemaphoreType.DMA((3,))],
            [FAR] * 3,
            60,
        )(keys, values, query)
        blocks = exchange(blocks, members)
    with jax.named_scope("weights_swap"):
        swap = [(0, 0), (1, 2), (2, 1), (3, 3), (4, 4), (5, 6), (6, 5), (7, 7)]
        w_t = lax.ppermute(w_t, ("x", "t0"), swap)
    with jax.named_scope("states"):
        packed, inside = call(
            state_kernel,
            [
                jax.ShapeDtypeStruct((4, PACK, LANES), BF16),
                jax.ShapeDtypeStruct((GROUPS, ORDER, LANES), F32),
            ],
            [tokens, rows, pltpu.VMEM((COLS, CHANS), BF16), pltpu.SemaphoreType.DMA],
            [SCALAR, WHOLE, WHOLE, FAR],
        )(member, blocks, rate_t, w_t)
        packed = exchange(packed, "zh")
    with jax.named_scope("local"):
        y_tok = call(
            local_kernel,
            jax.ShapeDtypeStruct((TOK * GROUPS, LANES), F32),
            [tokens],
            [SCALAR, WHOLE, WHOLE, WHOLE],
        )(member, blocks, rate_t, res_t)
    with jax.named_scope("scan_x"):
        packed = call(
            copies_kernel,
            jax.ShapeDtypeStruct((4, 4, PACK, LANES), BF16),
            specs=[WHOLE, FAR],
        )(packed, y_tok)
        packed = exchange(packed, "x")
    with jax.named_scope("weights"):
        other = lax.ppermute(packed, "core", [(0, 1), (1, 0)])
        w = call(
            join_kernel,
            jax.ShapeDtypeStruct((2, 2 * CHANS, 8 * COLS), BF16),
            specs=[SCALAR, WHOLE, WHOLE],
        )(core, packed, other)
    with jax.named_scope("gate"):
        gated = call(
            carry_kernel,
            jax.ShapeDtypeStruct((2 * GROUPS, 4, TOK, LANES), BF16),
            [tokens, rows],
            [SCALAR, SCALAR] + [WHOLE] * 7,
        )(member, group, packed[:, :, W_ROWS:], inside, y_tok, blocks, rate_t, res_t, skip)
        gated = exchange(gated, ("y", "core", "t0"))
    with jax.named_scope("project"):
        shares = call(
            dot_kernel,
            jax.ShapeDtypeStruct((4, 2, TOK, 256), BF16),
            [pltpu.VMEM((4 * TOK, 2 * CHANS), BF16)],
        )(gated, w).reshape(8, TOK, 256)
    with jax.named_scope("reduce"):
        shares = exchange(shares, ("y", "t1")).reshape(4, 2, TOK, 256)
        return call(order_kernel, jax.ShapeDtypeStruct((TOK, CHANS), BF16))(shares)


def solution(mesh):
    fine = Mesh(mesh.devices.reshape(4, 4, 4, 2, 2, 2), ("x", "zh", "y", "core", "t1", "t0"))
    ctx = ("x", "zh", "y", "core")
    tp = ("t1", "t0")
    placed = (
        P(ctx, tp),
        P(ctx, tp),
        P(ctx, tp),
        P(tp, None),
        P(tp, None),
        P(tp),
        P(tp, ctx),
    )
    return jax.shard_map(
        per_device, mesh=fine, in_specs=placed, out_specs=P(ctx, tp), check_vma=False
    )
```

time: 148 us -> 134 us (0.905)
  blocking collectives: 79.1 us -> 21.2 us
  waiting for transfers between devices: 20 us -> 53.9 us
  starting transfers between devices: 28.1 us -> 43.3 us
  Pallas kernels: 13.2 us -> 11 us
  local copies, waits for them, and re-layouts: 6 us -> 3.93 us
    all_to_all x4 -> x1, blocking collectives: 79.1 us -> 21.2 us  [exchange(): return lax.all_to_all(blocks, axis, split_axis=0, concat_axis=0, tiled=True)]
    all_to_all x3 -> x4, waiting for transfers between devices: 20 us -> 51.2 us  [exchange(): return lax.all_to_all(blocks, axis, split_axis=0, concat_axis=0, tiled=True)]
    all_to_all x3 -> x4, starting transfers between devices: 17.6 us -> 40.6 us  [exchange(): return lax.all_to_all(blocks, axis, split_axis=0, concat_axis=0, tiled=True)]
    ppermute x1, starting transfers between devices: 10.4 us -> 2.01 us  [per_device(): other = lax.ppermute(packed, 'core', [(0, 1), (1, 0)])]
    ppermute x1, waiting for transfers between devices: 0.01 us -> 2.62 us  [per_device(): other = lax.ppermute(packed, 'core', [(0, 1), (1, 0)])]
    pallas_call x9 -> x8, Pallas kernels: 13.2 us -> 11 us  [the longest x1 2.29 us: per_device(): call(carry_kernel, jax.ShapeDtypeStruct((2 * GROUPS, 4, TOK, LANES), BF16...]
    unnamed x20 -> x14, local copies, waits for them, and re-layouts: 5.86 us -> 3.93 us
  transfers between devices with their start and end apart: 4 -> 6, of which waited for: 3 -> 5; matrix products, arithmetic and copies ran while one was open for 0% -> 0% of each run, Pallas kernels for 3% -> 1%
where the time goes in v4:
time: 134 us; the launch traced here: 133 us
  waiting for transfers between devices  53.9 us (40%)
  starting transfers between devices  43.3 us (32%)
  blocking collectives  21.2 us (16%)
  Pallas kernels  11 us (8%)
  local copies, waits for them, and re-layouts  3.93 us (3%)
    all_to_all x4, waiting for transfers between devices, exchange(): return lax.all_to_all(blocks, axis, split_axis=0, concat_axis=0, tiled=True)  51.2 us
    all_to_all x4, starting transfers between devices, exchange(): return lax.all_to_all(blocks, axis, split_axis=0, concat_axis=0, tiled=True)  40.6 us
    all_to_all x1, blocking collectives, exchange(): return lax.all_to_all(blocks, axis, split_axis=0, concat_axis=0, tiled=True)  21.2 us
    unnamed x14, local copies, waits for them, and re-layouts  3.93 us
  transfers between devices with their start and end apart: 6, of which 5 were waited for; matrix products, arithmetic and copies ran while one was open for 0% of the time, Pallas kernels for 1%

profile of v4, /device:TPU:1, one launch (start us, length us, event | category | flops | bytes accessed | tf_op | source)
XLA Modules:
  0.0 133.4 jit_solution(15461016554616931581)
XLA Ops:
  0.0 0.0 copy-start.6
  0.0 0.0 copy-start.3
  0.0 0.0 copy-start.4
  0.0 2.0 %prepare.1 = bf16[8,2,128,128]{3,2,1,0:T(8,128)(2,1)} custom-call(bf16[128,1024]{1,0:T(8,128)(2,1)} %keys_far.1, bf16[128,1024]{1,0:T(8,128)(2,1)} %values_far.1, bf16[128,1024]{1,0:T(8,128)(2,1)} %query_far.1), custom_call_target="tpu_custom_call" | custom-call | tf_op jit(solution)/shard_map/prepare/pallas_call | solution.py:222
  2.0 10.3 %all-to-all-start = ((bf16[8,2,128,128]{3,2,1,0:T(8,128)(2,1)}), bf16[8,2,128,128]{3,2,1,0:T(8,128)(2,1)S(1)}, u32[]{:S(2)}, u32[]{:S(2)}) async-start(bf16[8,2,128,128]{3,2,1,0:T(8,128)(2,1)} %prepare.1), calls=%async_computation | async-start | bytes 1048576 | tf_op jit(solution)/shard_map/prepare/all_to_all | solution.py:198
  12.3 0.0 copy-done.6
  12.3 0.7 collective-permute-start
  13.0 0.0 collective-permute-done.w_far
  13.0 8.8 %all-to-all-done.blocks = bf16[8,2,128,128]{3,2,1,0:T(8,128)(2,1)S(1)} async-done(((bf16[8,2,128,128]{3,2,1,0:T(8,128)(2,1)}), bf16[8,2,128,128]{3,2,1,0:T(8,128)(2,1)S(1)}, u32[]{:S(2)}, u32[]{:S(2)}) %all-to-all-start) | async-done | bytes 524320 | tf_op jit(solution)/shard_map/prepare/all_to_all | solution.py:198
  21.8 0.0 copy-done.3
  21.8 1.6 %states.1 = (bf16[4,272,128]{2,1,0:T(8,128)(2,1)}, f32[8,16,128]{2,1,0:T(8,128)S(1)}) custom-call(s32[1]{0:T(128)S(6)} %add.6.member, bf16[8,2,128,128]{3,2,1,0:T(8,128)(2,1)S(1)} %all-to-all-done.blocks, f32[16,1024]{1,0:T(8,128)S(1)} %bitcast.11, bf16[32,1024]{1,0:T(8,128)(2,1)S(1)} %collective-permute-done.w_far), custom_call_target="tpu_custom_call" | custom-call | tf_op jit(solution)/shard_map/states/pallas_call | solution.py:234
  23.4 10.5 %all-to-all-start.1 = ((bf16[4,272,128]{2,1,0:T(8,128)(2,1)}), bf16[4,272,128]{2,1,0:T(8,128)(2,1)S(1)}, u32[]{:S(2)}, u32[]{:S(2)}) async-start(bf16[4,272,128]{2,1,0:T(8,128)(2,1)} %get-tuple-element.7), calls=%async_computation.1 | async-start | bytes 557056 | tf_op jit(solution)/shard_map/states/all_to_all | solution.py:198
  33.9 0.0 copy-done.4
  33.9 1.3 local.1.after.y_tok
  35.2 0.0 copy-start.5
  35.2 12.4 %all-to-all-done.1.packed = bf16[4,272,128]{2,1,0:T(8,128)(2,1)S(1)} async-done(((bf16[4,272,128]{2,1,0:T(8,128)(2,1)}), bf16[4,272,128]{2,1,0:T(8,128)(2,1)S(1)}, u32[]{:S(2)}, u32[]{:S(2)}) %all-to-all-start.1) | async-done | bytes 278560 | tf_op jit(solution)/shard_map/states/all_to_all | solution.py:198
  47.7 0.1 scan_x.1
  47.8 0.0 copy-start.2
  47.8 1.0 copy-done.2
  48.8 4.0 %all-to-all-start.2 = ((bf16[4,4,272,128]{3,2,1,0:T(8,128)(2,1)}), bf16[4,4,272,128]{3,2,1,0:T(8,128)(2,1)S(1)}, u32[]{:S(2)}, u32[]{:S(2)}) async-start(bf16[4,4,272,128]{3,2,1,0:T(8,128)(2,1)} %copy-done.2), calls=%async_computation.2 | async-start | bytes 2228224 | tf_op jit(solution)/shard_map/scan_x/all_to_all | solution.py:198
  52.8 10.1 %all-to-all-done.2.own = bf16[4,4,272,128]{3,2,1,0:T(8,128)(2,1)S(1)} async-done(((bf16[4,4,272,128]{3,2,1,0:T(8,128)(2,1)}), bf16[4,4,272,128]{3,2,1,0:T(8,128)(2,1)S(1)}, u32[]{:S(2)}, u32[]{:S(2)}) %all-to-all-start.2) | async-done | bytes 1114144 | tf_op jit(solution)/shard_map/scan_x/all_to_all | solution.py:198
  62.9 0.0 copy-done.5
  62.9 2.3 %gate.1 = bf16[16,4,128,128]{3,2,1,0:T(8,128)(2,1)} custom-call(s32[1]{0:T(128)S(6)} %add.6.member, s32[1]{0:T(128)} %bitcast.2.group, bf16[4,4,16,128]{3,2,1,0:T(8,128)(2,1)S(1)} %slice.4.packs, f32[8,16,128]{2,1,0:T(8,128)S(1)} %get-tuple-element.8.inside, f32[1024,128]{1,0:T(8,128)S(1)} %local.1.after.y_tok, ...), custom_call_target="tpu_custom_call" | custom-call | tf_op jit(solution)/shard_map/gate/pallas_call | solution.py:266
  65.2 15.8 %all-to-all-start.3 = ((bf16[16,4,128,128]{3,2,1,0:T(8,128)(2,1)}), bf16[16,4,128,128]{3,2,1,0:T(8,128)(2,1)S(1)}, u32[]{:S(2)}, u32[]{:S(2)}) async-start(bf16[16,4,128,128]{3,2,1,0:T(8,128)(2,1)} %gate.1), calls=%async_computation.3 | async-start | bytes 4194304 | tf_op jit(solution)/shard_map/gate/all_to_all | solution.py:198
  81.1 2.0 %collective-permute-start.1 = (bf16[4,4,272,128]{3,2,1,0:T(8,128)(2,1)S(1)}, bf16[4,4,272,128]{3,2,1,0:T(8,128)(2,1)S(1)}, u32[]{:S(2)}, u32[]{:S(2)}) collective-permute-start(bf16[4,4,272,128]{3,2,1,0:T(8,128)(2,1)S(1)} %all-to-all-done.2.own), channel_id=1, source_target_pairs={{0,4},{4,0},{1,5},{5,1},{2,6},{6,2},{3,7},{7,3},{8,12},{12,8},{9,1... | collective-permute-start | bytes 3342344 | tf_op jit(solution)/shard_map/weights/ppermute | solution.py:259
  83.1 2.6 %collective-permute-done.1.other = bf16[4,4,272,128]{3,2,1,0:T(8,128)(2,1)S(1)} collective-permute-done((bf16[4,4,272,128]{3,2,1,0:T(8,128)(2,1)S(1)}, bf16[4,4,272,128]{3,2,1,0:T(8,128)(2,1)S(1)}, u32[]{:S(2)}, u32[]{:S(2)}) %collective-permute-start.1) | collective-permute-done | bytes 1114144 | tf_op jit(solution)/shard_map/weights/ppermute | solution.py:259
  85.7 0.6 weights.1.w
  86.3 0.0 copy-start
  86.3 1.3 copy-done
  87.7 19.9 %all-to-all-done.3.gated = bf16[16,4,128,128]{3,2,1,0:T(8,128)(2,1)S(1)} async-done(((bf16[16,4,128,128]{3,2,1,0:T(8,128)(2,1)}), bf16[16,4,128,128]{3,2,1,0:T(8,128)(2,1)S(1)}, u32[]{:S(2)}, u32[]{:S(2)}) %all-to-all-start.3) | async-done | bytes 2097184 | tf_op jit(solution)/shard_map/gate/all_to_all | solution.py:198
  107.6 0.0 copy-start.1
  107.6 1.6 %copy-done.1 = bf16[2,2048,256]{2,1,0:T(8,128)(2,1)S(1)} copy-done((bf16[2,2048,256]{2,1,0:T(8,128)(2,1)S(1)}, bf16[2,2048,256]{2,1,0:T(8,128)(2,1)}, u32[]{:S(2)}) %copy-start.1) | copy-done | bytes 2097176
  109.2 2.0 %project.1 = bf16[4,2,128,256]{3,2,1,0:T(8,128)(2,1)S(1)} custom-call(bf16[16,4,128,128]{3,2,1,0:T(8,128)(2,1)S(1)} %all-to-all-done.3.gated, bf16[2,2048,256]{2,1,0:T(8,128)(2,1)S(1)} %copy-done.1), custom_call_target="tpu_custom_call" | custom-call | tf_op jit(solution)/shard_map/project/pallas_call | solution.py:274
  111.2 21.2 %all_to_all.25 = bf16[8,128,256]{2,1,0:T(8,128)(2,1)S(1)} all-to-all(bf16[8,128,256]{2,1,0:T(8,128)(2,1)S(1)} %bitcast.9), channel_id=1, replica_groups=mesh['x'=4,'zh'=4,'y'=4,'core'=2,'t1'=2,'t0'=2] {'y','t1'}, dimensions={0} | all-to-all | bytes 1048576 | tf_op jit(solution)/shard_map/reduce/all_to_all | solution.py:198
  132.4 1.0 reduce.1
  (1 shorter events, 0.0 us)
Async XLA Ops:
  0.0 12.3 %copy-start.6 = (bf16[1024,32]{0,1:T(8,128)(2,1)S(1)}, bf16[1024,32]{0,1:T(8,128)(2,1)}, u32[]{:S(2)}) copy-start(bf16[1024,32]{0,1:T(8,128)(2,1)} %param.13) | copy-start | bytes 196612
  0.0 21.8 %copy-start.3 = (f32[1024,16]{0,1:T(8,128)S(1)}, f32[1024,16]{0,1:T(8,128)}, u32[]{:S(2)}) copy-start(f32[1024,16]{0,1:T(8,128)} %param.11) | copy-start | bytes 196612
  0.0 33.9 %copy-start.4 = (f32[1024,16]{0,1:T(8,128)S(1)}, f32[1024,16]{0,1:T(8,128)}, u32[]{:S(2)}) copy-start(f32[1024,16]{0,1:T(8,128)} %param.10) | copy-start | bytes 196612
  2.0 19.8 %all-to-all-start = ((bf16[8,2,128,128]{3,2,1,0:T(8,128)(2,1)}), bf16[8,2,128,128]{3,2,1,0:T(8,128)(2,1)S(1)}, u32[]{:S(2)}, u32[]{:S(2)}) async-start(bf16[8,2,128,128]{3,2,1,0:T(8,128)(2,1)} %prepare.1), calls=%async_computation | async-start | bytes 1048576 | tf_op jit(solution)/shard_map/prepare/all_to_all | solution.py:198
  12.3 0.7 collective-permute-start
  23.4 24.3 %all-to-all-start.1 = ((bf16[4,272,128]{2,1,0:T(8,128)(2,1)}), bf16[4,272,128]{2,1,0:T(8,128)(2,1)S(1)}, u32[]{:S(2)}, u32[]{:S(2)}) async-start(bf16[4,272,128]{2,1,0:T(8,128)(2,1)} %get-tuple-element.7), calls=%async_computation.1 | async-start | bytes 557056 | tf_op jit(solution)/shard_map/states/all_to_all | solution.py:198
  35.2 27.7 %copy-start.5 = (f32[1024]{0:T(1024)S(1)}, f32[1024]{0:T(1024)}, u32[]{:S(2)}) copy-start(f32[1024]{0:T(1024)} %param.12) | copy-start | bytes 12292
  47.8 1.0 copy-start.2
  48.8 14.1 %all-to-all-start.2 = ((bf16[4,4,272,128]{3,2,1,0:T(8,128)(2,1)}), bf16[4,4,272,128]{3,2,1,0:T(8,128)(2,1)S(1)}, u32[]{:S(2)}, u32[]{:S(2)}) async-start(bf16[4,4,272,128]{3,2,1,0:T(8,128)(2,1)} %copy-done.2), calls=%async_computation.2 | async-start | bytes 2228224 | tf_op jit(solution)/shard_map/scan_x/all_to_all | solution.py:198
  65.2 42.3 %all-to-all-start.3 = ((bf16[16,4,128,128]{3,2,1,0:T(8,128)(2,1)}), bf16[16,4,128,128]{3,2,1,0:T(8,128)(2,1)S(1)}, u32[]{:S(2)}, u32[]{:S(2)}) async-start(bf16[16,4,128,128]{3,2,1,0:T(8,128)(2,1)} %gate.1), calls=%async_computation.3 | async-start | bytes 4194304 | tf_op jit(solution)/shard_map/gate/all_to_all | solution.py:198
  81.1 4.6 %collective-permute-start.1 = (bf16[4,4,272,128]{3,2,1,0:T(8,128)(2,1)S(1)}, bf16[4,4,272,128]{3,2,1,0:T(8,128)(2,1)S(1)}, u32[]{:S(2)}, u32[]{:S(2)}) collective-permute-start(bf16[4,4,272,128]{3,2,1,0:T(8,128)(2,1)S(1)} %all-to-all-done.2.own), channel_id=1, source_target_pairs={{0,4},{4,0},{1,5},{5,1},{2,6},{6,2},{3,7},{7,3},{8,12},{12,8},{9,1... | collective-permute-start | bytes 3342344 | tf_op jit(solution)/shard_map/weights/ppermute | solution.py:259
  86.3 1.3 copy-start
  107.6 1.6 %copy-start.1 = (bf16[2,2048,256]{2,1,0:T(8,128)(2,1)S(1)}, bf16[2,2048,256]{2,1,0:T(8,128)(2,1)}, u32[]{:S(2)}) copy-start(bf16[2,2048,256]{2,1,0:T(8,128)(2,1)} %copy-done) | copy-start | bytes 6291460

commit v5 on v4

--- a/solution.py
+++ b/solution.py
@@ -12,7 +12,8 @@
 CHANS = LANES * GROUPS
 COLS = 32
 W_ROWS = GROUPS * COLS
-PACK = W_ROWS + ORDER
+QUARTER = W_ROWS // 4
+PACK = QUARTER + ORDER
 F32 = jnp.float32
 BF16 = jnp.bfloat16
 
@@ -86,10 +87,14 @@
         total = one * total + s_rows[k * ORDER : (k + 1) * ORDER, :]
     total = total.astype(BF16)
     copy.wait()
-    for d in range(4):
-        packed[d, W_ROWS:, :] = total
-        for j in range(GROUPS):
-            packed[d, j * COLS : (j + 1) * COLS, :] = w_t[:, j * LANES : (j + 1) * LANES]
+    for x in range(4):
+        for zh in range(4):
+            packed[4 * x + zh, QUARTER:, :] = total
+            for half in range(2):
+                j = 2 * x + half
+                packed[4 * x + zh, half * COLS : (half + 1) * COLS, :] = w_t[
+                    :, j * LANES : (j + 1) * LANES
+                ]
 
 
 def local_kernel(member, blocks, rates, res, y_tok, x_tok):
@@ -115,7 +120,7 @@
     eight = jnp.exp(-rate * (8 * TOK))
     ahead = jnp.zeros((ORDER, LANES), F32)
     for g in range(16):
-        total = packs[g // 4, g % 4].astype(F32)
+        total = packs[g, QUARTER:, :].astype(F32)
         ahead = jnp.where(g < group[0], eight * ahead + total, ahead)
     for k in range(GROUPS):
         p_rows[k * ORDER : (k + 1) * ORDER, :] = ahead + inside[k]
@@ -142,34 +147,30 @@
                 out[2 * (2 * y + k % 2) + t0, k // 2] = gated
 
 
-def copies_kernel(packed, after, out):
-    del after
-    for d in range(4):
-        out[d] = packed[...]
-
-
-def join_kernel(core, own, other, w):
+def join_kernel(x, core, *refs):
+    w = refs[8:]
     first = core[0] == 0
-    for x in range(4):
-        for j in range(GROUPS):
-            rows = slice(j * COLS, (j + 1) * COLS)
-            mine = own[x, :, rows, :].reshape(4 * COLS, LANES)
-            theirs = other[x, :, rows, :].reshape(4 * COLS, LANES)
-            at = slice(x % 2 * CHANS + j * LANES, x % 2 * CHANS + (j + 1) * LANES)
-            w[x // 2, at, :LANES] = jnp.where(first, mine, theirs).T
-            w[x // 2, at, LANES:] = jnp.where(first, theirs, mine).T
-
-
-def dot_kernel(gated, w, out, lhs):
+    for k in range(4):
+        own, other = refs[k], refs[4 + k]
+        start = lax.rem(x[0] + k, 4) * 2 * LANES
+        for xs in range(4):
+            for half in range(2):
+                rows = slice(half * COLS, (half + 1) * COLS)
+                mine = own[4 * xs : 4 * xs + 4, rows, :].reshape(4 * COLS, LANES)
+                theirs = other[4 * xs : 4 * xs + 4, rows, :].reshape(4 * COLS, LANES)
+                at = pl.ds(pl.multiple_of(start + xs % 2 * CHANS + half * LANES, LANES), LANES)
+                w[xs // 2][at, :LANES] = jnp.where(first, mine, theirs).T
+                w[xs // 2][at, LANES:] = jnp.where(first, theirs, mine).T
+
+
+def dot_kernel(gated, w0, w1, out, lhs):
     for y in range(4):
         for j in range(GROUPS):
             for t0 in range(2):
                 at = t0 * CHANS + j * LANES
                 lhs[y * TOK : (y + 1) * TOK, at : at + LANES] = gated[2 * j + t0, y]
-
-    @pl.loop(0, 2)
-    def _(t1):
-        part = jnp.dot(lhs[...], w[t1], preferred_element_type=F32).astype(BF16)
+    for t1, w in enumerate((w0, w1)):
+        part = jnp.dot(lhs[...], w[...], preferred_element_type=F32).astype(BF16)
         for y in range(4):
             out[y, t1] = part[y * TOK : (y + 1) * TOK]
 
@@ -234,13 +235,13 @@
         packed, inside = call(
             state_kernel,
             [
-                jax.ShapeDtypeStruct((4, PACK, LANES), BF16),
+                jax.ShapeDtypeStruct((16, PACK, LANES), BF16),
                 jax.ShapeDtypeStruct((GROUPS, ORDER, LANES), F32),
             ],
             [tokens, rows, pltpu.VMEM((COLS, CHANS), BF16), pltpu.SemaphoreType.DMA],
             [SCALAR, WHOLE, WHOLE, FAR],
         )(member, blocks, rate_t, w_t)
-        packed = exchange(packed, "zh")
+        packed = exchange(packed, ("x", "zh"))
     with jax.named_scope("local"):
         y_tok = call(
             local_kernel,
@@ -248,34 +249,32 @@
             [tokens],
             [SCALAR, WHOLE, WHOLE, WHOLE],
         )(member, blocks, rate_t, res_t)
-    with jax.named_scope("scan_x"):
-        packed = call(
-            copies_kernel,
-            jax.ShapeDtypeStruct((4, 4, PACK, LANES), BF16),
-            specs=[WHOLE, FAR],
-        )(packed, y_tok)
-        packed = exchange(packed, "x")
     with jax.named_scope("weights"):
-        other = lax.ppermute(packed, "core", [(0, 1), (1, 0)])
+        quarter = packed[:, :QUARTER]
+        further = [
+            lax.ppermute(quarter, "x", [(i, (i - k) % 4) for i in range(4)]) for k in (1, 2, 3)
+        ]
+        own = [quarter, *further]
+        other = [lax.ppermute(block, "core", [(0, 1), (1, 0)]) for block in own]
         w = call(
             join_kernel,
-            jax.ShapeDtypeStruct((2, 2 * CHANS, 8 * COLS), BF16),
-            specs=[SCALAR, WHOLE, WHOLE],
-        )(core, packed, other)
+            [jax.ShapeDtypeStruct((2 * CHANS, 8 * COLS), BF16)] * 2,
+            specs=[SCALAR, SCALAR] + [WHOLE] * 8,
+        )(lax.axis_index("x").reshape(1), core, *own, *other)
     with jax.named_scope("gate"):
         gated = call(
             carry_kernel,
             jax.ShapeDtypeStruct((2 * GROUPS, 4, TOK, LANES), BF16),
             [tokens, rows],
             [SCALAR, SCALAR] + [WHOLE] * 7,
-        )(member, group, packed[:, :, W_ROWS:], inside, y_tok, blocks, rate_t, res_t, skip)
+        )(member, group, packed, inside, y_tok, blocks, rate_t, res_t, skip)
         gated = exchange(gated, ("y", "core", "t0"))
     with jax.named_scope("project"):
         shares = call(
             dot_kernel,
             jax.ShapeDtypeStruct((4, 2, TOK, 256), BF16),
             [pltpu.VMEM((4 * TOK, 2 * CHANS), BF16)],
-        )(gated, w).reshape(8, TOK, 256)
+        )(gated, *w).reshape(8, TOK, 256)
     with jax.named_scope("reduce"):
         shares = exchange(shares, ("y", "t1")).reshape(4, 2, TOK, 256)
         return call(order_kernel, jax.ShapeDtypeStruct((TOK, CHANS), BF16))(shares)

time: 134 us -> 121 us (0.903)
  waiting for transfers between devices: 53.9 us -> 32.6 us
  starting transfers between devices: 43.3 us -> 53.9 us
  local copies, waits for them, and re-layouts: 3.93 us -> 2.23 us
    all_to_all x4 -> x3, waiting for transfers between devices: 51.2 us -> 28.6 us  [exchange(): return lax.all_to_all(blocks, axis, split_axis=0, concat_axis=0, tiled=True)]
    ppermute x1 -> x7, starting transfers between devices: 2.01 us -> 19.2 us  [the longest x4 12 us: per_device(): other = [lax.ppermute(block, 'core', [(0, 1), (1, 0)]) for block in own]]
    all_to_all x4 -> x3, starting transfers between devices: 40.6 us -> 34 us  [exchange(): return lax.all_to_all(blocks, axis, split_axis=0, concat_axis=0, tiled=True)]
    unnamed x14 -> x12, local copies, waits for them, and re-layouts: 3.93 us -> 2.21 us
    ppermute x1 -> x7, waiting for transfers between devices: 2.62 us -> 4 us  [the longest x3 2.88 us: per_device(): lax.ppermute(quarter, 'x', [(i, (i - k) % 4) for i in range(4)])]
  transfers between devices with their start and end apart: 6 -> 11, of which waited for: 5 -> 6; matrix products, arithmetic and copies ran while one was open for 0% -> 0% of each run, Pallas kernels for 1% -> 2%
where the time goes in v5:
time: 121 us; the launch traced here: 120 us
  starting transfers between devices  53.9 us (45%)
  waiting for transfers between devices  32.6 us (27%)
  blocking collectives  20.9 us (17%)
  Pallas kernels  10.1 us (8%)
  local copies, waits for them, and re-layouts  2.23 us (2%)
    all_to_all x3, starting transfers between devices, exchange(): return lax.all_to_all(blocks, axis, split_axis=0, concat_axis=0, tiled=True)  34 us
    all_to_all x3, waiting for transfers between devices, exchange(): return lax.all_to_all(blocks, axis, split_axis=0, concat_axis=0, tiled=True)  28.6 us
    all_to_all x1, blocking collectives, exchange(): return lax.all_to_all(blocks, axis, split_axis=0, concat_axis=0, tiled=True)  20.9 us
    ppermute x4, starting transfers between devices, per_device(): other = [lax.ppermute(block, 'core', [(0, 1), (1, 0)]) for block in own]  12 us
    ppermute x3, starting transfers between devices, per_device(): lax.ppermute(quarter, 'x', [(i, (i - k) % 4) for i in range(4)])  7.22 us
    ppermute x3, waiting for transfers between devices, per_device(): lax.ppermute(quarter, 'x', [(i, (i - k) % 4) for i in range(4)])  2.88 us
  transfers between devices with their start and end apart: 11, of which 6 were waited for; matrix products, arithmetic and copies ran while one was open for 0% of the time, Pallas kernels for 2%

profile of v5, /device:TPU:1, one launch (start us, length us, event | category | flops | bytes accessed | tf_op | source)
XLA Modules:
  0.0 119.9 jit_solution(10711492674764432617)
XLA Ops:
  0.0 0.0 copy-start.5
  0.0 0.0 copy-start.2
  0.0 0.0 copy-start.3
  0.0 2.0 %prepare.1 = bf16[8,2,128,128]{3,2,1,0:T(8,128)(2,1)} custom-call(bf16[128,1024]{1,0:T(8,128)(2,1)} %keys_far.1, bf16[128,1024]{1,0:T(8,128)(2,1)} %values_far.1, bf16[128,1024]{1,0:T(8,128)(2,1)} %query_far.1), custom_call_target="tpu_custom_call" | custom-call | tf_op jit(solution)/shard_map/prepare/pallas_call | solution.py:223
  2.0 0.0 copy-start.4
  2.1 10.3 %all-to-all-start = ((bf16[8,2,128,128]{3,2,1,0:T(8,128)(2,1)}), bf16[8,2,128,128]{3,2,1,0:T(8,128)(2,1)S(1)}, u32[]{:S(2)}, u32[]{:S(2)}) async-start(bf16[8,2,128,128]{3,2,1,0:T(8,128)(2,1)} %prepare.1), calls=%async_computation | async-start | bytes 1048576 | tf_op jit(solution)/shard_map/prepare/all_to_all | solution.py:199
  12.3 0.0 copy-done.5
  12.3 0.7 collective-permute-start
  13.0 0.0 collective-permute-done.w_far
  13.0 8.8 %all-to-all-done.blocks = bf16[8,2,128,128]{3,2,1,0:T(8,128)(2,1)S(1)} async-done(((bf16[8,2,128,128]{3,2,1,0:T(8,128)(2,1)}), bf16[8,2,128,128]{3,2,1,0:T(8,128)(2,1)S(1)}, u32[]{:S(2)}, u32[]{:S(2)}) %all-to-all-start) | async-done | bytes 524320 | tf_op jit(solution)/shard_map/prepare/all_to_all | solution.py:199
  21.8 0.0 copy-done.2
  21.8 1.6 %states.1 = (bf16[16,80,128]{2,1,0:T(8,128)(2,1)}, f32[8,16,128]{2,1,0:T(8,128)S(1)}) custom-call(s32[1]{0:T(128)S(6)} %add.6.member, bf16[8,2,128,128]{3,2,1,0:T(8,128)(2,1)S(1)} %all-to-all-done.blocks, f32[16,1024]{1,0:T(8,128)S(1)} %bitcast.12, bf16[32,1024]{1,0:T(8,128)(2,1)S(1)} %collective-permute-done.w_far), custom_call_target="tpu_custom_call" | custom-call | tf_op jit(solution)/shard_map/states/pallas_call | solution.py:235
  23.5 13.1 %all-to-all-start.1 = ((bf16[16,80,128]{2,1,0:T(8,128)(2,1)}), bf16[16,80,128]{2,1,0:T(8,128)(2,1)S(1)}, u32[]{:S(2)}, u32[]{:S(2)}) async-start(bf16[16,80,128]{2,1,0:T(8,128)(2,1)} %get-tuple-element.9), calls=%async_computation.1 | async-start | bytes 655360 | tf_op jit(solution)/shard_map/states/all_to_all | solution.py:199
  36.5 0.0 copy-done.3
  36.6 1.3 %local.1.y_tok = f32[1024,128]{1,0:T(8,128)S(1)} custom-call(s32[1]{0:T(128)S(6)} %add.6.member, bf16[8,2,128,128]{3,2,1,0:T(8,128)(2,1)S(1)} %all-to-all-done.blocks, f32[16,1024]{1,0:T(8,128)S(1)} %bitcast.13, f32[16,1024]{1,0:T(8,128)S(1)} %bitcast.15), custom_call_target="tpu_custom_call" | custom-call | tf_op jit(solution)/shard_map/local/pallas_call | solution.py:246
  37.9 18.2 %all-to-all-done.1.packs = bf16[16,80,128]{2,1,0:T(8,128)(2,1)S(1)} async-done(((bf16[16,80,128]{2,1,0:T(8,128)(2,1)}), bf16[16,80,128]{2,1,0:T(8,128)(2,1)S(1)}, u32[]{:S(2)}, u32[]{:S(2)}) %all-to-all-start.1) | async-done | bytes 327712 | tf_op jit(solution)/shard_map/states/all_to_all | solution.py:199
  56.1 0.0 copy-done.4
  56.1 2.3 %gate.1 = bf16[16,4,128,128]{3,2,1,0:T(8,128)(2,1)} custom-call(s32[1]{0:T(128)S(6)} %add.6.member, s32[1]{0:T(128)} %bitcast.2.group, bf16[16,80,128]{2,1,0:T(8,128)(2,1)S(1)} %all-to-all-done.1.packs, f32[8,16,128]{2,1,0:T(8,128)S(1)} %get-tuple-element.10.inside, f32[1024,128]{1,0:T(8,128)S(1)} %local.1.y_tok, ...), custom_call_target="tpu_custom_call" | custom-call | tf_op jit(solution)/shard_map/gate/pallas_call | solution.py:265
  58.4 10.7 %all-to-all-start.2 = ((bf16[16,4,128,128]{3,2,1,0:T(8,128)(2,1)}), bf16[16,4,128,128]{3,2,1,0:T(8,128)(2,1)S(1)}, u32[]{:S(2)}, u32[]{:S(2)}) async-start(bf16[16,4,128,128]{3,2,1,0:T(8,128)(2,1)} %gate.1), calls=%async_computation.2 | async-start | bytes 4194304 | tf_op jit(solution)/shard_map/gate/all_to_all | solution.py:199
  69.0 2.5 %collective-permute-start.1 = (bf16[16,64,128]{2,1,0:T(8,128)(2,1)S(1)}, bf16[16,64,128]{2,1,0:T(8,128)(2,1)S(1)}, u32[]{:S(2)}, u32[]{:S(2)}) collective-permute-start(bf16[16,64,128]{2,1,0:T(8,128)(2,1)S(1)} %slice.4.refs_0_), channel_id=1, source_target_pairs={{0,384},{128,0},{256,128},{384,256},{1,385},{129,1},{257,129},{385... | collective-permute-start | bytes 786440 | tf_op jit(solution)/shard_map/weights/ppermute | solution.py:255
  71.5 1.9 %collective-permute-start.2 = (bf16[16,64,128]{2,1,0:T(8,128)(2,1)S(1)}, bf16[16,64,128]{2,1,0:T(8,128)(2,1)S(1)}, u32[]{:S(2)}, u32[]{:S(2)}) collective-permute-start(bf16[16,64,128]{2,1,0:T(8,128)(2,1)S(1)} %slice.4.refs_0_), channel_id=1, source_target_pairs={{0,256},{128,384},{256,0},{384,128},{1,257},{129,385},{257,1},{385... | collective-permute-start | bytes 786440 | tf_op jit(solution)/shard_map/weights/ppermute | solution.py:255
  73.5 2.8 %collective-permute-start.3 = (bf16[16,64,128]{2,1,0:T(8,128)(2,1)S(1)}, bf16[16,64,128]{2,1,0:T(8,128)(2,1)S(1)}, u32[]{:S(2)}, u32[]{:S(2)}) collective-permute-start(bf16[16,64,128]{2,1,0:T(8,128)(2,1)S(1)} %slice.4.refs_0_), channel_id=1, source_target_pairs={{0,128},{128,256},{256,384},{384,0},{1,129},{129,257},{257,385},{3... | collective-permute-start | bytes 786440 | tf_op jit(solution)/shard_map/weights/ppermute | solution.py:255
  76.3 2.8 %collective-permute-start.4 = (bf16[16,64,128]{2,1,0:T(8,128)(2,1)S(1)}, bf16[16,64,128]{2,1,0:T(8,128)(2,1)S(1)}, u32[]{:S(2)}, u32[]{:S(2)}) collective-permute-start(bf16[16,64,128]{2,1,0:T(8,128)(2,1)S(1)} %slice.4.refs_0_), channel_id=1, source_target_pairs={{0,4},{4,0},{1,5},{5,1},{2,6},{6,2},{3,7},{7,3},{8,12},{12,8},{9,1... | collective-permute-start | bytes 786440 | tf_op jit(solution)/shard_map/weights/ppermute | solution.py:258
  79.1 0.0 collective-permute-done.1.refs_1_
  79.1 3.0 %collective-permute-start.5 = (bf16[16,64,128]{2,1,0:T(8,128)(2,1)S(1)}, bf16[16,64,128]{2,1,0:T(8,128)(2,1)S(1)}, u32[]{:S(2)}, u32[]{:S(2)}) collective-permute-start(bf16[16,64,128]{2,1,0:T(8,128)(2,1)S(1)} %collective-permute-done.1.refs_1_), channel_id=1, source_target_pairs={{0,4},{4,0},{1,5},{5,1},{2,6},{6,2},{3,7},{7,3},{8,12},{12,8},{9,1... | collective-permute-start | bytes 786440 | tf_op jit(solution)/shard_map/weights/ppermute | solution.py:258
  82.1 0.5 collective-permute-done.2.refs_2_
  82.5 3.9 %collective-permute-start.6 = (bf16[16,64,128]{2,1,0:T(8,128)(2,1)S(1)}, bf16[16,64,128]{2,1,0:T(8,128)(2,1)S(1)}, u32[]{:S(2)}, u32[]{:S(2)}) collective-permute-start(bf16[16,64,128]{2,1,0:T(8,128)(2,1)S(1)} %collective-permute-done.2.refs_2_), channel_id=1, source_target_pairs={{0,4},{4,0},{1,5},{5,1},{2,6},{6,2},{3,7},{7,3},{8,12},{12,8},{9,1... | collective-permute-start | bytes 786440 | tf_op jit(solution)/shard_map/weights/ppermute | solution.py:258
  86.4 2.4 %collective-permute-done.3.refs_3_ = bf16[16,64,128]{2,1,0:T(8,128)(2,1)S(1)} collective-permute-done((bf16[16,64,128]{2,1,0:T(8,128)(2,1)S(1)}, bf16[16,64,128]{2,1,0:T(8,128)(2,1)S(1)}, u32[]{:S(2)}, u32[]{:S(2)}) %collective-permute-start.3) | collective-permute-done | bytes 262176 | tf_op jit(solution)/shard_map/weights/ppermute | solution.py:255
  88.8 2.4 %collective-permute-start.7 = (bf16[16,64,128]{2,1,0:T(8,128)(2,1)S(1)}, bf16[16,64,128]{2,1,0:T(8,128)(2,1)S(1)}, u32[]{:S(2)}, u32[]{:S(2)}) collective-permute-start(bf16[16,64,128]{2,1,0:T(8,128)(2,1)S(1)} %collective-permute-done.3.refs_3_), channel_id=1, source_target_pairs={{0,4},{4,0},{1,5},{5,1},{2,6},{6,2},{3,7},{7,3},{8,12},{12,8},{9,1... | collective-permute-start | bytes 786440 | tf_op jit(solution)/shard_map/weights/ppermute | solution.py:258
  91.2 0.0 collective-permute-done.4.refs_4_
  91.2 0.0 collective-permute-done.5.refs_5_
  91.2 0.0 collective-permute-done.6.refs_6_
  91.2 1.1 collective-permute-done.7.refs_7_
  92.3 0.6 weights.1
  92.9 0.0 copy-start
  92.9 1.0 copy-done
  93.9 1.6 %all-to-all-done.2.gated = bf16[16,4,128,128]{3,2,1,0:T(8,128)(2,1)S(1)} async-done(((bf16[16,4,128,128]{3,2,1,0:T(8,128)(2,1)}), bf16[16,4,128,128]{3,2,1,0:T(8,128)(2,1)S(1)}, u32[]{:S(2)}, u32[]{:S(2)}) %all-to-all-start.2) | async-done | bytes 2097184 | tf_op jit(solution)/shard_map/gate/all_to_all | solution.py:199
  95.5 0.0 copy-start.1
  95.5 1.2 %copy-done.1 = bf16[2048,256]{1,0:T(8,128)(2,1)S(1)} copy-done((bf16[2048,256]{1,0:T(8,128)(2,1)S(1)}, bf16[2048,256]{1,0:T(8,128)(2,1)}, u32[]{:S(2)}) %copy-start.1) | copy-done | bytes 1048600
  96.8 1.3 %project.1 = bf16[4,2,128,256]{3,2,1,0:T(8,128)(2,1)S(1)} custom-call(bf16[16,4,128,128]{3,2,1,0:T(8,128)(2,1)S(1)} %all-to-all-done.2.gated, bf16[2048,256]{1,0:T(8,128)(2,1)S(1)} %get-tuple-element.11.w0, bf16[2048,256]{1,0:T(8,128)(2,1)S(1)} %copy-done.1), custom_call_target="tpu_custom_call" | custom-call | tf_op jit(solution)/shard_map/project/pallas_call | solution.py:273
  98.0 20.9 %all_to_all.20 = bf16[8,128,256]{2,1,0:T(8,128)(2,1)S(1)} all-to-all(bf16[8,128,256]{2,1,0:T(8,128)(2,1)S(1)} %bitcast.10), channel_id=1, replica_groups=mesh['x'=4,'zh'=4,'y'=4,'core'=2,'t1'=2,'t0'=2] {'y','t1'}, dimensions={0} | all-to-all | bytes 1048576 | tf_op jit(solution)/shard_map/reduce/all_to_all | solution.py:199
  119.0 1.0 reduce.1
  (1 shorter events, 0.0 us)
Async XLA Ops:
  0.0 12.3 %copy-start.5 = (bf16[1024,32]{0,1:T(8,128)(2,1)S(1)}, bf16[1024,32]{0,1:T(8,128)(2,1)}, u32[]{:S(2)}) copy-start(bf16[1024,32]{0,1:T(8,128)(2,1)} %param.13) | copy-start | bytes 196612
  0.0 21.8 %copy-start.2 = (f32[1024,16]{0,1:T(8,128)S(1)}, f32[1024,16]{0,1:T(8,128)}, u32[]{:S(2)}) copy-start(f32[1024,16]{0,1:T(8,128)} %param.11) | copy-start | bytes 196612
  0.0 36.5 %copy-start.3 = (f32[1024,16]{0,1:T(8,128)S(1)}, f32[1024,16]{0,1:T(8,128)}, u32[]{:S(2)}) copy-start(f32[1024,16]{0,1:T(8,128)} %param.10) | copy-start | bytes 196612
  2.0 54.0 %copy-start.4 = (f32[1024]{0:T(1024)S(1)}, f32[1024]{0:T(1024)}, u32[]{:S(2)}) copy-start(f32[1024]{0:T(1024)} %param.12) | copy-start | bytes 12292
  2.1 19.8 %all-to-all-start = ((bf16[8,2,128,128]{3,2,1,0:T(8,128)(2,1)}), bf16[8,2,128,128]{3,2,1,0:T(8,128)(2,1)S(1)}, u32[]{:S(2)}, u32[]{:S(2)}) async-start(bf16[8,2,128,128]{3,2,1,0:T(8,128)(2,1)} %prepare.1), calls=%async_computation | async-start | bytes 1048576 | tf_op jit(solution)/shard_map/prepare/all_to_all | solution.py:199
  12.3 0.7 collective-permute-start
  23.5 32.6 %all-to-all-start.1 = ((bf16[16,80,128]{2,1,0:T(8,128)(2,1)}), bf16[16,80,128]{2,1,0:T(8,128)(2,1)S(1)}, u32[]{:S(2)}, u32[]{:S(2)}) async-start(bf16[16,80,128]{2,1,0:T(8,128)(2,1)} %get-tuple-element.9), calls=%async_computation.1 | async-start | bytes 655360 | tf_op jit(solution)/shard_map/states/all_to_all | solution.py:199
  58.4 37.2 %all-to-all-start.2 = ((bf16[16,4,128,128]{3,2,1,0:T(8,128)(2,1)}), bf16[16,4,128,128]{3,2,1,0:T(8,128)(2,1)S(1)}, u32[]{:S(2)}, u32[]{:S(2)}) async-start(bf16[16,4,128,128]{3,2,1,0:T(8,128)(2,1)} %gate.1), calls=%async_computation.2 | async-start | bytes 4194304 | tf_op jit(solution)/shard_map/gate/all_to_all | solution.py:199
  69.0 10.0 %collective-permute-start.1 = (bf16[16,64,128]{2,1,0:T(8,128)(2,1)S(1)}, bf16[16,64,128]{2,1,0:T(8,128)(2,1)S(1)}, u32[]{:S(2)}, u32[]{:S(2)}) collective-permute-start(bf16[16,64,128]{2,1,0:T(8,128)(2,1)S(1)} %slice.4.refs_0_), channel_id=1, source_target_pairs={{0,384},{128,0},{256,128},{384,256},{1,385},{129,1},{257,129},{385... | collective-permute-start | bytes 786440 | tf_op jit(solution)/shard_map/weights/ppermute | solution.py:255
  71.5 11.0 %collective-permute-start.2 = (bf16[16,64,128]{2,1,0:T(8,128)(2,1)S(1)}, bf16[16,64,128]{2,1,0:T(8,128)(2,1)S(1)}, u32[]{:S(2)}, u32[]{:S(2)}) collective-permute-start(bf16[16,64,128]{2,1,0:T(8,128)(2,1)S(1)} %slice.4.refs_0_), channel_id=1, source_target_pairs={{0,256},{128,384},{256,0},{384,128},{1,257},{129,385},{257,1},{385... | collective-permute-start | bytes 786440 | tf_op jit(solution)/shard_map/weights/ppermute | solution.py:255
  73.5 15.3 %collective-permute-start.3 = (bf16[16,64,128]{2,1,0:T(8,128)(2,1)S(1)}, bf16[16,64,128]{2,1,0:T(8,128)(2,1)S(1)}, u32[]{:S(2)}, u32[]{:S(2)}) collective-permute-start(bf16[16,64,128]{2,1,0:T(8,128)(2,1)S(1)} %slice.4.refs_0_), channel_id=1, source_target_pairs={{0,128},{128,256},{256,384},{384,0},{1,129},{129,257},{257,385},{3... | collective-permute-start | bytes 786440 | tf_op jit(solution)/shard_map/weights/ppermute | solution.py:255
  76.3 14.9 %collective-permute-start.4 = (bf16[16,64,128]{2,1,0:T(8,128)(2,1)S(1)}, bf16[16,64,128]{2,1,0:T(8,128)(2,1)S(1)}, u32[]{:S(2)}, u32[]{:S(2)}) collective-permute-start(bf16[16,64,128]{2,1,0:T(8,128)(2,1)S(1)} %slice.4.refs_0_), channel_id=1, source_target_pairs={{0,4},{4,0},{1,5},{5,1},{2,6},{6,2},{3,7},{7,3},{8,12},{12,8},{9,1... | collective-permute-start | bytes 786440 | tf_op jit(solution)/shard_map/weights/ppermute | solution.py:258
  79.1 12.1 %collective-permute-start.5 = (bf16[16,64,128]{2,1,0:T(8,128)(2,1)S(1)}, bf16[16,64,128]{2,1,0:T(8,128)(2,1)S(1)}, u32[]{:S(2)}, u32[]{:S(2)}) collective-permute-start(bf16[16,64,128]{2,1,0:T(8,128)(2,1)S(1)} %collective-permute-done.1.refs_1_), channel_id=1, source_target_pairs={{0,4},{4,0},{1,5},{5,1},{2,6},{6,2},{3,7},{7,3},{8,12},{12,8},{9,1... | collective-permute-start | bytes 786440 | tf_op jit(solution)/shard_map/weights/ppermute | solution.py:258
  82.5 8.7 %collective-permute-start.6 = (bf16[16,64,128]{2,1,0:T(8,128)(2,1)S(1)}, bf16[16,64,128]{2,1,0:T(8,128)(2,1)S(1)}, u32[]{:S(2)}, u32[]{:S(2)}) collective-permute-start(bf16[16,64,128]{2,1,0:T(8,128)(2,1)S(1)} %collective-permute-done.2.refs_2_), channel_id=1, source_target_pairs={{0,4},{4,0},{1,5},{5,1},{2,6},{6,2},{3,7},{7,3},{8,12},{12,8},{9,1... | collective-permute-start | bytes 786440 | tf_op jit(solution)/shard_map/weights/ppermute | solution.py:258
  88.8 3.5 %collective-permute-start.7 = (bf16[16,64,128]{2,1,0:T(8,128)(2,1)S(1)}, bf16[16,64,128]{2,1,0:T(8,128)(2,1)S(1)}, u32[]{:S(2)}, u32[]{:S(2)}) collective-permute-start(bf16[16,64,128]{2,1,0:T(8,128)(2,1)S(1)} %collective-permute-done.3.refs_3_), channel_id=1, source_target_pairs={{0,4},{4,0},{1,5},{5,1},{2,6},{6,2},{3,7},{7,3},{8,12},{12,8},{9,1... | collective-permute-start | bytes 786440 | tf_op jit(solution)/shard_map/weights/ppermute | solution.py:258
  92.9 1.0 copy-start
  95.5 1.2 %copy-start.1 = (bf16[2048,256]{1,0:T(8,128)(2,1)S(1)}, bf16[2048,256]{1,0:T(8,128)(2,1)}, u32[]{:S(2)}) copy-start(bf16[2048,256]{1,0:T(8,128)(2,1)} %copy-done) | copy-start | bytes 3145732

commit v6 on v5

--- a/solution.py
+++ b/solution.py
@@ -11,9 +11,6 @@
 GROUPS = 8
 CHANS = LANES * GROUPS
 COLS = 32
-W_ROWS = GROUPS * COLS
-QUARTER = W_ROWS // 4
-PACK = QUARTER + ORDER
 F32 = jnp.float32
 BF16 = jnp.bfloat16
 
@@ -64,9 +61,8 @@
         x_tok[pl.ds(k, TOK, stride=GROUPS), :] = blocks[k, 0].astype(F32)
 
 
-def state_kernel(member, blocks, rates, w_far, packed, inside, x_tok, s_rows, w_t, sem):
-    copy = pltpu.make_async_copy(w_far, w_t, sem)
-    copy.start()
+def state_kernel(member, blocks, rates, after, also, totals, inside, x_tok, s_rows):
+    del after, also
     rate = own_channels(member, rates)
     decay = per_pole(jnp.exp(-rate))
     by_token(blocks, x_tok)
@@ -85,19 +81,12 @@
     for k in range(GROUPS):
         inside[k] = total
         total = one * total + s_rows[k * ORDER : (k + 1) * ORDER, :]
-    total = total.astype(BF16)
-    copy.wait()
-    for x in range(4):
-        for zh in range(4):
-            packed[4 * x + zh, QUARTER:, :] = total
-            for half in range(2):
-                j = 2 * x + half
-                packed[4 * x + zh, half * COLS : (half + 1) * COLS, :] = w_t[
-                    :, j * LANES : (j + 1) * LANES
-                ]
-
-
-def local_kernel(member, blocks, rates, res, y_tok, x_tok):
+    for g in range(16):
+        totals[g] = total.astype(BF16)
+
+
+def local_kernel(member, blocks, rates, res, after, y_tok, x_tok):
+    del after
     decay = per_pole(jnp.exp(-own_channels(member, rates)))
     resid = per_pole(own_channels(member, res))
     by_token(blocks, x_tok)
@@ -113,14 +102,15 @@
 
 
 def carry_kernel(
-    member, group, packs, inside, y_tok, blocks, rates, res, skips, out, c_tok, p_rows
+    member, group, packs, inside, y_tok, blocks, rates, res, skips, after, out, c_tok, p_rows
 ):
+    del after
     rate = own_channels(member, rates)
     one = jnp.exp(-rate * TOK)
     eight = jnp.exp(-rate * (8 * TOK))
     ahead = jnp.zeros((ORDER, LANES), F32)
     for g in range(16):
-        total = packs[g, QUARTER:, :].astype(F32)
+        total = packs[g].astype(F32)
         ahead = jnp.where(g < group[0], eight * ahead + total, ahead)
     for k in range(GROUPS):
         p_rows[k * ORDER : (k + 1) * ORDER, :] = ahead + inside[k]
@@ -147,20 +137,35 @@
                 out[2 * (2 * y + k % 2) + t0, k // 2] = gated
 
 
+def pair_kernel(at, own, other, after, out):
+    del after
+    low = lax.rem(at[0], 2)
+    out[low] = own[...]
+    out[1 - low] = other[...]
+
+
+def quad_kernel(at, own, other, out):
+    high = at[0] // 2
+    out[high] = own[...]
+    out[1 - high] = other[...]
+
+
 def join_kernel(x, core, *refs):
-    w = refs[8:]
     first = core[0] == 0
     for k in range(4):
         own, other = refs[k], refs[4 + k]
-        start = lax.rem(x[0] + k, 4) * 2 * LANES
-        for xs in range(4):
-            for half in range(2):
-                rows = slice(half * COLS, (half + 1) * COLS)
-                mine = own[4 * xs : 4 * xs + 4, rows, :].reshape(4 * COLS, LANES)
-                theirs = other[4 * xs : 4 * xs + 4, rows, :].reshape(4 * COLS, LANES)
-                at = pl.ds(pl.multiple_of(start + xs % 2 * CHANS + half * LANES, LANES), LANES)
-                w[xs // 2][at, :LANES] = jnp.where(first, mine, theirs).T
-                w[xs // 2][at, LANES:] = jnp.where(first, theirs, mine).T
+        xs = lax.rem(x[0] + k, 4)
+        for t1 in range(2):
+
+            @pl.when(xs // 2 == t1)
+            def _(own=own, other=other, xs=xs, w=refs[8 + t1]):
+                for j in range(GROUPS):
+                    lanes = slice(j * LANES, (j + 1) * LANES)
+                    mine = own[:, :, lanes].reshape(4 * COLS, LANES)
+                    theirs = other[:, :, lanes].reshape(4 * COLS, LANES)
+                    at = pl.ds(pl.multiple_of(lax.rem(xs, 2) * CHANS + j * LANES, LANES), LANES)
+                    w[at, :LANES] = jnp.where(first, mine, theirs).T
+                    w[at, LANES:] = jnp.where(first, theirs, mine).T
 
 
 def dot_kernel(gated, w0, w1, out, lhs):
@@ -199,8 +204,10 @@
     return lax.all_to_all(blocks, axis, split_axis=0, concat_axis=0, tiled=True)
 
 
-def call(kernel, out_shape, scratch=(), specs=None, mib=24):
+def call(kernel, out_shape, scratch=(), specs=None, mib=24, flops=0):
     extra = {} if specs is None else {"in_specs": specs}
+    if flops:
+        extra["cost_estimate"] = pl.CostEstimate(flops=flops, bytes_accessed=0, transcendentals=0)
     return pl.pallas_call(
         kernel, out_shape=out_shape, scratch_shapes=list(scratch), compiler_params=params(mib), **extra
     )
@@ -228,29 +235,54 @@
             60,
         )(keys, values, query)
         blocks = exchange(blocks, members)
-    with jax.named_scope("weights_swap"):
-        swap = [(0, 0), (1, 2), (2, 1), (3, 3), (4, 4), (5, 6), (6, 5), (7, 7)]
-        w_t = lax.ppermute(w_t, ("x", "t0"), swap)
+    with jax.named_scope("weights_zh"):
+        zh_here = lax.axis_index("zh").reshape(1)
+        w_near = lax.ppermute(w_t, "zh", [(0, 1), (1, 0), (2, 3), (3, 2)])
+    with jax.named_scope("weights_pairs"):
+        two = call(
+            pair_kernel,
+            jax.ShapeDtypeStruct((2, COLS, CHANS), BF16),
+            specs=[SCALAR, WHOLE, WHOLE, FAR],
+            flops=6000000000,
+        )(zh_here, w_t, w_near, w_t)
     with jax.named_scope("states"):
-        packed, inside = call(
+        totals, inside = call(
             state_kernel,
             [
-                jax.ShapeDtypeStruct((16, PACK, LANES), BF16),
+                jax.ShapeDtypeStruct((16, ORDER, LANES), BF16),
                 jax.ShapeDtypeStruct((GROUPS, ORDER, LANES), F32),
             ],
-            [tokens, rows, pltpu.VMEM((COLS, CHANS), BF16), pltpu.SemaphoreType.DMA],
-            [SCALAR, WHOLE, WHOLE, FAR],
-        )(member, blocks, rate_t, w_t)
-        packed = exchange(packed, ("x", "zh"))
+            [tokens, rows],
+            [SCALAR, WHOLE, WHOLE, FAR, FAR],
+        )(member, blocks, rate_t, two, w_t)
+        packed = exchange(totals, ("x", "zh"))
+    with jax.named_scope("weights_quads"):
+        ring = [(x, zh, t0) for x in range(4) for zh in range(4) for t0 in range(2)]
+        number = {place: i for i, place in enumerate(ring)}
+
+        def swapped(zh_from):
+            moves = []
+            for x, zh, t0 in ring:
+                here = (x, t0) if x % 2 == t0 else (x ^ 1, 1 - t0)
+                moves.append((number[here[0], zh_from(zh), here[1]], number[x, zh, t0]))
+            return lax.ppermute(two, ("x", "zh", "t0"), moves)
+
+        other_two = swapped(lambda zh: 3 - zh)
+        own_two = swapped(lambda zh: zh)
+        quarter = call(
+            quad_kernel,
+            jax.ShapeDtypeStruct((2, 2, COLS, CHANS), BF16),
+            specs=[SCALAR, WHOLE, WHOLE],
+        )(zh_here, own_two, other_two).reshape(4, COLS, CHANS)
     with jax.named_scope("local"):
         y_tok = call(
             local_kernel,
             jax.ShapeDtypeStruct((TOK * GROUPS, LANES), F32),
             [tokens],
-            [SCALAR, WHOLE, WHOLE, WHOLE],
-        )(member, blocks, rate_t, res_t)
+            [SCALAR, WHOLE, WHOLE, WHOLE, FAR],
+            flops=2000000000,
+        )(member, blocks, rate_t, res_t, quarter)
     with jax.named_scope("weights"):
-        quarter = packed[:, :QUARTER]
         further = [
             lax.ppermute(quarter, "x", [(i, (i - k) % 4) for i in range(4)]) for k in (1, 2, 3)
         ]
@@ -266,8 +298,8 @@
             carry_kernel,
             jax.ShapeDtypeStruct((2 * GROUPS, 4, TOK, LANES), BF16),
             [tokens, rows],
-            [SCALAR, SCALAR] + [WHOLE] * 7,
-        )(member, group, packed, inside, y_tok, blocks, rate_t, res_t, skip)
+            [SCALAR, SCALAR] + [WHOLE] * 7 + [FAR],
+        )(member, group, packed, inside, y_tok, blocks, rate_t, res_t, skip, w_t)
         gated = exchange(gated, ("y", "core", "t0"))
     with jax.named_scope("project"):
         shares = call(

time: 121 us -> 114 us (0.942)
  waiting for transfers between devices: 32.6 us -> 18 us
  starting transfers between devices: 53.9 us -> 62.6 us
    ppermute x1 -> x3, starting transfers between devices: 0.65 us -> 19.4 us  [the longest x1 9.77 us: per_device(): w_near = lax.ppermute(w_t, 'zh', [(0, 1), (1, 0), (2, 3), (3, 2)])]
    all_to_all x3, waiting for transfers between devices: 28.6 us -> 13.9 us  [exchange(): return lax.all_to_all(blocks, axis, split_axis=0, concat_axis=0, tiled=True)]
    all_to_all x3, starting transfers between devices: 34 us -> 24 us  [exchange(): return lax.all_to_all(blocks, axis, split_axis=0, concat_axis=0, tiled=True)]
  transfers between devices with their start and end apart: 11 -> 13, of which waited for: 6 -> 5; matrix products, arithmetic and copies ran while one was open for 0% -> 0% of each run, Pallas kernels for 2% -> 5%
where the time goes in v6:
time: 114 us; the launch traced here: 113 us
  starting transfers between devices  62.6 us (55%)
  blocking collectives  19.8 us (17%)
  waiting for transfers between devices  18 us (16%)
  Pallas kernels  10.1 us (9%)
  local copies, waits for them, and re-layouts  2.22 us (2%)
    all_to_all x3, starting transfers between devices, exchange(): return lax.all_to_all(blocks, axis, split_axis=0, concat_axis=0, tiled=True)  24 us
    all_to_all x1, blocking collectives, exchange(): return lax.all_to_all(blocks, axis, split_axis=0, concat_axis=0, tiled=True)  19.8 us
    all_to_all x3, waiting for transfers between devices, exchange(): return lax.all_to_all(blocks, axis, split_axis=0, concat_axis=0, tiled=True)  13.9 us
    ppermute x4, starting transfers between devices, per_device(): other = [lax.ppermute(block, 'core', [(0, 1), (1, 0)]) for block in own]  11.6 us
    ppermute x1, starting transfers between devices, per_device(): w_near = lax.ppermute(w_t, 'zh', [(0, 1), (1, 0), (2, 3), (3, 2)])  9.77 us
    ppermute x2, starting transfers between devices, swapped(): return lax.ppermute(two, ('x', 'zh', 't0'), moves)  9.62 us
    ppermute x3, starting transfers between devices, per_device(): lax.ppermute(quarter, 'x', [(i, (i - k) % 4) for i in range(4)])  7.63 us
    ppermute x3, waiting for transfers between devices, per_device(): lax.ppermute(quarter, 'x', [(i, (i - k) % 4) for i in range(4)])  2.97 us
  transfers between devices with their start and end apart: 13, of which 5 were waited for; matrix products, arithmetic and copies ran while one was open for 0% of the time, Pallas kernels for 5%

profile of v6, /device:TPU:1, one launch (start us, length us, event | category | flops | bytes accessed | tf_op | source)
XLA Modules:
  0.0 113.0 jit_solution(10414068948739582168)
XLA Ops:
  0.0 0.0 copy-start.3
  0.0 9.8 %collective-permute-start = (bf16[32,1024]{1,0:T(8,128)(2,1)}, bf16[32,1024]{1,0:T(8,128)(2,1)S(1)}, u32[]{:S(2)}, u32[]{:S(2)}) collective-permute-start(bf16[32,1024]{1,0:T(8,128)(2,1)} %bitcast.23), channel_id=1, source_target_pairs={{0,32},{32,0},{64,96},{96,64},{1,33},{33,1},{65,97},{97,65},{2,34}... | collective-permute-start | bytes 196616 | tf_op jit(solution)/shard_map/weights_zh/ppermute | solution.py:240
  9.8 2.0 %prepare.1 = bf16[8,2,128,128]{3,2,1,0:T(8,128)(2,1)} custom-call(bf16[128,1024]{1,0:T(8,128)(2,1)} %keys_far.1, bf16[128,1024]{1,0:T(8,128)(2,1)} %values_far.1, bf16[128,1024]{1,0:T(8,128)(2,1)} %query_far.1), custom_call_target="tpu_custom_call" | custom-call | tf_op jit(solution)/shard_map/prepare/pallas_call | solution.py:230
  11.8 5.4 %all-to-all-start = ((bf16[8,2,128,128]{3,2,1,0:T(8,128)(2,1)}), bf16[8,2,128,128]{3,2,1,0:T(8,128)(2,1)S(1)}, u32[]{:S(2)}, u32[]{:S(2)}) async-start(bf16[8,2,128,128]{3,2,1,0:T(8,128)(2,1)} %prepare.1), calls=%async_computation | async-start | bytes 1048576 | tf_op jit(solution)/shard_map/prepare/all_to_all | solution.py:204
  17.2 0.0 collective-permute-done.other
  17.2 0.0 copy-done.3
  17.2 0.0 copy-start.2
  17.2 0.0 copy-start.4
  17.3 0.8 collective-permute-start.1
  18.1 8.8 %collective-permute-start.2 = (bf16[2,32,1024]{2,1,0:T(8,128)(2,1)S(1)}, bf16[2,32,1024]{2,1,0:T(8,128)(2,1)S(1)}, u32[]{:S(2)}, u32[]{:S(2)}) collective-permute-start(bf16[2,32,1024]{2,1,0:T(8,128)(2,1)S(1)} %weights_pairs.1.after), channel_id=1, source_target_pairs={{96,0},{224,1},{64,32},{192,33},{32,64},{160,65},{0,96},{128,97},{... | collective-permute-start | bytes 393224 | tf_op jit(solution)/shard_map/weights_quads/ppermute | solution.py:268
  26.9 0.0 all-to-all-done.blocks
  26.9 0.0 copy-done.2
  26.9 1.4 %states.1 = (bf16[16,16,128]{2,1,0:T(8,128)(2,1)}, f32[8,16,128]{2,1,0:T(8,128)S(1)}) custom-call(s32[1]{0:T(128)S(6)} %add.6.member, bf16[8,2,128,128]{3,2,1,0:T(8,128)(2,1)S(1)} %all-to-all-done.blocks, f32[16,1024]{1,0:T(8,128)S(1)} %bitcast.20, bf16[2,32,1024]{2,1,0:T(8,128)(2,1)S(1)} %weights_pairs.1.after, bf16[32,1024]{1,0:T(8,128)(2,1)S(1)} %bitcast.26), custom_call_target="tpu_custom_call" | custom-call | tf_op jit(solution)/shard_map/states/pallas_call | solution.py:249
  28.3 12.3 %all-to-all-start.1 = ((bf16[16,16,128]{2,1,0:T(8,128)(2,1)}), bf16[16,16,128]{2,1,0:T(8,128)(2,1)S(1)}, u32[]{:S(2)}, u32[]{:S(2)}) async-start(bf16[16,16,128]{2,1,0:T(8,128)(2,1)} %get-tuple-element.9), calls=%async_computation.1 | async-start | bytes 131072 | tf_op jit(solution)/shard_map/states/all_to_all | solution.py:204
  40.7 0.0 collective-permute-done.1.own
  40.7 0.0 collective-permute-done.2.other
  40.7 0.0 copy-done.4
  40.7 0.0 copy-start.5
  40.8 1.3 %local.1.y_tok = f32[1024,128]{1,0:T(8,128)S(1)} custom-call(s32[1]{0:T(128)S(6)} %add.6.member, bf16[8,2,128,128]{3,2,1,0:T(8,128)(2,1)S(1)} %all-to-all-done.blocks, f32[16,1024]{1,0:T(8,128)S(1)} %bitcast.21, f32[16,1024]{1,0:T(8,128)S(1)} %bitcast.28, bf16[4,32,1024]{2,1,0:T(8,128)(2,1)S(1)} %bitcast.14), custom_call_target="tpu_custom_call" | custom-call | flops 2000000000 | tf_op jit(solution)/shard_map/local/pallas_call | solution.py:278
  42.1 12.6 %all-to-all-done.1.packs = bf16[16,16,128]{2,1,0:T(8,128)(2,1)S(1)} async-done(((bf16[16,16,128]{2,1,0:T(8,128)(2,1)}), bf16[16,16,128]{2,1,0:T(8,128)(2,1)S(1)}, u32[]{:S(2)}, u32[]{:S(2)}) %all-to-all-start.1) | async-done | bytes 65568 | tf_op jit(solution)/shard_map/states/all_to_all | solution.py:204
  54.7 0.0 copy-done.5
  54.7 2.3 %gate.1 = bf16[16,4,128,128]{3,2,1,0:T(8,128)(2,1)} custom-call(s32[1]{0:T(128)S(6)} %add.6.member, s32[1]{0:T(128)} %bitcast.2.group, bf16[16,16,128]{2,1,0:T(8,128)(2,1)S(1)} %all-to-all-done.1.packs, f32[8,16,128]{2,1,0:T(8,128)S(1)} %get-tuple-element.10.inside, f32[1024,128]{1,0:T(8,128)S(1)} %local.1.y_tok, ...), custom_call_target="tpu_custom_call" | custom-call | tf_op jit(solution)/shard_map/gate/pallas_call | solution.py:297
  56.9 6.3 %all-to-all-start.2 = ((bf16[16,4,128,128]{3,2,1,0:T(8,128)(2,1)}), bf16[16,4,128,128]{3,2,1,0:T(8,128)(2,1)S(1)}, u32[]{:S(2)}, u32[]{:S(2)}) async-start(bf16[16,4,128,128]{3,2,1,0:T(8,128)(2,1)} %gate.1), calls=%async_computation.2 | async-start | bytes 4194304 | tf_op jit(solution)/shard_map/gate/all_to_all | solution.py:204
  63.2 2.6 %collective-permute-start.3 = (bf16[4,32,1024]{2,1,0:T(8,128)(2,1)S(1)}, bf16[4,32,1024]{2,1,0:T(8,128)(2,1)S(1)}, u32[]{:S(2)}, u32[]{:S(2)}) collective-permute-start(bf16[4,32,1024]{2,1,0:T(8,128)(2,1)S(1)} %bitcast.15), channel_id=1, source_target_pairs={{0,384},{128,0},{256,128},{384,256},{1,385},{129,1},{257,129},{385... | collective-permute-start | bytes 786440 | tf_op jit(solution)/shard_map/weights/ppermute | solution.py:287
  65.8 3.1 %collective-permute-start.4 = (bf16[4,32,1024]{2,1,0:T(8,128)(2,1)S(1)}, bf16[4,32,1024]{2,1,0:T(8,128)(2,1)S(1)}, u32[]{:S(2)}, u32[]{:S(2)}) collective-permute-start(bf16[4,32,1024]{2,1,0:T(8,128)(2,1)S(1)} %bitcast.16), channel_id=1, source_target_pairs={{0,256},{128,384},{256,0},{384,128},{1,257},{129,385},{257,1},{385... | collective-permute-start | bytes 786440 | tf_op jit(solution)/shard_map/weights/ppermute | solution.py:287
  68.9 1.9 %collective-permute-start.5 = (bf16[4,32,1024]{2,1,0:T(8,128)(2,1)S(1)}, bf16[4,32,1024]{2,1,0:T(8,128)(2,1)S(1)}, u32[]{:S(2)}, u32[]{:S(2)}) collective-permute-start(bf16[4,32,1024]{2,1,0:T(8,128)(2,1)S(1)} %bitcast.17), channel_id=1, source_target_pairs={{0,128},{128,256},{256,384},{384,0},{1,129},{129,257},{257,385},{3... | collective-permute-start | bytes 786440 | tf_op jit(solution)/shard_map/weights/ppermute | solution.py:287
  70.9 2.5 %collective-permute-start.6 = (bf16[4,32,1024]{2,1,0:T(8,128)(2,1)S(1)}, bf16[4,32,1024]{2,1,0:T(8,128)(2,1)S(1)}, u32[]{:S(2)}, u32[]{:S(2)}) collective-permute-start(bf16[4,32,1024]{2,1,0:T(8,128)(2,1)S(1)} %bitcast.18), channel_id=1, source_target_pairs={{0,4},{4,0},{1,5},{5,1},{2,6},{6,2},{3,7},{7,3},{8,12},{12,8},{9,1... | collective-permute-start | bytes 786440 | tf_op jit(solution)/shard_map/weights/ppermute | solution.py:290
  73.4 0.0 collective-permute-done.3.refs_1_
  73.4 2.8 %collective-permute-start.7 = (bf16[4,32,1024]{2,1,0:T(8,128)(2,1)S(1)}, bf16[4,32,1024]{2,1,0:T(8,128)(2,1)S(1)}, u32[]{:S(2)}, u32[]{:S(2)}) collective-permute-start(bf16[4,32,1024]{2,1,0:T(8,128)(2,1)S(1)} %collective-permute-done.3.refs_1_), channel_id=1, source_target_pairs={{0,4},{4,0},{1,5},{5,1},{2,6},{6,2},{3,7},{7,3},{8,12},{12,8},{9,1... | collective-permute-start | bytes 786440 | tf_op jit(solution)/shard_map/weights/ppermute | solution.py:290
  76.2 0.6 collective-permute-done.4.refs_2_
  76.8 3.9 %collective-permute-start.8 = (bf16[4,32,1024]{2,1,0:T(8,128)(2,1)S(1)}, bf16[4,32,1024]{2,1,0:T(8,128)(2,1)S(1)}, u32[]{:S(2)}, u32[]{:S(2)}) collective-permute-start(bf16[4,32,1024]{2,1,0:T(8,128)(2,1)S(1)} %collective-permute-done.4.refs_2_), channel_id=1, source_target_pairs={{0,4},{4,0},{1,5},{5,1},{2,6},{6,2},{3,7},{7,3},{8,12},{12,8},{9,1... | collective-permute-start | bytes 786440 | tf_op jit(solution)/shard_map/weights/ppermute | solution.py:290
  80.7 2.4 %collective-permute-done.5.refs_3_ = bf16[4,32,1024]{2,1,0:T(8,128)(2,1)S(1)} collective-permute-done((bf16[4,32,1024]{2,1,0:T(8,128)(2,1)S(1)}, bf16[4,32,1024]{2,1,0:T(8,128)(2,1)S(1)}, u32[]{:S(2)}, u32[]{:S(2)}) %collective-permute-start.5) | collective-permute-done | bytes 262176 | tf_op jit(solution)/shard_map/weights/ppermute | solution.py:287
  83.1 2.4 %collective-permute-start.9 = (bf16[4,32,1024]{2,1,0:T(8,128)(2,1)S(1)}, bf16[4,32,1024]{2,1,0:T(8,128)(2,1)S(1)}, u32[]{:S(2)}, u32[]{:S(2)}) collective-permute-start(bf16[4,32,1024]{2,1,0:T(8,128)(2,1)S(1)} %collective-permute-done.5.refs_3_), channel_id=1, source_target_pairs={{0,4},{4,0},{1,5},{5,1},{2,6},{6,2},{3,7},{7,3},{8,12},{12,8},{9,1... | collective-permute-start | bytes 786440 | tf_op jit(solution)/shard_map/weights/ppermute | solution.py:290
  85.5 0.0 collective-permute-done.6.refs_4_
  85.5 0.0 collective-permute-done.7.refs_5_
  85.5 0.0 collective-permute-done.8.refs_6_
  85.5 1.1 collective-permute-done.9.refs_7_
  86.6 0.8 weights.1
  87.5 0.0 copy-start
  87.5 1.0 copy-done
  88.4 1.3 %all-to-all-done.2.gated = bf16[16,4,128,128]{3,2,1,0:T(8,128)(2,1)S(1)} async-done(((bf16[16,4,128,128]{3,2,1,0:T(8,128)(2,1)}), bf16[16,4,128,128]{3,2,1,0:T(8,128)(2,1)S(1)}, u32[]{:S(2)}, u32[]{:S(2)}) %all-to-all-start.2) | async-done | bytes 2097184 | tf_op jit(solution)/shard_map/gate/all_to_all | solution.py:204
  89.7 0.0 copy-start.1
  89.7 1.2 %copy-done.1 = bf16[2048,256]{1,0:T(8,128)(2,1)S(1)} copy-done((bf16[2048,256]{1,0:T(8,128)(2,1)S(1)}, bf16[2048,256]{1,0:T(8,128)(2,1)}, u32[]{:S(2)}) %copy-start.1) | copy-done | bytes 1048600
  91.0 1.3 %project.1 = bf16[4,2,128,256]{3,2,1,0:T(8,128)(2,1)S(1)} custom-call(bf16[16,4,128,128]{3,2,1,0:T(8,128)(2,1)S(1)} %all-to-all-done.2.gated, bf16[2048,256]{1,0:T(8,128)(2,1)S(1)} %get-tuple-element.11.w0, bf16[2048,256]{1,0:T(8,128)(2,1)S(1)} %copy-done.1), custom_call_target="tpu_custom_call" | custom-call | tf_op jit(solution)/shard_map/project/pallas_call | solution.py:305
  92.2 19.8 %all_to_all.20 = bf16[8,128,256]{2,1,0:T(8,128)(2,1)S(1)} all-to-all(bf16[8,128,256]{2,1,0:T(8,128)(2,1)S(1)} %bitcast.12), channel_id=1, replica_groups=mesh['x'=4,'zh'=4,'y'=4,'core'=2,'t1'=2,'t0'=2] {'y','t1'}, dimensions={0} | all-to-all | bytes 1048576 | tf_op jit(solution)/shard_map/reduce/all_to_all | solution.py:204
  112.0 1.0 reduce.1
  (2 shorter events, 0.0 us)
Async XLA Ops:
  0.0 17.2 %copy-start.3 = (bf16[1024,32]{0,1:T(8,128)(2,1)S(1)}, bf16[1024,32]{0,1:T(8,128)(2,1)}, u32[]{:S(2)}) copy-start(bf16[1024,32]{0,1:T(8,128)(2,1)} %param.13) | copy-start | bytes 196612
  0.0 17.2 %collective-permute-start = (bf16[32,1024]{1,0:T(8,128)(2,1)}, bf16[32,1024]{1,0:T(8,128)(2,1)S(1)}, u32[]{:S(2)}, u32[]{:S(2)}) collective-permute-start(bf16[32,1024]{1,0:T(8,128)(2,1)} %bitcast.23), channel_id=1, source_target_pairs={{0,32},{32,0},{64,96},{96,64},{1,33},{33,1},{65,97},{97,65},{2,34}... | collective-permute-start | bytes 196616 | tf_op jit(solution)/shard_map/weights_zh/ppermute | solution.py:240
  11.8 15.1 %all-to-all-start = ((bf16[8,2,128,128]{3,2,1,0:T(8,128)(2,1)}), bf16[8,2,128,128]{3,2,1,0:T(8,128)(2,1)S(1)}, u32[]{:S(2)}, u32[]{:S(2)}) async-start(bf16[8,2,128,128]{3,2,1,0:T(8,128)(2,1)} %prepare.1), calls=%async_computation | async-start | bytes 1048576 | tf_op jit(solution)/shard_map/prepare/all_to_all | solution.py:204
  17.2 9.7 %copy-start.2 = (f32[1024,16]{0,1:T(8,128)S(1)}, f32[1024,16]{0,1:T(8,128)}, u32[]{:S(2)}) copy-start(f32[1024,16]{0,1:T(8,128)} %param.11) | copy-start | bytes 196612
  17.2 23.5 %copy-start.4 = (f32[1024,16]{0,1:T(8,128)S(1)}, f32[1024,16]{0,1:T(8,128)}, u32[]{:S(2)}) copy-start(f32[1024,16]{0,1:T(8,128)} %param.10) | copy-start | bytes 196612
  17.3 23.4 %collective-permute-start.1 = (bf16[2,32,1024]{2,1,0:T(8,128)(2,1)S(1)}, bf16[2,32,1024]{2,1,0:T(8,128)(2,1)S(1)}, u32[]{:S(2)}, u32[]{:S(2)}) collective-permute-start(bf16[2,32,1024]{2,1,0:T(8,128)(2,1)S(1)} %weights_pairs.1.after), channel_id=1, source_target_pairs={{0,0},{128,1},{32,32},{160,33},{64,64},{192,65},{96,96},{224,97},{... | collective-permute-start | bytes 393224 | tf_op jit(solution)/shard_map/weights_quads/ppermute | solution.py:268
  18.1 22.6 %collective-permute-start.2 = (bf16[2,32,1024]{2,1,0:T(8,128)(2,1)S(1)}, bf16[2,32,1024]{2,1,0:T(8,128)(2,1)S(1)}, u32[]{:S(2)}, u32[]{:S(2)}) collective-permute-start(bf16[2,32,1024]{2,1,0:T(8,128)(2,1)S(1)} %weights_pairs.1.after), channel_id=1, source_target_pairs={{96,0},{224,1},{64,32},{192,33},{32,64},{160,65},{0,96},{128,97},{... | collective-permute-start | bytes 393224 | tf_op jit(solution)/shard_map/weights_quads/ppermute | solution.py:268
  28.3 26.3 %all-to-all-start.1 = ((bf16[16,16,128]{2,1,0:T(8,128)(2,1)}), bf16[16,16,128]{2,1,0:T(8,128)(2,1)S(1)}, u32[]{:S(2)}, u32[]{:S(2)}) async-start(bf16[16,16,128]{2,1,0:T(8,128)(2,1)} %get-tuple-element.9), calls=%async_computation.1 | async-start | bytes 131072 | tf_op jit(solution)/shard_map/states/all_to_all | solution.py:204
  40.7 13.9 %copy-start.5 = (f32[1024]{0:T(1024)S(1)}, f32[1024]{0:T(1024)}, u32[]{:S(2)}) copy-start(f32[1024]{0:T(1024)} %param.12) | copy-start | bytes 12292
  56.9 32.8 %all-to-all-start.2 = ((bf16[16,4,128,128]{3,2,1,0:T(8,128)(2,1)}), bf16[16,4,128,128]{3,2,1,0:T(8,128)(2,1)S(1)}, u32[]{:S(2)}, u32[]{:S(2)}) async-start(bf16[16,4,128,128]{3,2,1,0:T(8,128)(2,1)} %gate.1), calls=%async_computation.2 | async-start | bytes 4194304 | tf_op jit(solution)/shard_map/gate/all_to_all | solution.py:204
  63.2 10.2 %collective-permute-start.3 = (bf16[4,32,1024]{2,1,0:T(8,128)(2,1)S(1)}, bf16[4,32,1024]{2,1,0:T(8,128)(2,1)S(1)}, u32[]{:S(2)}, u32[]{:S(2)}) collective-permute-start(bf16[4,32,1024]{2,1,0:T(8,128)(2,1)S(1)} %bitcast.15), channel_id=1, source_target_pairs={{0,384},{128,0},{256,128},{384,256},{1,385},{129,1},{257,129},{385... | collective-permute-start | bytes 786440 | tf_op jit(solution)/shard_map/weights/ppermute | solution.py:287
  65.8 11.0 %collective-permute-start.4 = (bf16[4,32,1024]{2,1,0:T(8,128)(2,1)S(1)}, bf16[4,32,1024]{2,1,0:T(8,128)(2,1)S(1)}, u32[]{:S(2)}, u32[]{:S(2)}) collective-permute-start(bf16[4,32,1024]{2,1,0:T(8,128)(2,1)S(1)} %bitcast.16), channel_id=1, source_target_pairs={{0,256},{128,384},{256,0},{384,128},{1,257},{129,385},{257,1},{385... | collective-permute-start | bytes 786440 | tf_op jit(solution)/shard_map/weights/ppermute | solution.py:287
  68.9 14.1 %collective-permute-start.5 = (bf16[4,32,1024]{2,1,0:T(8,128)(2,1)S(1)}, bf16[4,32,1024]{2,1,0:T(8,128)(2,1)S(1)}, u32[]{:S(2)}, u32[]{:S(2)}) collective-permute-start(bf16[4,32,1024]{2,1,0:T(8,128)(2,1)S(1)} %bitcast.17), channel_id=1, source_target_pairs={{0,128},{128,256},{256,384},{384,0},{1,129},{129,257},{257,385},{3... | collective-permute-start | bytes 786440 | tf_op jit(solution)/shard_map/weights/ppermute | solution.py:287
  70.9 14.6 %collective-permute-start.6 = (bf16[4,32,1024]{2,1,0:T(8,128)(2,1)S(1)}, bf16[4,32,1024]{2,1,0:T(8,128)(2,1)S(1)}, u32[]{:S(2)}, u32[]{:S(2)}) collective-permute-start(bf16[4,32,1024]{2,1,0:T(8,128)(2,1)S(1)} %bitcast.18), channel_id=1, source_target_pairs={{0,4},{4,0},{1,5},{5,1},{2,6},{6,2},{3,7},{7,3},{8,12},{12,8},{9,1... | collective-permute-start | bytes 786440 | tf_op jit(solution)/shard_map/weights/ppermute | solution.py:290
  73.4 12.1 %collective-permute-start.7 = (bf16[4,32,1024]{2,1,0:T(8,128)(2,1)S(1)}, bf16[4,32,1024]{2,1,0:T(8,128)(2,1)S(1)}, u32[]{:S(2)}, u32[]{:S(2)}) collective-permute-start(bf16[4,32,1024]{2,1,0:T(8,128)(2,1)S(1)} %collective-permute-done.3.refs_1_), channel_id=1, source_target_pairs={{0,4},{4,0},{1,5},{5,1},{2,6},{6,2},{3,7},{7,3},{8,12},{12,8},{9,1... | collective-permute-start | bytes 786440 | tf_op jit(solution)/shard_map/weights/ppermute | solution.py:290
  76.8 8.7 %collective-permute-start.8 = (bf16[4,32,1024]{2,1,0:T(8,128)(2,1)S(1)}, bf16[4,32,1024]{2,1,0:T(8,128)(2,1)S(1)}, u32[]{:S(2)}, u32[]{:S(2)}) collective-permute-start(bf16[4,32,1024]{2,1,0:T(8,128)(2,1)S(1)} %collective-permute-done.4.refs_2_), channel_id=1, source_target_pairs={{0,4},{4,0},{1,5},{5,1},{2,6},{6,2},{3,7},{7,3},{8,12},{12,8},{9,1... | collective-permute-start | bytes 786440 | tf_op jit(solution)/shard_map/weights/ppermute | solution.py:290
  83.1 3.5 %collective-permute-start.9 = (bf16[4,32,1024]{2,1,0:T(8,128)(2,1)S(1)}, bf16[4,32,1024]{2,1,0:T(8,128)(2,1)S(1)}, u32[]{:S(2)}, u32[]{:S(2)}) collective-permute-start(bf16[4,32,1024]{2,1,0:T(8,128)(2,1)S(1)} %collective-permute-done.5.refs_3_), channel_id=1, source_target_pairs={{0,4},{4,0},{1,5},{5,1},{2,6},{6,2},{3,7},{7,3},{8,12},{12,8},{9,1... | collective-permute-start | bytes 786440 | tf_op jit(solution)/shard_map/weights/ppermute | solution.py:290
  87.5 1.0 copy-start
  89.7 1.2 %copy-start.1 = (bf16[2048,256]{1,0:T(8,128)(2,1)S(1)}, bf16[2048,256]{1,0:T(8,128)(2,1)}, u32[]{:S(2)}) copy-start(bf16[2048,256]{1,0:T(8,128)(2,1)} %copy-done) | copy-start | bytes 3145732

commit v7 on v6

--- a/solution.py
+++ b/solution.py
@@ -144,7 +144,8 @@
     out[1 - low] = other[...]
 
 
-def quad_kernel(at, own, other, out):
+def quad_kernel(at, own, other, after, out):
+    del after
     high = at[0] // 2
     out[high] = own[...]
     out[1 - high] = other[...]
@@ -269,11 +270,6 @@
 
         other_two = swapped(lambda zh: 3 - zh)
         own_two = swapped(lambda zh: zh)
-        quarter = call(
-            quad_kernel,
-            jax.ShapeDtypeStruct((2, 2, COLS, CHANS), BF16),
-            specs=[SCALAR, WHOLE, WHOLE],
-        )(zh_here, own_two, other_two).reshape(4, COLS, CHANS)
     with jax.named_scope("local"):
         y_tok = call(
             local_kernel,
@@ -281,7 +277,13 @@
             [tokens],
             [SCALAR, WHOLE, WHOLE, WHOLE, FAR],
             flops=2000000000,
-        )(member, blocks, rate_t, res_t, quarter)
+        )(member, blocks, rate_t, res_t, other_two)
+    with jax.named_scope("weights_quads"):
+        quarter = call(
+            quad_kernel,
+            jax.ShapeDtypeStruct((2, 2, COLS, CHANS), BF16),
+            specs=[SCALAR, WHOLE, WHOLE, FAR],
+        )(zh_here, own_two, other_two, y_tok).reshape(4, COLS, CHANS)
     with jax.named_scope("weights"):
         further = [
             lax.ppermute(quarter, "x", [(i, (i - k) % 4) for i in range(4)]) for k in (1, 2, 3)
@@ -299,7 +301,7 @@
             jax.ShapeDtypeStruct((2 * GROUPS, 4, TOK, LANES), BF16),
             [tokens, rows],
             [SCALAR, SCALAR] + [WHOLE] * 7 + [FAR],
-        )(member, group, packed, inside, y_tok, blocks, rate_t, res_t, skip, w_t)
+        )(member, group, packed, inside, y_tok, blocks, rate_t, res_t, skip, quarter)
         gated = exchange(gated, ("y", "core", "t0"))
     with jax.named_scope("project"):
         shares = call(

time: 114 us -> 114 us (level)
  transfers between devices with their start and end apart: 13 -> 13, of which waited for: 5 -> 6; matrix products, arithmetic and copies ran while one was open for 0% -> 0% of each run, Pallas kernels for 5% -> 5%
where the time goes in v7:
time: 114 us; the launch traced here: 113 us
  starting transfers between devices  62.7 us (55%)
  blocking collectives  20.3 us (18%)
  waiting for transfers between devices  17.3 us (15%)
  Pallas kernels  10.1 us (9%)
  local copies, waits for them, and re-layouts  2.22 us (2%)
    all_to_all x3, starting transfers between devices, exchange(): return lax.all_to_all(blocks, axis, split_axis=0, concat_axis=0, tiled=True)  23.6 us
    all_to_all x1, blocking collectives, exchange(): return lax.all_to_all(blocks, axis, split_axis=0, concat_axis=0, tiled=True)  20.3 us
    all_to_all x3, waiting for transfers between devices, exchange(): return lax.all_to_all(blocks, axis, split_axis=0, concat_axis=0, tiled=True)  13.6 us
    ppermute x4, starting transfers between devices, per_device(): other = [lax.ppermute(block, 'core', [(0, 1), (1, 0)]) for block in own]  12 us
    ppermute x1, starting transfers between devices, per_device(): w_near = lax.ppermute(w_t, 'zh', [(0, 1), (1, 0), (2, 3), (3, 2)])  9.77 us
    ppermute x2, starting transfers between devices, swapped(): return lax.ppermute(two, ('x', 'zh', 't0'), moves)  9.62 us
    ppermute x3, starting transfers between devices, per_device(): lax.ppermute(quarter, 'x', [(i, (i - k) % 4) for i in range(4)])  7.65 us
    ppermute x3, waiting for transfers between devices, per_device(): lax.ppermute(quarter, 'x', [(i, (i - k) % 4) for i in range(4)])  2.64 us
  transfers between devices with their start and end apart: 13, of which 6 were waited for; matrix products, arithmetic and copies ran while one was open for 0% of the time, Pallas kernels for 5%

profile of v7, /device:TPU:1, one launch (start us, length us, event | category | flops | bytes accessed | tf_op | source)
XLA Modules:
  0.0 112.9 jit_solution(4444603088214329596)
XLA Ops:
  0.0 0.0 copy-start.4
  0.0 9.8 %collective-permute-start = (bf16[32,1024]{1,0:T(8,128)(2,1)}, bf16[32,1024]{1,0:T(8,128)(2,1)S(1)}, u32[]{:S(2)}, u32[]{:S(2)}) collective-permute-start(bf16[32,1024]{1,0:T(8,128)(2,1)} %bitcast.25), channel_id=1, source_target_pairs={{0,32},{32,0},{64,96},{96,64},{1,33},{33,1},{65,97},{97,65},{2,34}... | collective-permute-start | bytes 196616 | tf_op jit(solution)/shard_map/weights_zh/ppermute | solution.py:241
  9.8 2.0 %prepare.1 = bf16[8,2,128,128]{3,2,1,0:T(8,128)(2,1)} custom-call(bf16[128,1024]{1,0:T(8,128)(2,1)} %keys_far.1, bf16[128,1024]{1,0:T(8,128)(2,1)} %values_far.1, bf16[128,1024]{1,0:T(8,128)(2,1)} %query_far.1), custom_call_target="tpu_custom_call" | custom-call | tf_op jit(solution)/shard_map/prepare/pallas_call | solution.py:231
  11.8 5.4 %all-to-all-start = ((bf16[8,2,128,128]{3,2,1,0:T(8,128)(2,1)}), bf16[8,2,128,128]{3,2,1,0:T(8,128)(2,1)S(1)}, u32[]{:S(2)}, u32[]{:S(2)}) async-start(bf16[8,2,128,128]{3,2,1,0:T(8,128)(2,1)} %prepare.1), calls=%async_computation | async-start | bytes 1048576 | tf_op jit(solution)/shard_map/prepare/all_to_all | solution.py:205
  17.2 0.0 collective-permute-done.other
  17.2 0.0 copy-done.4
  17.2 0.0 copy-start.2
  17.2 0.0 copy-start.3
  17.3 8.9 %collective-permute-start.1 = (bf16[2,32,1024]{2,1,0:T(8,128)(2,1)S(1)}, bf16[2,32,1024]{2,1,0:T(8,128)(2,1)S(1)}, u32[]{:S(2)}, u32[]{:S(2)}) collective-permute-start(bf16[2,32,1024]{2,1,0:T(8,128)(2,1)S(1)} %weights_pairs.1.after), channel_id=1, source_target_pairs={{96,0},{224,1},{64,32},{192,33},{32,64},{160,65},{0,96},{128,97},{... | collective-permute-start | bytes 393224 | tf_op jit(solution)/shard_map/weights_quads/ppermute | solution.py:269
  26.2 0.5 all-to-all-done.blocks
  26.7 0.0 copy-done.2
  26.7 1.4 %states.1 = (bf16[16,16,128]{2,1,0:T(8,128)(2,1)}, f32[8,16,128]{2,1,0:T(8,128)S(1)}) custom-call(s32[1]{0:T(128)S(6)} %add.6.member, bf16[8,2,128,128]{3,2,1,0:T(8,128)(2,1)S(1)} %all-to-all-done.blocks, f32[16,1024]{1,0:T(8,128)S(1)} %bitcast.20, bf16[2,32,1024]{2,1,0:T(8,128)(2,1)S(1)} %weights_pairs.1.after, bf16[32,1024]{1,0:T(8,128)(2,1)S(1)} %bitcast.28), custom_call_target="tpu_custom_call" | custom-call | tf_op jit(solution)/shard_map/states/pallas_call | solution.py:250
  28.1 12.6 %all-to-all-start.1 = ((bf16[16,16,128]{2,1,0:T(8,128)(2,1)}), bf16[16,16,128]{2,1,0:T(8,128)(2,1)S(1)}, u32[]{:S(2)}, u32[]{:S(2)}) async-start(bf16[16,16,128]{2,1,0:T(8,128)(2,1)} %get-tuple-element.9), calls=%async_computation.1 | async-start | bytes 131072 | tf_op jit(solution)/shard_map/states/all_to_all | solution.py:205
  40.7 0.7 collective-permute-start.2
  41.4 0.0 collective-permute-done.1.after.other
  41.4 0.0 copy-done.3
  41.4 0.0 copy-start.5
  41.4 1.3 %local.1.after.y_tok = f32[1024,128]{1,0:T(8,128)S(1)} custom-call(s32[1]{0:T(128)S(6)} %add.6.member, bf16[8,2,128,128]{3,2,1,0:T(8,128)(2,1)S(1)} %all-to-all-done.blocks, f32[16,1024]{1,0:T(8,128)S(1)} %bitcast.21, f32[16,1024]{1,0:T(8,128)S(1)} %bitcast.23, bf16[2,32,1024]{2,1,0:T(8,128)(2,1)S(1)} %collective-permute-done.1.after.other), custom_call_target="tpu_custom_call" | custom-call | flops 2000000000 | tf_op jit(solution)/shard_map/local/pallas_call | solution.py:274
  42.7 0.0 collective-permute-done.2.own
  42.8 11.9 %all-to-all-done.1.packs = bf16[16,16,128]{2,1,0:T(8,128)(2,1)S(1)} async-done(((bf16[16,16,128]{2,1,0:T(8,128)(2,1)}), bf16[16,16,128]{2,1,0:T(8,128)(2,1)S(1)}, u32[]{:S(2)}, u32[]{:S(2)}) %all-to-all-start.1) | async-done | bytes 65568 | tf_op jit(solution)/shard_map/states/all_to_all | solution.py:205
  54.7 0.0 copy-done.5
  54.7 2.3 %gate.1 = bf16[16,4,128,128]{3,2,1,0:T(8,128)(2,1)} custom-call(s32[1]{0:T(128)S(6)} %add.6.member, s32[1]{0:T(128)} %bitcast.2.group, bf16[16,16,128]{2,1,0:T(8,128)(2,1)S(1)} %all-to-all-done.1.packs, f32[8,16,128]{2,1,0:T(8,128)S(1)} %get-tuple-element.10.inside, f32[1024,128]{1,0:T(8,128)S(1)} %local.1.after.y_tok, ...), custom_call_target="tpu_custom_call" | custom-call | tf_op jit(solution)/shard_map/gate/pallas_call | solution.py:299
  57.0 5.6 %all-to-all-start.2 = ((bf16[16,4,128,128]{3,2,1,0:T(8,128)(2,1)}), bf16[16,4,128,128]{3,2,1,0:T(8,128)(2,1)S(1)}, u32[]{:S(2)}, u32[]{:S(2)}) async-start(bf16[16,4,128,128]{3,2,1,0:T(8,128)(2,1)} %gate.1), calls=%async_computation.2 | async-start | bytes 4194304 | tf_op jit(solution)/shard_map/gate/all_to_all | solution.py:205
  62.6 2.7 %collective-permute-start.3 = (bf16[4,32,1024]{2,1,0:T(8,128)(2,1)S(1)}, bf16[4,32,1024]{2,1,0:T(8,128)(2,1)S(1)}, u32[]{:S(2)}, u32[]{:S(2)}) collective-permute-start(bf16[4,32,1024]{2,1,0:T(8,128)(2,1)S(1)} %bitcast.13), channel_id=1, source_target_pairs={{0,384},{128,0},{256,128},{384,256},{1,385},{129,1},{257,129},{385... | collective-permute-start | bytes 786440 | tf_op jit(solution)/shard_map/weights/ppermute | solution.py:289
  65.3 3.0 %collective-permute-start.4 = (bf16[4,32,1024]{2,1,0:T(8,128)(2,1)S(1)}, bf16[4,32,1024]{2,1,0:T(8,128)(2,1)S(1)}, u32[]{:S(2)}, u32[]{:S(2)}) collective-permute-start(bf16[4,32,1024]{2,1,0:T(8,128)(2,1)S(1)} %bitcast.14), channel_id=1, source_target_pairs={{0,256},{128,384},{256,0},{384,128},{1,257},{129,385},{257,1},{385... | collective-permute-start | bytes 786440 | tf_op jit(solution)/shard_map/weights/ppermute | solution.py:289
  68.3 1.9 %collective-permute-start.5 = (bf16[4,32,1024]{2,1,0:T(8,128)(2,1)S(1)}, bf16[4,32,1024]{2,1,0:T(8,128)(2,1)S(1)}, u32[]{:S(2)}, u32[]{:S(2)}) collective-permute-start(bf16[4,32,1024]{2,1,0:T(8,128)(2,1)S(1)} %bitcast.15), channel_id=1, source_target_pairs={{0,128},{128,256},{256,384},{384,0},{1,129},{129,257},{257,385},{3... | collective-permute-start | bytes 786440 | tf_op jit(solution)/shard_map/weights/ppermute | solution.py:289
  70.3 2.7 %collective-permute-start.6 = (bf16[4,32,1024]{2,1,0:T(8,128)(2,1)S(1)}, bf16[4,32,1024]{2,1,0:T(8,128)(2,1)S(1)}, u32[]{:S(2)}, u32[]{:S(2)}) collective-permute-start(bf16[4,32,1024]{2,1,0:T(8,128)(2,1)S(1)} %bitcast.16), channel_id=1, source_target_pairs={{0,4},{4,0},{1,5},{5,1},{2,6},{6,2},{3,7},{7,3},{8,12},{12,8},{9,1... | collective-permute-start | bytes 786440 | tf_op jit(solution)/shard_map/weights/ppermute | solution.py:292
  73.0 0.0 collective-permute-done.3.refs_1_
  73.0 2.7 %collective-permute-start.7 = (bf16[4,32,1024]{2,1,0:T(8,128)(2,1)S(1)}, bf16[4,32,1024]{2,1,0:T(8,128)(2,1)S(1)}, u32[]{:S(2)}, u32[]{:S(2)}) collective-permute-start(bf16[4,32,1024]{2,1,0:T(8,128)(2,1)S(1)} %collective-permute-done.3.refs_1_), channel_id=1, source_target_pairs={{0,4},{4,0},{1,5},{5,1},{2,6},{6,2},{3,7},{7,3},{8,12},{12,8},{9,1... | collective-permute-start | bytes 786440 | tf_op jit(solution)/shard_map/weights/ppermute | solution.py:292
  75.7 0.4 collective-permute-done.4.refs_2_
  76.1 4.2 %collective-permute-start.8 = (bf16[4,32,1024]{2,1,0:T(8,128)(2,1)S(1)}, bf16[4,32,1024]{2,1,0:T(8,128)(2,1)S(1)}, u32[]{:S(2)}, u32[]{:S(2)}) collective-permute-start(bf16[4,32,1024]{2,1,0:T(8,128)(2,1)S(1)} %collective-permute-done.4.refs_2_), channel_id=1, source_target_pairs={{0,4},{4,0},{1,5},{5,1},{2,6},{6,2},{3,7},{7,3},{8,12},{12,8},{9,1... | collective-permute-start | bytes 786440 | tf_op jit(solution)/shard_map/weights/ppermute | solution.py:292
  80.4 2.2 %collective-permute-done.5.refs_3_ = bf16[4,32,1024]{2,1,0:T(8,128)(2,1)S(1)} collective-permute-done((bf16[4,32,1024]{2,1,0:T(8,128)(2,1)S(1)}, bf16[4,32,1024]{2,1,0:T(8,128)(2,1)S(1)}, u32[]{:S(2)}, u32[]{:S(2)}) %collective-permute-start.5) | collective-permute-done | bytes 262176 | tf_op jit(solution)/shard_map/weights/ppermute | solution.py:289
  82.6 2.4 %collective-permute-start.9 = (bf16[4,32,1024]{2,1,0:T(8,128)(2,1)S(1)}, bf16[4,32,1024]{2,1,0:T(8,128)(2,1)S(1)}, u32[]{:S(2)}, u32[]{:S(2)}) collective-permute-start(bf16[4,32,1024]{2,1,0:T(8,128)(2,1)S(1)} %collective-permute-done.5.refs_3_), channel_id=1, source_target_pairs={{0,4},{4,0},{1,5},{5,1},{2,6},{6,2},{3,7},{7,3},{8,12},{12,8},{9,1... | collective-permute-start | bytes 786440 | tf_op jit(solution)/shard_map/weights/ppermute | solution.py:292
  85.0 0.0 collective-permute-done.6.refs_4_
  85.0 0.0 collective-permute-done.7.refs_5_
  85.0 0.0 collective-permute-done.8.refs_6_
  85.0 1.1 collective-permute-done.9.refs_7_
  86.1 0.8 weights.1
  86.9 0.0 copy-start
  87.0 1.0 copy-done
  87.9 1.2 %all-to-all-done.2.gated = bf16[16,4,128,128]{3,2,1,0:T(8,128)(2,1)S(1)} async-done(((bf16[16,4,128,128]{3,2,1,0:T(8,128)(2,1)}), bf16[16,4,128,128]{3,2,1,0:T(8,128)(2,1)S(1)}, u32[]{:S(2)}, u32[]{:S(2)}) %all-to-all-start.2) | async-done | bytes 2097184 | tf_op jit(solution)/shard_map/gate/all_to_all | solution.py:205
  89.1 0.0 copy-start.1
  89.1 1.2 %copy-done.1 = bf16[2048,256]{1,0:T(8,128)(2,1)S(1)} copy-done((bf16[2048,256]{1,0:T(8,128)(2,1)S(1)}, bf16[2048,256]{1,0:T(8,128)(2,1)}, u32[]{:S(2)}) %copy-start.1) | copy-done | bytes 1048600
  90.4 1.3 %project.1 = bf16[4,2,128,256]{3,2,1,0:T(8,128)(2,1)S(1)} custom-call(bf16[16,4,128,128]{3,2,1,0:T(8,128)(2,1)S(1)} %all-to-all-done.2.gated, bf16[2048,256]{1,0:T(8,128)(2,1)S(1)} %get-tuple-element.11.w0, bf16[2048,256]{1,0:T(8,128)(2,1)S(1)} %copy-done.1), custom_call_target="tpu_custom_call" | custom-call | tf_op jit(solution)/shard_map/project/pallas_call | solution.py:307
  91.6 20.3 %all_to_all.20 = bf16[8,128,256]{2,1,0:T(8,128)(2,1)S(1)} all-to-all(bf16[8,128,256]{2,1,0:T(8,128)(2,1)S(1)} %bitcast.18), channel_id=1, replica_groups=mesh['x'=4,'zh'=4,'y'=4,'core'=2,'t1'=2,'t0'=2] {'y','t1'}, dimensions={0} | all-to-all | bytes 1048576 | tf_op jit(solution)/shard_map/reduce/all_to_all | solution.py:205
  111.9 1.0 reduce.1
  (2 shorter events, 0.0 us)
Async XLA Ops:
  0.0 17.2 %copy-start.4 = (bf16[1024,32]{0,1:T(8,128)(2,1)S(1)}, bf16[1024,32]{0,1:T(8,128)(2,1)}, u32[]{:S(2)}) copy-start(bf16[1024,32]{0,1:T(8,128)(2,1)} %param.13) | copy-start | bytes 196612
  0.0 17.2 %collective-permute-start = (bf16[32,1024]{1,0:T(8,128)(2,1)}, bf16[32,1024]{1,0:T(8,128)(2,1)S(1)}, u32[]{:S(2)}, u32[]{:S(2)}) collective-permute-start(bf16[32,1024]{1,0:T(8,128)(2,1)} %bitcast.25), channel_id=1, source_target_pairs={{0,32},{32,0},{64,96},{96,64},{1,33},{33,1},{65,97},{97,65},{2,34}... | collective-permute-start | bytes 196616 | tf_op jit(solution)/shard_map/weights_zh/ppermute | solution.py:241
  11.8 14.9 %all-to-all-start = ((bf16[8,2,128,128]{3,2,1,0:T(8,128)(2,1)}), bf16[8,2,128,128]{3,2,1,0:T(8,128)(2,1)S(1)}, u32[]{:S(2)}, u32[]{:S(2)}) async-start(bf16[8,2,128,128]{3,2,1,0:T(8,128)(2,1)} %prepare.1), calls=%async_computation | async-start | bytes 1048576 | tf_op jit(solution)/shard_map/prepare/all_to_all | solution.py:205
  17.2 9.5 %copy-start.2 = (f32[1024,16]{0,1:T(8,128)S(1)}, f32[1024,16]{0,1:T(8,128)}, u32[]{:S(2)}) copy-start(f32[1024,16]{0,1:T(8,128)} %param.11) | copy-start | bytes 196612
  17.2 24.1 %copy-start.3 = (f32[1024,16]{0,1:T(8,128)S(1)}, f32[1024,16]{0,1:T(8,128)}, u32[]{:S(2)}) copy-start(f32[1024,16]{0,1:T(8,128)} %param.10) | copy-start | bytes 196612
  17.3 24.1 %collective-permute-start.1 = (bf16[2,32,1024]{2,1,0:T(8,128)(2,1)S(1)}, bf16[2,32,1024]{2,1,0:T(8,128)(2,1)S(1)}, u32[]{:S(2)}, u32[]{:S(2)}) collective-permute-start(bf16[2,32,1024]{2,1,0:T(8,128)(2,1)S(1)} %weights_pairs.1.after), channel_id=1, source_target_pairs={{96,0},{224,1},{64,32},{192,33},{32,64},{160,65},{0,96},{128,97},{... | collective-permute-start | bytes 393224 | tf_op jit(solution)/shard_map/weights_quads/ppermute | solution.py:269
  28.1 26.6 %all-to-all-start.1 = ((bf16[16,16,128]{2,1,0:T(8,128)(2,1)}), bf16[16,16,128]{2,1,0:T(8,128)(2,1)S(1)}, u32[]{:S(2)}, u32[]{:S(2)}) async-start(bf16[16,16,128]{2,1,0:T(8,128)(2,1)} %get-tuple-element.9), calls=%async_computation.1 | async-start | bytes 131072 | tf_op jit(solution)/shard_map/states/all_to_all | solution.py:205
  40.7 2.0 %collective-permute-start.2 = (bf16[2,32,1024]{2,1,0:T(8,128)(2,1)S(1)}, bf16[2,32,1024]{2,1,0:T(8,128)(2,1)S(1)}, u32[]{:S(2)}, u32[]{:S(2)}) collective-permute-start(bf16[2,32,1024]{2,1,0:T(8,128)(2,1)S(1)} %weights_pairs.1.after), channel_id=1, source_target_pairs={{0,0},{128,1},{32,32},{160,33},{64,64},{192,65},{96,96},{224,97},{... | collective-permute-start | bytes 393224 | tf_op jit(solution)/shard_map/weights_quads/ppermute | solution.py:269
  41.4 13.3 %copy-start.5 = (f32[1024]{0:T(1024)S(1)}, f32[1024]{0:T(1024)}, u32[]{:S(2)}) copy-start(f32[1024]{0:T(1024)} %param.12) | copy-start | bytes 12292
  57.0 32.2 %all-to-all-start.2 = ((bf16[16,4,128,128]{3,2,1,0:T(8,128)(2,1)}), bf16[16,4,128,128]{3,2,1,0:T(8,128)(2,1)S(1)}, u32[]{:S(2)}, u32[]{:S(2)}) async-start(bf16[16,4,128,128]{3,2,1,0:T(8,128)(2,1)} %gate.1), calls=%async_computation.2 | async-start | bytes 4194304 | tf_op jit(solution)/shard_map/gate/all_to_all | solution.py:205
  62.6 10.4 %collective-permute-start.3 = (bf16[4,32,1024]{2,1,0:T(8,128)(2,1)S(1)}, bf16[4,32,1024]{2,1,0:T(8,128)(2,1)S(1)}, u32[]{:S(2)}, u32[]{:S(2)}) collective-permute-start(bf16[4,32,1024]{2,1,0:T(8,128)(2,1)S(1)} %bitcast.13), channel_id=1, source_target_pairs={{0,384},{128,0},{256,128},{384,256},{1,385},{129,1},{257,129},{385... | collective-permute-start | bytes 786440 | tf_op jit(solution)/shard_map/weights/ppermute | solution.py:289
  65.3 10.8 %collective-permute-start.4 = (bf16[4,32,1024]{2,1,0:T(8,128)(2,1)S(1)}, bf16[4,32,1024]{2,1,0:T(8,128)(2,1)S(1)}, u32[]{:S(2)}, u32[]{:S(2)}) collective-permute-start(bf16[4,32,1024]{2,1,0:T(8,128)(2,1)S(1)} %bitcast.14), channel_id=1, source_target_pairs={{0,256},{128,384},{256,0},{384,128},{1,257},{129,385},{257,1},{385... | collective-permute-start | bytes 786440 | tf_op jit(solution)/shard_map/weights/ppermute | solution.py:289
  68.3 14.2 %collective-permute-start.5 = (bf16[4,32,1024]{2,1,0:T(8,128)(2,1)S(1)}, bf16[4,32,1024]{2,1,0:T(8,128)(2,1)S(1)}, u32[]{:S(2)}, u32[]{:S(2)}) collective-permute-start(bf16[4,32,1024]{2,1,0:T(8,128)(2,1)S(1)} %bitcast.15), channel_id=1, source_target_pairs={{0,128},{128,256},{256,384},{384,0},{1,129},{129,257},{257,385},{3... | collective-permute-start | bytes 786440 | tf_op jit(solution)/shard_map/weights/ppermute | solution.py:289
  70.3 14.7 %collective-permute-start.6 = (bf16[4,32,1024]{2,1,0:T(8,128)(2,1)S(1)}, bf16[4,32,1024]{2,1,0:T(8,128)(2,1)S(1)}, u32[]{:S(2)}, u32[]{:S(2)}) collective-permute-start(bf16[4,32,1024]{2,1,0:T(8,128)(2,1)S(1)} %bitcast.16), channel_id=1, source_target_pairs={{0,4},{4,0},{1,5},{5,1},{2,6},{6,2},{3,7},{7,3},{8,12},{12,8},{9,1... | collective-permute-start | bytes 786440 | tf_op jit(solution)/shard_map/weights/ppermute | solution.py:292
  73.0 12.0 %collective-permute-start.7 = (bf16[4,32,1024]{2,1,0:T(8,128)(2,1)S(1)}, bf16[4,32,1024]{2,1,0:T(8,128)(2,1)S(1)}, u32[]{:S(2)}, u32[]{:S(2)}) collective-permute-start(bf16[4,32,1024]{2,1,0:T(8,128)(2,1)S(1)} %collective-permute-done.3.refs_1_), channel_id=1, source_target_pairs={{0,4},{4,0},{1,5},{5,1},{2,6},{6,2},{3,7},{7,3},{8,12},{12,8},{9,1... | collective-permute-start | bytes 786440 | tf_op jit(solution)/shard_map/weights/ppermute | solution.py:292
  76.1 8.9 %collective-permute-start.8 = (bf16[4,32,1024]{2,1,0:T(8,128)(2,1)S(1)}, bf16[4,32,1024]{2,1,0:T(8,128)(2,1)S(1)}, u32[]{:S(2)}, u32[]{:S(2)}) collective-permute-start(bf16[4,32,1024]{2,1,0:T(8,128)(2,1)S(1)} %collective-permute-done.4.refs_2_), channel_id=1, source_target_pairs={{0,4},{4,0},{1,5},{5,1},{2,6},{6,2},{3,7},{7,3},{8,12},{12,8},{9,1... | collective-permute-start | bytes 786440 | tf_op jit(solution)/shard_map/weights/ppermute | solution.py:292
  82.6 3.5 %collective-permute-start.9 = (bf16[4,32,1024]{2,1,0:T(8,128)(2,1)S(1)}, bf16[4,32,1024]{2,1,0:T(8,128)(2,1)S(1)}, u32[]{:S(2)}, u32[]{:S(2)}) collective-permute-start(bf16[4,32,1024]{2,1,0:T(8,128)(2,1)S(1)} %collective-permute-done.5.refs_3_), channel_id=1, source_target_pairs={{0,4},{4,0},{1,5},{5,1},{2,6},{6,2},{3,7},{7,3},{8,12},{12,8},{9,1... | collective-permute-start | bytes 786440 | tf_op jit(solution)/shard_map/weights/ppermute | solution.py:292
  86.9 1.0 copy-start
  89.1 1.2 %copy-start.1 = (bf16[2048,256]{1,0:T(8,128)(2,1)S(1)}, bf16[2048,256]{1,0:T(8,128)(2,1)}, u32[]{:S(2)}) copy-start(bf16[2048,256]{1,0:T(8,128)(2,1)} %copy-done) | copy-start | bytes 3145732

commit v8 on v7

--- a/solution.py
+++ b/solution.py
@@ -294,6 +294,7 @@
             join_kernel,
             [jax.ShapeDtypeStruct((2 * CHANS, 8 * COLS), BF16)] * 2,
             specs=[SCALAR, SCALAR] + [WHOLE] * 8,
+            flops=79000000000,
         )(lax.axis_index("x").reshape(1), core, *own, *other)
     with jax.named_scope("gate"):
         gated = call(

time: 114 us -> 114 us (level)
  local copies, waits for them, and re-layouts: 2.22 us -> 7.16 us
  waiting for transfers between devices: 17.3 us -> 14.2 us
  starting transfers between devices: 62.7 us -> 60.9 us
    unnamed x12 -> x24, local copies, waits for them, and re-layouts: 2.22 us -> 7.16 us
    ppermute x4, starting transfers between devices: 12 us -> 8.62 us  [per_device(): other = [lax.ppermute(block, 'core', [(0, 1), (1, 0)]) for block in own]]
    ppermute x3, waiting for transfers between devices: 2.64 us -> 0.01 us  [per_device(): lax.ppermute(quarter, 'x', [(i, (i - k) % 4) for i in range(4)])]
    ppermute x3, starting transfers between devices: 7.65 us -> 9.45 us  [per_device(): lax.ppermute(quarter, 'x', [(i, (i - k) % 4) for i in range(4)])]
  transfers between devices with their start and end apart: 13 -> 13, of which waited for: 6 -> 3; matrix products, arithmetic and copies ran while one was open for 0% -> 0% of each run, Pallas kernels for 5% -> 7%
where the time goes in v8:
time: 114 us; the launch traced here: 113 us
  starting transfers between devices  60.9 us (53%)
  blocking collectives  20.7 us (18%)
  waiting for transfers between devices  14.2 us (12%)
  Pallas kernels  10.1 us (9%)
  local copies, waits for them, and re-layouts  7.16 us (6%)
    all_to_all x3, starting transfers between devices, exchange(): return lax.all_to_all(blocks, axis, split_axis=0, concat_axis=0, tiled=True)  23.4 us
    all_to_all x1, blocking collectives, exchange(): return lax.all_to_all(blocks, axis, split_axis=0, concat_axis=0, tiled=True)  20.7 us
    all_to_all x3, waiting for transfers between devices, exchange(): return lax.all_to_all(blocks, axis, split_axis=0, concat_axis=0, tiled=True)  13.8 us
    ppermute x1, starting transfers between devices, per_device(): w_near = lax.ppermute(w_t, 'zh', [(0, 1), (1, 0), (2, 3), (3, 2)])  9.77 us
    ppermute x2, starting transfers between devices, swapped(): return lax.ppermute(two, ('x', 'zh', 't0'), moves)  9.62 us
    ppermute x3, starting transfers between devices, per_device(): lax.ppermute(quarter, 'x', [(i, (i - k) % 4) for i in range(4)])  9.45 us
    ppermute x4, starting transfers between devices, per_device(): other = [lax.ppermute(block, 'core', [(0, 1), (1, 0)]) for block in own]  8.62 us
    unnamed x24, local copies, waits for them, and re-layouts  7.16 us
  transfers between devices with their start and end apart: 13, of which 3 were waited for; matrix products, arithmetic and copies ran while one was open for 0% of the time, Pallas kernels for 7%

profile of v8, /device:TPU:1, one launch (start us, length us, event | category | flops | bytes accessed | tf_op | source)
XLA Modules:
  0.0 113.4 jit_solution(2258540921075533289)
XLA Ops:
  0.0 9.8 %collective-permute-start = (bf16[32,1024]{1,0:T(8,128)(2,1)}, bf16[32,1024]{1,0:T(8,128)(2,1)S(1)}, u32[]{:S(2)}, u32[]{:S(2)}) collective-permute-start(bf16[32,1024]{1,0:T(8,128)(2,1)} %bitcast.25), channel_id=1, source_target_pairs={{0,32},{32,0},{64,96},{96,64},{1,33},{33,1},{65,97},{97,65},{2,34}... | collective-permute-start | bytes 196616 | tf_op jit(solution)/shard_map/weights_zh/ppermute | solution.py:241
  9.8 2.0 %prepare.1 = bf16[8,2,128,128]{3,2,1,0:T(8,128)(2,1)} custom-call(bf16[128,1024]{1,0:T(8,128)(2,1)} %keys_far.1, bf16[128,1024]{1,0:T(8,128)(2,1)} %values_far.1, bf16[128,1024]{1,0:T(8,128)(2,1)} %query_far.1), custom_call_target="tpu_custom_call" | custom-call | tf_op jit(solution)/shard_map/prepare/pallas_call | solution.py:231
  11.8 5.4 %all-to-all-start = ((bf16[8,2,128,128]{3,2,1,0:T(8,128)(2,1)}), bf16[8,2,128,128]{3,2,1,0:T(8,128)(2,1)S(1)}, u32[]{:S(2)}, u32[]{:S(2)}) async-start(bf16[8,2,128,128]{3,2,1,0:T(8,128)(2,1)} %prepare.1), calls=%async_computation | async-start | bytes 1048576 | tf_op jit(solution)/shard_map/prepare/all_to_all | solution.py:205
  17.2 0.0 collective-permute-done.other
  17.2 0.0 copy-done.4
  17.2 0.0 copy-start.2
  17.2 0.0 copy-start.3
  17.3 8.9 %collective-permute-start.1 = (bf16[2,32,1024]{2,1,0:T(8,128)(2,1)S(1)}, bf16[2,32,1024]{2,1,0:T(8,128)(2,1)S(1)}, u32[]{:S(2)}, u32[]{:S(2)}) collective-permute-start(bf16[2,32,1024]{2,1,0:T(8,128)(2,1)S(1)} %weights_pairs.1.after), channel_id=1, source_target_pairs={{96,0},{224,1},{64,32},{192,33},{32,64},{160,65},{0,96},{128,97},{... | collective-permute-start | bytes 393224 | tf_op jit(solution)/shard_map/weights_quads/ppermute | solution.py:269
  26.2 0.7 collective-permute-start.2
  26.9 0.0 all-to-all-done.blocks
  26.9 1.4 %states.1 = (bf16[16,16,128]{2,1,0:T(8,128)(2,1)}, f32[8,16,128]{2,1,0:T(8,128)S(1)}) custom-call(s32[1]{0:T(128)S(6)} %add.6.member, bf16[8,2,128,128]{3,2,1,0:T(8,128)(2,1)S(1)} %all-to-all-done.blocks, f32[16,1024]{1,0:T(8,128)S(1)} %bitcast.20, bf16[2,32,1024]{2,1,0:T(8,128)(2,1)S(1)} %weights_pairs.1.after, bf16[32,1024]{1,0:T(8,128)(2,1)S(1)} %bitcast.28), custom_call_target="tpu_custom_call" | custom-call | tf_op jit(solution)/shard_map/states/pallas_call | solution.py:250
  28.3 12.3 %all-to-all-start.1 = ((bf16[16,16,128]{2,1,0:T(8,128)(2,1)}), bf16[16,16,128]{2,1,0:T(8,128)(2,1)S(1)}, u32[]{:S(2)}, u32[]{:S(2)}) async-start(bf16[16,16,128]{2,1,0:T(8,128)(2,1)} %get-tuple-element.9), calls=%async_computation.1 | async-start | bytes 131072 | tf_op jit(solution)/shard_map/states/all_to_all | solution.py:205
  40.7 0.0 collective-permute-done.1.after.other
  40.7 0.0 copy-done.3
  40.7 0.0 copy-start.5
  40.7 1.3 %local.1.after.y_tok = f32[1024,128]{1,0:T(8,128)S(1)} custom-call(s32[1]{0:T(128)S(6)} %add.6.member, bf16[8,2,128,128]{3,2,1,0:T(8,128)(2,1)S(1)} %all-to-all-done.blocks, f32[16,1024]{1,0:T(8,128)S(1)} %bitcast.21, f32[16,1024]{1,0:T(8,128)S(1)} %bitcast.23, bf16[2,32,1024]{2,1,0:T(8,128)(2,1)S(1)} %collective-permute-done.1.after.other), custom_call_target="tpu_custom_call" | custom-call | flops 2000000000 | tf_op jit(solution)/shard_map/local/pallas_call | solution.py:274
  42.0 0.0 collective-permute-done.2.own
  42.1 4.5 %collective-permute-start.3 = (bf16[4,32,1024]{2,1,0:T(8,128)(2,1)S(1)}, bf16[4,32,1024]{2,1,0:T(8,128)(2,1)S(1)}, u32[]{:S(2)}, u32[]{:S(2)}) collective-permute-start(bf16[4,32,1024]{2,1,0:T(8,128)(2,1)S(1)} %bitcast.14), channel_id=1, source_target_pairs={{0,384},{128,0},{256,128},{384,256},{1,385},{129,1},{257,129},{385... | collective-permute-start | bytes 786440 | tf_op jit(solution)/shard_map/weights/ppermute | solution.py:289
  46.6 2.5 %collective-permute-start.4 = (bf16[4,32,1024]{2,1,0:T(8,128)(2,1)S(1)}, bf16[4,32,1024]{2,1,0:T(8,128)(2,1)S(1)}, u32[]{:S(2)}, u32[]{:S(2)}) collective-permute-start(bf16[4,32,1024]{2,1,0:T(8,128)(2,1)S(1)} %bitcast.15), channel_id=1, source_target_pairs={{0,256},{128,384},{256,0},{384,128},{1,257},{129,385},{257,1},{385... | collective-permute-start | bytes 786440 | tf_op jit(solution)/shard_map/weights/ppermute | solution.py:289
  49.1 2.5 %collective-permute-start.5 = (bf16[4,32,1024]{2,1,0:T(8,128)(2,1)S(1)}, bf16[4,32,1024]{2,1,0:T(8,128)(2,1)S(1)}, u32[]{:S(2)}, u32[]{:S(2)}) collective-permute-start(bf16[4,32,1024]{2,1,0:T(8,128)(2,1)S(1)} %bitcast.16), channel_id=1, source_target_pairs={{0,128},{128,256},{256,384},{384,0},{1,129},{129,257},{257,385},{3... | collective-permute-start | bytes 786440 | tf_op jit(solution)/shard_map/weights/ppermute | solution.py:289
  51.6 3.2 %all-to-all-done.1.packs = bf16[16,16,128]{2,1,0:T(8,128)(2,1)S(1)} async-done(((bf16[16,16,128]{2,1,0:T(8,128)(2,1)}), bf16[16,16,128]{2,1,0:T(8,128)(2,1)S(1)}, u32[]{:S(2)}, u32[]{:S(2)}) %all-to-all-start.1) | async-done | bytes 65568 | tf_op jit(solution)/shard_map/states/all_to_all | solution.py:205
  54.7 2.3 %gate.1 = bf16[16,4,128,128]{3,2,1,0:T(8,128)(2,1)} custom-call(s32[1]{0:T(128)S(6)} %add.6.member, s32[1]{0:T(128)} %bitcast.2.group, bf16[16,16,128]{2,1,0:T(8,128)(2,1)S(1)} %all-to-all-done.1.packs, f32[8,16,128]{2,1,0:T(8,128)S(1)} %get-tuple-element.10.inside, f32[1024,128]{1,0:T(8,128)S(1)} %local.1.after.y_tok, ...), custom_call_target="tpu_custom_call" | custom-call | tf_op jit(solution)/shard_map/gate/pallas_call | solution.py:300
  57.0 5.7 %all-to-all-start.2 = ((bf16[16,4,128,128]{3,2,1,0:T(8,128)(2,1)}), bf16[16,4,128,128]{3,2,1,0:T(8,128)(2,1)S(1)}, u32[]{:S(2)}, u32[]{:S(2)}) async-start(bf16[16,4,128,128]{3,2,1,0:T(8,128)(2,1)} %gate.1), calls=%async_computation.2 | async-start | bytes 4194304 | tf_op jit(solution)/shard_map/gate/all_to_all | solution.py:205
  62.7 2.1 %collective-permute-start.6 = (bf16[4,32,1024]{2,1,0:T(8,128)(2,1)S(1)}, bf16[4,32,1024]{2,1,0:T(8,128)(2,1)S(1)}, u32[]{:S(2)}, u32[]{:S(2)}) collective-permute-start(bf16[4,32,1024]{2,1,0:T(8,128)(2,1)S(1)} %bitcast.18), channel_id=1, source_target_pairs={{0,4},{4,0},{1,5},{5,1},{2,6},{6,2},{3,7},{7,3},{8,12},{12,8},{9,1... | collective-permute-start | bytes 786440 | tf_op jit(solution)/shard_map/weights/ppermute | solution.py:292
  64.8 0.0 collective-permute-done.3.refs_1_
  64.8 2.2 %collective-permute-start.7 = (bf16[4,32,1024]{2,1,0:T(8,128)(2,1)S(1)}, bf16[4,32,1024]{2,1,0:T(8,128)(2,1)S(1)}, u32[]{:S(2)}, u32[]{:S(2)}) collective-permute-start(bf16[4,32,1024]{2,1,0:T(8,128)(2,1)S(1)} %collective-permute-done.3.refs_1_), channel_id=1, source_target_pairs={{0,4},{4,0},{1,5},{5,1},{2,6},{6,2},{3,7},{7,3},{8,12},{12,8},{9,1... | collective-permute-start | bytes 786440 | tf_op jit(solution)/shard_map/weights/ppermute | solution.py:292
  67.0 0.0 copy-start.6
  67.1 0.7 copy-done.6
  67.8 0.0 collective-permute-done.4.refs_2_
  67.8 2.1 %collective-permute-start.8 = (bf16[4,32,1024]{2,1,0:T(8,128)(2,1)S(1)}, bf16[4,32,1024]{2,1,0:T(8,128)(2,1)S(1)}, u32[]{:S(2)}, u32[]{:S(2)}) collective-permute-start(bf16[4,32,1024]{2,1,0:T(8,128)(2,1)S(1)} %collective-permute-done.4.refs_2_), channel_id=1, source_target_pairs={{0,4},{4,0},{1,5},{5,1},{2,6},{6,2},{3,7},{7,3},{8,12},{12,8},{9,1... | collective-permute-start | bytes 786440 | tf_op jit(solution)/shard_map/weights/ppermute | solution.py:292
  69.9 0.7 copy-done.8
  70.5 0.0 collective-permute-done.5.refs_3_
  70.5 2.2 %collective-permute-start.9 = (bf16[4,32,1024]{2,1,0:T(8,128)(2,1)S(1)}, bf16[4,32,1024]{2,1,0:T(8,128)(2,1)S(1)}, u32[]{:S(2)}, u32[]{:S(2)}) collective-permute-start(bf16[4,32,1024]{2,1,0:T(8,128)(2,1)S(1)} %collective-permute-done.5.refs_3_), channel_id=1, source_target_pairs={{0,4},{4,0},{1,5},{5,1},{2,6},{6,2},{3,7},{7,3},{8,12},{12,8},{9,1... | collective-permute-start | bytes 786440 | tf_op jit(solution)/shard_map/weights/ppermute | solution.py:292
  72.8 0.7 copy-done.10
  73.5 0.0 collective-permute-done.6.refs_4_
  73.5 0.0 collective-permute-done.7.refs_5_
  73.5 0.0 collective-permute-done.8.refs_6_
  73.5 0.5 collective-permute-done.9.refs_7_
  74.0 0.9 copy-done.7
  74.9 0.9 copy-done.9
  75.9 0.9 copy-done.11
  76.8 0.8 weights.1
  77.7 1.0 copy-done
  78.6 10.6 %all-to-all-done.2.gated = bf16[16,4,128,128]{3,2,1,0:T(8,128)(2,1)S(1)} async-done(((bf16[16,4,128,128]{3,2,1,0:T(8,128)(2,1)}), bf16[16,4,128,128]{3,2,1,0:T(8,128)(2,1)S(1)}, u32[]{:S(2)}, u32[]{:S(2)}) %all-to-all-start.2) | async-done | bytes 2097184 | tf_op jit(solution)/shard_map/gate/all_to_all | solution.py:205
  89.2 1.2 %copy-done.1 = bf16[2048,256]{1,0:T(8,128)(2,1)S(1)} copy-done((bf16[2048,256]{1,0:T(8,128)(2,1)S(1)}, bf16[2048,256]{1,0:T(8,128)(2,1)}, u32[]{:S(2)}) %copy-start.1) | copy-done | bytes 1048600
  90.4 1.3 %project.1 = bf16[4,2,128,256]{3,2,1,0:T(8,128)(2,1)S(1)} custom-call(bf16[16,4,128,128]{3,2,1,0:T(8,128)(2,1)S(1)} %all-to-all-done.2.gated, bf16[2048,256]{1,0:T(8,128)(2,1)S(1)} %get-tuple-element.11.w0, bf16[2048,256]{1,0:T(8,128)(2,1)S(1)} %copy-done.1), custom_call_target="tpu_custom_call" | custom-call | tf_op jit(solution)/shard_map/project/pallas_call | solution.py:308
  91.7 20.7 %all_to_all.20 = bf16[8,128,256]{2,1,0:T(8,128)(2,1)S(1)} all-to-all(bf16[8,128,256]{2,1,0:T(8,128)(2,1)S(1)} %bitcast.12), channel_id=1, replica_groups=mesh['x'=4,'zh'=4,'y'=4,'core'=2,'t1'=2,'t0'=2] {'y','t1'}, dimensions={0} | all-to-all | bytes 1048576 | tf_op jit(solution)/shard_map/reduce/all_to_all | solution.py:205
  112.4 1.0 reduce.1
  (12 shorter events, 0.1 us)
Async XLA Ops:
  0.0 17.2 %copy-start.4 = (bf16[1024,32]{0,1:T(8,128)(2,1)S(1)}, bf16[1024,32]{0,1:T(8,128)(2,1)}, u32[]{:S(2)}) copy-start(bf16[1024,32]{0,1:T(8,128)(2,1)} %param.13) | copy-start | bytes 196612
  0.0 17.2 %collective-permute-start = (bf16[32,1024]{1,0:T(8,128)(2,1)}, bf16[32,1024]{1,0:T(8,128)(2,1)S(1)}, u32[]{:S(2)}, u32[]{:S(2)}) collective-permute-start(bf16[32,1024]{1,0:T(8,128)(2,1)} %bitcast.25), channel_id=1, source_target_pairs={{0,32},{32,0},{64,96},{96,64},{1,33},{33,1},{65,97},{97,65},{2,34}... | collective-permute-start | bytes 196616 | tf_op jit(solution)/shard_map/weights_zh/ppermute | solution.py:241
  11.8 15.1 %all-to-all-start = ((bf16[8,2,128,128]{3,2,1,0:T(8,128)(2,1)}), bf16[8,2,128,128]{3,2,1,0:T(8,128)(2,1)S(1)}, u32[]{:S(2)}, u32[]{:S(2)}) async-start(bf16[8,2,128,128]{3,2,1,0:T(8,128)(2,1)} %prepare.1), calls=%async_computation | async-start | bytes 1048576 | tf_op jit(solution)/shard_map/prepare/all_to_all | solution.py:205
  17.2 9.7 %copy-start.2 = (f32[1024,16]{0,1:T(8,128)S(1)}, f32[1024,16]{0,1:T(8,128)}, u32[]{:S(2)}) copy-start(f32[1024,16]{0,1:T(8,128)} %param.11) | copy-start | bytes 196612
  17.2 23.5 %copy-start.3 = (f32[1024,16]{0,1:T(8,128)S(1)}, f32[1024,16]{0,1:T(8,128)}, u32[]{:S(2)}) copy-start(f32[1024,16]{0,1:T(8,128)} %param.10) | copy-start | bytes 196612
  17.3 23.4 %collective-permute-start.1 = (bf16[2,32,1024]{2,1,0:T(8,128)(2,1)S(1)}, bf16[2,32,1024]{2,1,0:T(8,128)(2,1)S(1)}, u32[]{:S(2)}, u32[]{:S(2)}) collective-permute-start(bf16[2,32,1024]{2,1,0:T(8,128)(2,1)S(1)} %weights_pairs.1.after), channel_id=1, source_target_pairs={{96,0},{224,1},{64,32},{192,33},{32,64},{160,65},{0,96},{128,97},{... | collective-permute-start | bytes 393224 | tf_op jit(solution)/shard_map/weights_quads/ppermute | solution.py:269
  26.2 15.8 %collective-permute-start.2 = (bf16[2,32,1024]{2,1,0:T(8,128)(2,1)S(1)}, bf16[2,32,1024]{2,1,0:T(8,128)(2,1)S(1)}, u32[]{:S(2)}, u32[]{:S(2)}) collective-permute-start(bf16[2,32,1024]{2,1,0:T(8,128)(2,1)S(1)} %weights_pairs.1.after), channel_id=1, source_target_pairs={{0,0},{128,1},{32,32},{160,33},{64,64},{192,65},{96,96},{224,97},{... | collective-permute-start | bytes 393224 | tf_op jit(solution)/shard_map/weights_quads/ppermute | solution.py:269
  28.3 26.4 %all-to-all-start.1 = ((bf16[16,16,128]{2,1,0:T(8,128)(2,1)}), bf16[16,16,128]{2,1,0:T(8,128)(2,1)S(1)}, u32[]{:S(2)}, u32[]{:S(2)}) async-start(bf16[16,16,128]{2,1,0:T(8,128)(2,1)} %get-tuple-element.9), calls=%async_computation.1 | async-start | bytes 131072 | tf_op jit(solution)/shard_map/states/all_to_all | solution.py:205
  40.7 14.0 %copy-start.5 = (f32[1024]{0:T(1024)S(1)}, f32[1024]{0:T(1024)}, u32[]{:S(2)}) copy-start(f32[1024]{0:T(1024)} %param.12) | copy-start | bytes 12292
  42.1 22.7 %collective-permute-start.3 = (bf16[4,32,1024]{2,1,0:T(8,128)(2,1)S(1)}, bf16[4,32,1024]{2,1,0:T(8,128)(2,1)S(1)}, u32[]{:S(2)}, u32[]{:S(2)}) collective-permute-start(bf16[4,32,1024]{2,1,0:T(8,128)(2,1)S(1)} %bitcast.14), channel_id=1, source_target_pairs={{0,384},{128,0},{256,128},{384,256},{1,385},{129,1},{257,129},{385... | collective-permute-start | bytes 786440 | tf_op jit(solution)/shard_map/weights/ppermute | solution.py:289
  46.6 21.2 %collective-permute-start.4 = (bf16[4,32,1024]{2,1,0:T(8,128)(2,1)S(1)}, bf16[4,32,1024]{2,1,0:T(8,128)(2,1)S(1)}, u32[]{:S(2)}, u32[]{:S(2)}) collective-permute-start(bf16[4,32,1024]{2,1,0:T(8,128)(2,1)S(1)} %bitcast.15), channel_id=1, source_target_pairs={{0,256},{128,384},{256,0},{384,128},{1,257},{129,385},{257,1},{385... | collective-permute-start | bytes 786440 | tf_op jit(solution)/shard_map/weights/ppermute | solution.py:289
  49.1 21.5 %collective-permute-start.5 = (bf16[4,32,1024]{2,1,0:T(8,128)(2,1)S(1)}, bf16[4,32,1024]{2,1,0:T(8,128)(2,1)S(1)}, u32[]{:S(2)}, u32[]{:S(2)}) collective-permute-start(bf16[4,32,1024]{2,1,0:T(8,128)(2,1)S(1)} %bitcast.16), channel_id=1, source_target_pairs={{0,128},{128,256},{256,384},{384,0},{1,129},{129,257},{257,385},{3... | collective-permute-start | bytes 786440 | tf_op jit(solution)/shard_map/weights/ppermute | solution.py:289
  57.0 32.2 %all-to-all-start.2 = ((bf16[16,4,128,128]{3,2,1,0:T(8,128)(2,1)}), bf16[16,4,128,128]{3,2,1,0:T(8,128)(2,1)S(1)}, u32[]{:S(2)}, u32[]{:S(2)}) async-start(bf16[16,4,128,128]{3,2,1,0:T(8,128)(2,1)} %gate.1), calls=%async_computation.2 | async-start | bytes 4194304 | tf_op jit(solution)/shard_map/gate/all_to_all | solution.py:205
  62.7 10.8 %collective-permute-start.6 = (bf16[4,32,1024]{2,1,0:T(8,128)(2,1)S(1)}, bf16[4,32,1024]{2,1,0:T(8,128)(2,1)S(1)}, u32[]{:S(2)}, u32[]{:S(2)}) collective-permute-start(bf16[4,32,1024]{2,1,0:T(8,128)(2,1)S(1)} %bitcast.18), channel_id=1, source_target_pairs={{0,4},{4,0},{1,5},{5,1},{2,6},{6,2},{3,7},{7,3},{8,12},{12,8},{9,1... | collective-permute-start | bytes 786440 | tf_op jit(solution)/shard_map/weights/ppermute | solution.py:292
  64.8 8.7 %collective-permute-start.7 = (bf16[4,32,1024]{2,1,0:T(8,128)(2,1)S(1)}, bf16[4,32,1024]{2,1,0:T(8,128)(2,1)S(1)}, u32[]{:S(2)}, u32[]{:S(2)}) collective-permute-start(bf16[4,32,1024]{2,1,0:T(8,128)(2,1)S(1)} %collective-permute-done.3.refs_1_), channel_id=1, source_target_pairs={{0,4},{4,0},{1,5},{5,1},{2,6},{6,2},{3,7},{7,3},{8,12},{12,8},{9,1... | collective-permute-start | bytes 786440 | tf_op jit(solution)/shard_map/weights/ppermute | solution.py:292
  67.0 0.7 copy-start.6
  67.8 5.7 %collective-permute-start.8 = (bf16[4,32,1024]{2,1,0:T(8,128)(2,1)S(1)}, bf16[4,32,1024]{2,1,0:T(8,128)(2,1)S(1)}, u32[]{:S(2)}, u32[]{:S(2)}) collective-permute-start(bf16[4,32,1024]{2,1,0:T(8,128)(2,1)S(1)} %collective-permute-done.4.refs_2_), channel_id=1, source_target_pairs={{0,4},{4,0},{1,5},{5,1},{2,6},{6,2},{3,7},{7,3},{8,12},{12,8},{9,1... | collective-permute-start | bytes 786440 | tf_op jit(solution)/shard_map/weights/ppermute | solution.py:292
  69.8 0.7 copy-start.8
  70.5 3.4 %collective-permute-start.9 = (bf16[4,32,1024]{2,1,0:T(8,128)(2,1)S(1)}, bf16[4,32,1024]{2,1,0:T(8,128)(2,1)S(1)}, u32[]{:S(2)}, u32[]{:S(2)}) collective-permute-start(bf16[4,32,1024]{2,1,0:T(8,128)(2,1)S(1)} %collective-permute-done.5.refs_3_), channel_id=1, source_target_pairs={{0,4},{4,0},{1,5},{5,1},{2,6},{6,2},{3,7},{7,3},{8,12},{12,8},{9,1... | collective-permute-start | bytes 786440 | tf_op jit(solution)/shard_map/weights/ppermute | solution.py:292
  72.8 0.7 copy-start.10
  74.0 1.0 copy-start.7
  74.9 0.9 copy-start.9
  75.9 0.9 copy-start.11
  77.6 1.0 copy-start
  89.2 1.2 %copy-start.1 = (bf16[2048,256]{1,0:T(8,128)(2,1)S(1)}, bf16[2048,256]{1,0:T(8,128)(2,1)}, u32[]{:S(2)}) copy-start(bf16[2048,256]{1,0:T(8,128)(2,1)} %copy-done) | copy-start | bytes 3145732

commit v9 on v7

--- a/solution.py
+++ b/solution.py
@@ -308,6 +308,7 @@
             dot_kernel,
             jax.ShapeDtypeStruct((4, 2, TOK, 256), BF16),
             [pltpu.VMEM((4 * TOK, 2 * CHANS), BF16)],
+            mib=50,
         )(gated, *w).reshape(8, TOK, 256)
     with jax.named_scope("reduce"):
         shares = exchange(shares, ("y", "t1")).reshape(4, 2, TOK, 256)

time: 114 us -> 115 us (level)
  local copies, waits for them, and re-layouts: 2.22 us -> 0.02 us
  Pallas kernels: 10.1 us -> 11.7 us
    unnamed x12 -> x8, local copies, waits for them, and re-layouts: 2.22 us -> 0.02 us
    pallas_call x1, Pallas kernels: 1.26 us -> 2.85 us  [per_device(): call(dot_kernel, jax.ShapeDtypeStruct((4, 2, TOK, 256), BF16), [pltpu.VME...]
where the time goes in v9:
time: 115 us
  starting transfers between devices  63.5 us (55%)
  blocking collectives  20.8 us (18%)
  waiting for transfers between devices  18.3 us (16%)
  Pallas kernels  11.7 us (10%)
    all_to_all x3, starting transfers between devices, exchange(): return lax.all_to_all(blocks, axis, split_axis=0, concat_axis=0, tiled=True)  24.3 us
    all_to_all x1, blocking collectives, exchange(): return lax.all_to_all(blocks, axis, split_axis=0, concat_axis=0, tiled=True)  20.8 us
    all_to_all x3, waiting for transfers between devices, exchange(): return lax.all_to_all(blocks, axis, split_axis=0, concat_axis=0, tiled=True)  14.7 us
    ppermute x4, starting transfers between devices, per_device(): other = [lax.ppermute(block, 'core', [(0, 1), (1, 0)]) for block in own]  12.1 us
    ppermute x1, starting transfers between devices, per_device(): w_near = lax.ppermute(w_t, 'zh', [(0, 1), (1, 0), (2, 3), (3, 2)])  9.77 us
    ppermute x2, starting transfers between devices, swapped(): return lax.ppermute(two, ('x', 'zh', 't0'), moves)  9.62 us
    ppermute x3, starting transfers between devices, per_device(): lax.ppermute(quarter, 'x', [(i, (i - k) % 4) for i in range(4)])  7.65 us
    pallas_call x1, Pallas kernels, per_device(): call(dot_kernel, jax.ShapeDtypeStruct((4, 2, TOK, 256), BF16), [pltpu.VME...  2.85 us
  transfers between devices with their start and end apart: 13, of which 6 were waited for; matrix products, arithmetic and copies ran while one was open for 0% of the time, Pallas kernels for 5%

profile of v9, /device:TPU:1, one launch (start us, length us, event | category | flops | bytes accessed | tf_op | source)
XLA Modules:
  0.0 114.5 jit_solution(5301309908312905573)
XLA Ops:
  0.0 0.0 copy-start.2
  0.0 9.8 %collective-permute-start = (bf16[32,1024]{1,0:T(8,128)(2,1)}, bf16[32,1024]{1,0:T(8,128)(2,1)S(1)}, u32[]{:S(2)}, u32[]{:S(2)}) collective-permute-start(bf16[32,1024]{1,0:T(8,128)(2,1)} %bitcast.25), channel_id=1, source_target_pairs={{0,32},{32,0},{64,96},{96,64},{1,33},{33,1},{65,97},{97,65},{2,34}... | collective-permute-start | bytes 196616 | tf_op jit(solution)/shard_map/weights_zh/ppermute | solution.py:241
  9.8 2.0 %prepare.1 = bf16[8,2,128,128]{3,2,1,0:T(8,128)(2,1)} custom-call(bf16[128,1024]{1,0:T(8,128)(2,1)} %keys_far.1, bf16[128,1024]{1,0:T(8,128)(2,1)} %values_far.1, bf16[128,1024]{1,0:T(8,128)(2,1)} %query_far.1), custom_call_target="tpu_custom_call" | custom-call | tf_op jit(solution)/shard_map/prepare/pallas_call | solution.py:231
  11.8 5.4 %all-to-all-start = ((bf16[8,2,128,128]{3,2,1,0:T(8,128)(2,1)}), bf16[8,2,128,128]{3,2,1,0:T(8,128)(2,1)S(1)}, u32[]{:S(2)}, u32[]{:S(2)}) async-start(bf16[8,2,128,128]{3,2,1,0:T(8,128)(2,1)} %prepare.1), calls=%async_computation | async-start | bytes 1048576 | tf_op jit(solution)/shard_map/prepare/all_to_all | solution.py:205
  17.2 0.0 collective-permute-done.other
  17.2 0.0 copy-done.2
  17.2 0.0 copy-start
  17.2 0.0 copy-start.1
  17.3 8.9 %collective-permute-start.1 = (bf16[2,32,1024]{2,1,0:T(8,128)(2,1)S(1)}, bf16[2,32,1024]{2,1,0:T(8,128)(2,1)S(1)}, u32[]{:S(2)}, u32[]{:S(2)}) collective-permute-start(bf16[2,32,1024]{2,1,0:T(8,128)(2,1)S(1)} %weights_pairs.1.after), channel_id=1, source_target_pairs={{96,0},{224,1},{64,32},{192,33},{32,64},{160,65},{0,96},{128,97},{... | collective-permute-start | bytes 393224 | tf_op jit(solution)/shard_map/weights_quads/ppermute | solution.py:269
  26.2 0.5 all-to-all-done.blocks
  26.7 0.0 copy-done
  26.7 1.4 %states.1 = (bf16[16,16,128]{2,1,0:T(8,128)(2,1)}, f32[8,16,128]{2,1,0:T(8,128)S(1)}) custom-call(s32[1]{0:T(128)S(6)} %add.6.member, bf16[8,2,128,128]{3,2,1,0:T(8,128)(2,1)S(1)} %all-to-all-done.blocks, f32[16,1024]{1,0:T(8,128)S(1)} %bitcast.20, bf16[2,32,1024]{2,1,0:T(8,128)(2,1)S(1)} %weights_pairs.1.after, bf16[32,1024]{1,0:T(8,128)(2,1)S(1)} %bitcast.28), custom_call_target="tpu_custom_call" | custom-call | tf_op jit(solution)/shard_map/states/pallas_call | solution.py:250
  28.1 12.6 %all-to-all-start.1 = ((bf16[16,16,128]{2,1,0:T(8,128)(2,1)}), bf16[16,16,128]{2,1,0:T(8,128)(2,1)S(1)}, u32[]{:S(2)}, u32[]{:S(2)}) async-start(bf16[16,16,128]{2,1,0:T(8,128)(2,1)} %get-tuple-element.9), calls=%async_computation.1 | async-start | bytes 131072 | tf_op jit(solution)/shard_map/states/all_to_all | solution.py:205
  40.7 0.7 collective-permute-start.2
  41.4 0.0 collective-permute-done.1.after.other
  41.4 0.0 copy-done.1
  41.4 0.0 copy-start.3
  41.4 1.3 %local.1.after.y_tok = f32[1024,128]{1,0:T(8,128)S(1)} custom-call(s32[1]{0:T(128)S(6)} %add.6.member, bf16[8,2,128,128]{3,2,1,0:T(8,128)(2,1)S(1)} %all-to-all-done.blocks, f32[16,1024]{1,0:T(8,128)S(1)} %bitcast.21, f32[16,1024]{1,0:T(8,128)S(1)} %bitcast.23, bf16[2,32,1024]{2,1,0:T(8,128)(2,1)S(1)} %collective-permute-done.1.after.other), custom_call_target="tpu_custom_call" | custom-call | flops 2000000000 | tf_op jit(solution)/shard_map/local/pallas_call | solution.py:274
  42.7 0.0 collective-permute-done.2.own
  42.8 11.9 %all-to-all-done.1.packs = bf16[16,16,128]{2,1,0:T(8,128)(2,1)S(1)} async-done(((bf16[16,16,128]{2,1,0:T(8,128)(2,1)}), bf16[16,16,128]{2,1,0:T(8,128)(2,1)S(1)}, u32[]{:S(2)}, u32[]{:S(2)}) %all-to-all-start.1) | async-done | bytes 65568 | tf_op jit(solution)/shard_map/states/all_to_all | solution.py:205
  54.7 0.0 copy-done.3
  54.7 2.3 %gate.1 = bf16[16,4,128,128]{3,2,1,0:T(8,128)(2,1)} custom-call(s32[1]{0:T(128)S(6)} %add.6.member, s32[1]{0:T(128)} %bitcast.2.group, bf16[16,16,128]{2,1,0:T(8,128)(2,1)S(1)} %all-to-all-done.1.packs, f32[8,16,128]{2,1,0:T(8,128)S(1)} %get-tuple-element.10.inside, f32[1024,128]{1,0:T(8,128)S(1)} %local.1.after.y_tok, ...), custom_call_target="tpu_custom_call" | custom-call | tf_op jit(solution)/shard_map/gate/pallas_call | solution.py:299
  57.0 6.3 %all-to-all-start.2 = ((bf16[16,4,128,128]{3,2,1,0:T(8,128)(2,1)}), bf16[16,4,128,128]{3,2,1,0:T(8,128)(2,1)}, u32[]{:S(2)}, u32[]{:S(2)}) async-start(bf16[16,4,128,128]{3,2,1,0:T(8,128)(2,1)} %gate.1), calls=%async_computation.2 | async-start | bytes 4194304 | tf_op jit(solution)/shard_map/gate/all_to_all | solution.py:205
  63.3 2.7 %collective-permute-start.3 = (bf16[4,32,1024]{2,1,0:T(8,128)(2,1)S(1)}, bf16[4,32,1024]{2,1,0:T(8,128)(2,1)S(1)}, u32[]{:S(2)}, u32[]{:S(2)}) collective-permute-start(bf16[4,32,1024]{2,1,0:T(8,128)(2,1)S(1)} %bitcast.13), channel_id=1, source_target_pairs={{0,384},{128,0},{256,128},{384,256},{1,385},{129,1},{257,129},{385... | collective-permute-start | bytes 786440 | tf_op jit(solution)/shard_map/weights/ppermute | solution.py:289
  66.0 3.0 %collective-permute-start.4 = (bf16[4,32,1024]{2,1,0:T(8,128)(2,1)S(1)}, bf16[4,32,1024]{2,1,0:T(8,128)(2,1)S(1)}, u32[]{:S(2)}, u32[]{:S(2)}) collective-permute-start(bf16[4,32,1024]{2,1,0:T(8,128)(2,1)S(1)} %bitcast.14), channel_id=1, source_target_pairs={{0,256},{128,384},{256,0},{384,128},{1,257},{129,385},{257,1},{385... | collective-permute-start | bytes 786440 | tf_op jit(solution)/shard_map/weights/ppermute | solution.py:289
  69.0 1.9 %collective-permute-start.5 = (bf16[4,32,1024]{2,1,0:T(8,128)(2,1)S(1)}, bf16[4,32,1024]{2,1,0:T(8,128)(2,1)S(1)}, u32[]{:S(2)}, u32[]{:S(2)}) collective-permute-start(bf16[4,32,1024]{2,1,0:T(8,128)(2,1)S(1)} %bitcast.15), channel_id=1, source_target_pairs={{0,128},{128,256},{256,384},{384,0},{1,129},{129,257},{257,385},{3... | collective-permute-start | bytes 786440 | tf_op jit(solution)/shard_map/weights/ppermute | solution.py:289
  70.9 2.8 %collective-permute-start.6 = (bf16[4,32,1024]{2,1,0:T(8,128)(2,1)S(1)}, bf16[4,32,1024]{2,1,0:T(8,128)(2,1)S(1)}, u32[]{:S(2)}, u32[]{:S(2)}) collective-permute-start(bf16[4,32,1024]{2,1,0:T(8,128)(2,1)S(1)} %bitcast.16), channel_id=1, source_target_pairs={{0,4},{4,0},{1,5},{5,1},{2,6},{6,2},{3,7},{7,3},{8,12},{12,8},{9,1... | collective-permute-start | bytes 786440 | tf_op jit(solution)/shard_map/weights/ppermute | solution.py:292
  73.7 0.0 collective-permute-done.3.refs_1_
  73.7 2.8 %collective-permute-start.7 = (bf16[4,32,1024]{2,1,0:T(8,128)(2,1)S(1)}, bf16[4,32,1024]{2,1,0:T(8,128)(2,1)S(1)}, u32[]{:S(2)}, u32[]{:S(2)}) collective-permute-start(bf16[4,32,1024]{2,1,0:T(8,128)(2,1)S(1)} %collective-permute-done.3.refs_1_), channel_id=1, source_target_pairs={{0,4},{4,0},{1,5},{5,1},{2,6},{6,2},{3,7},{7,3},{8,12},{12,8},{9,1... | collective-permute-start | bytes 786440 | tf_op jit(solution)/shard_map/weights/ppermute | solution.py:292
  76.5 0.3 collective-permute-done.4.refs_2_
  76.7 4.3 %collective-permute-start.8 = (bf16[4,32,1024]{2,1,0:T(8,128)(2,1)S(1)}, bf16[4,32,1024]{2,1,0:T(8,128)(2,1)S(1)}, u32[]{:S(2)}, u32[]{:S(2)}) collective-permute-start(bf16[4,32,1024]{2,1,0:T(8,128)(2,1)S(1)} %collective-permute-done.4.refs_2_), channel_id=1, source_target_pairs={{0,4},{4,0},{1,5},{5,1},{2,6},{6,2},{3,7},{7,3},{8,12},{12,8},{9,1... | collective-permute-start | bytes 786440 | tf_op jit(solution)/shard_map/weights/ppermute | solution.py:292
  81.1 2.3 %collective-permute-done.5.refs_3_ = bf16[4,32,1024]{2,1,0:T(8,128)(2,1)S(1)} collective-permute-done((bf16[4,32,1024]{2,1,0:T(8,128)(2,1)S(1)}, bf16[4,32,1024]{2,1,0:T(8,128)(2,1)S(1)}, u32[]{:S(2)}, u32[]{:S(2)}) %collective-permute-start.5) | collective-permute-done | bytes 262176 | tf_op jit(solution)/shard_map/weights/ppermute | solution.py:289
  83.4 2.3 %collective-permute-start.9 = (bf16[4,32,1024]{2,1,0:T(8,128)(2,1)S(1)}, bf16[4,32,1024]{2,1,0:T(8,128)(2,1)S(1)}, u32[]{:S(2)}, u32[]{:S(2)}) collective-permute-start(bf16[4,32,1024]{2,1,0:T(8,128)(2,1)S(1)} %collective-permute-done.5.refs_3_), channel_id=1, source_target_pairs={{0,4},{4,0},{1,5},{5,1},{2,6},{6,2},{3,7},{7,3},{8,12},{12,8},{9,1... | collective-permute-start | bytes 786440 | tf_op jit(solution)/shard_map/weights/ppermute | solution.py:292
  85.6 0.0 collective-permute-done.6.refs_4_
  85.7 0.0 collective-permute-done.7.refs_5_
  85.7 0.0 collective-permute-done.8.refs_6_
  85.7 1.1 collective-permute-done.9.refs_7_
  86.8 0.8 weights.1
  87.6 2.3 %all-to-all-done.2.gated = bf16[16,4,128,128]{3,2,1,0:T(8,128)(2,1)} async-done(((bf16[16,4,128,128]{3,2,1,0:T(8,128)(2,1)}), bf16[16,4,128,128]{3,2,1,0:T(8,128)(2,1)}, u32[]{:S(2)}, u32[]{:S(2)}) %all-to-all-start.2) | async-done | bytes 2097184 | tf_op jit(solution)/shard_map/gate/all_to_all | solution.py:205
  89.9 2.8 %project.1 = bf16[4,2,128,256]{3,2,1,0:T(8,128)(2,1)S(1)} custom-call(bf16[16,4,128,128]{3,2,1,0:T(8,128)(2,1)} %all-to-all-done.2.gated, bf16[2048,256]{1,0:T(8,128)(2,1)S(1)} %get-tuple-element.11.w0, bf16[2048,256]{1,0:T(8,128)(2,1)S(1)} %get-tuple-element.12.w1), custom_call_target="tpu_custom_call" | custom-call | tf_op jit(solution)/shard_map/project/pallas_call | solution.py:307
  92.8 20.8 %all_to_all.20 = bf16[8,128,256]{2,1,0:T(8,128)(2,1)S(1)} all-to-all(bf16[8,128,256]{2,1,0:T(8,128)(2,1)S(1)} %bitcast.18), channel_id=1, replica_groups=mesh['x'=4,'zh'=4,'y'=4,'core'=2,'t1'=2,'t0'=2] {'y','t1'}, dimensions={0} | all-to-all | bytes 1048576 | tf_op jit(solution)/shard_map/reduce/all_to_all | solution.py:205
  113.5 1.0 reduce.1
  (2 shorter events, 0.0 us)
Async XLA Ops:
  0.0 17.2 %copy-start.2 = (bf16[1024,32]{0,1:T(8,128)(2,1)S(1)}, bf16[1024,32]{0,1:T(8,128)(2,1)}, u32[]{:S(2)}) copy-start(bf16[1024,32]{0,1:T(8,128)(2,1)} %param.13) | copy-start | bytes 196612
  0.0 17.2 %collective-permute-start = (bf16[32,1024]{1,0:T(8,128)(2,1)}, bf16[32,1024]{1,0:T(8,128)(2,1)S(1)}, u32[]{:S(2)}, u32[]{:S(2)}) collective-permute-start(bf16[32,1024]{1,0:T(8,128)(2,1)} %bitcast.25), channel_id=1, source_target_pairs={{0,32},{32,0},{64,96},{96,64},{1,33},{33,1},{65,97},{97,65},{2,34}... | collective-permute-start | bytes 196616 | tf_op jit(solution)/shard_map/weights_zh/ppermute | solution.py:241
  11.8 14.9 %all-to-all-start = ((bf16[8,2,128,128]{3,2,1,0:T(8,128)(2,1)}), bf16[8,2,128,128]{3,2,1,0:T(8,128)(2,1)S(1)}, u32[]{:S(2)}, u32[]{:S(2)}) async-start(bf16[8,2,128,128]{3,2,1,0:T(8,128)(2,1)} %prepare.1), calls=%async_computation | async-start | bytes 1048576 | tf_op jit(solution)/shard_map/prepare/all_to_all | solution.py:205
  17.2 9.5 %copy-start = (f32[1024,16]{0,1:T(8,128)S(1)}, f32[1024,16]{0,1:T(8,128)}, u32[]{:S(2)}) copy-start(f32[1024,16]{0,1:T(8,128)} %param.11) | copy-start | bytes 196612
  17.2 24.1 %copy-start.1 = (f32[1024,16]{0,1:T(8,128)S(1)}, f32[1024,16]{0,1:T(8,128)}, u32[]{:S(2)}) copy-start(f32[1024,16]{0,1:T(8,128)} %param.10) | copy-start | bytes 196612
  17.3 24.1 %collective-permute-start.1 = (bf16[2,32,1024]{2,1,0:T(8,128)(2,1)S(1)}, bf16[2,32,1024]{2,1,0:T(8,128)(2,1)S(1)}, u32[]{:S(2)}, u32[]{:S(2)}) collective-permute-start(bf16[2,32,1024]{2,1,0:T(8,128)(2,1)S(1)} %weights_pairs.1.after), channel_id=1, source_target_pairs={{96,0},{224,1},{64,32},{192,33},{32,64},{160,65},{0,96},{128,97},{... | collective-permute-start | bytes 393224 | tf_op jit(solution)/shard_map/weights_quads/ppermute | solution.py:269
  28.1 26.6 %all-to-all-start.1 = ((bf16[16,16,128]{2,1,0:T(8,128)(2,1)}), bf16[16,16,128]{2,1,0:T(8,128)(2,1)S(1)}, u32[]{:S(2)}, u32[]{:S(2)}) async-start(bf16[16,16,128]{2,1,0:T(8,128)(2,1)} %get-tuple-element.9), calls=%async_computation.1 | async-start | bytes 131072 | tf_op jit(solution)/shard_map/states/all_to_all | solution.py:205
  40.7 2.0 %collective-permute-start.2 = (bf16[2,32,1024]{2,1,0:T(8,128)(2,1)S(1)}, bf16[2,32,1024]{2,1,0:T(8,128)(2,1)S(1)}, u32[]{:S(2)}, u32[]{:S(2)}) collective-permute-start(bf16[2,32,1024]{2,1,0:T(8,128)(2,1)S(1)} %weights_pairs.1.after), channel_id=1, source_target_pairs={{0,0},{128,1},{32,32},{160,33},{64,64},{192,65},{96,96},{224,97},{... | collective-permute-start | bytes 393224 | tf_op jit(solution)/shard_map/weights_quads/ppermute | solution.py:269
  41.4 13.3 %copy-start.3 = (f32[1024]{0:T(1024)S(1)}, f32[1024]{0:T(1024)}, u32[]{:S(2)}) copy-start(f32[1024]{0:T(1024)} %param.12) | copy-start | bytes 12292
  57.0 32.9 %all-to-all-start.2 = ((bf16[16,4,128,128]{3,2,1,0:T(8,128)(2,1)}), bf16[16,4,128,128]{3,2,1,0:T(8,128)(2,1)}, u32[]{:S(2)}, u32[]{:S(2)}) async-start(bf16[16,4,128,128]{3,2,1,0:T(8,128)(2,1)} %gate.1), calls=%async_computation.2 | async-start | bytes 4194304 | tf_op jit(solution)/shard_map/gate/all_to_all | solution.py:205
  63.3 10.4 %collective-permute-start.3 = (bf16[4,32,1024]{2,1,0:T(8,128)(2,1)S(1)}, bf16[4,32,1024]{2,1,0:T(8,128)(2,1)S(1)}, u32[]{:S(2)}, u32[]{:S(2)}) collective-permute-start(bf16[4,32,1024]{2,1,0:T(8,128)(2,1)S(1)} %bitcast.13), channel_id=1, source_target_pairs={{0,384},{128,0},{256,128},{384,256},{1,385},{129,1},{257,129},{385... | collective-permute-start | bytes 786440 | tf_op jit(solution)/shard_map/weights/ppermute | solution.py:289
  66.0 10.7 %collective-permute-start.4 = (bf16[4,32,1024]{2,1,0:T(8,128)(2,1)S(1)}, bf16[4,32,1024]{2,1,0:T(8,128)(2,1)S(1)}, u32[]{:S(2)}, u32[]{:S(2)}) collective-permute-start(bf16[4,32,1024]{2,1,0:T(8,128)(2,1)S(1)} %bitcast.14), channel_id=1, source_target_pairs={{0,256},{128,384},{256,0},{384,128},{1,257},{129,385},{257,1},{385... | collective-permute-start | bytes 786440 | tf_op jit(solution)/shard_map/weights/ppermute | solution.py:289
  69.0 14.4 %collective-permute-start.5 = (bf16[4,32,1024]{2,1,0:T(8,128)(2,1)S(1)}, bf16[4,32,1024]{2,1,0:T(8,128)(2,1)S(1)}, u32[]{:S(2)}, u32[]{:S(2)}) collective-permute-start(bf16[4,32,1024]{2,1,0:T(8,128)(2,1)S(1)} %bitcast.15), channel_id=1, source_target_pairs={{0,128},{128,256},{256,384},{384,0},{1,129},{129,257},{257,385},{3... | collective-permute-start | bytes 786440 | tf_op jit(solution)/shard_map/weights/ppermute | solution.py:289
  70.9 14.7 %collective-permute-start.6 = (bf16[4,32,1024]{2,1,0:T(8,128)(2,1)S(1)}, bf16[4,32,1024]{2,1,0:T(8,128)(2,1)S(1)}, u32[]{:S(2)}, u32[]{:S(2)}) collective-permute-start(bf16[4,32,1024]{2,1,0:T(8,128)(2,1)S(1)} %bitcast.16), channel_id=1, source_target_pairs={{0,4},{4,0},{1,5},{5,1},{2,6},{6,2},{3,7},{7,3},{8,12},{12,8},{9,1... | collective-permute-start | bytes 786440 | tf_op jit(solution)/shard_map/weights/ppermute | solution.py:292
  73.7 12.0 %collective-permute-start.7 = (bf16[4,32,1024]{2,1,0:T(8,128)(2,1)S(1)}, bf16[4,32,1024]{2,1,0:T(8,128)(2,1)S(1)}, u32[]{:S(2)}, u32[]{:S(2)}) collective-permute-start(bf16[4,32,1024]{2,1,0:T(8,128)(2,1)S(1)} %collective-permute-done.3.refs_1_), channel_id=1, source_target_pairs={{0,4},{4,0},{1,5},{5,1},{2,6},{6,2},{3,7},{7,3},{8,12},{12,8},{9,1... | collective-permute-start | bytes 786440 | tf_op jit(solution)/shard_map/weights/ppermute | solution.py:292
  76.7 8.9 %collective-permute-start.8 = (bf16[4,32,1024]{2,1,0:T(8,128)(2,1)S(1)}, bf16[4,32,1024]{2,1,0:T(8,128)(2,1)S(1)}, u32[]{:S(2)}, u32[]{:S(2)}) collective-permute-start(bf16[4,32,1024]{2,1,0:T(8,128)(2,1)S(1)} %collective-permute-done.4.refs_2_), channel_id=1, source_target_pairs={{0,4},{4,0},{1,5},{5,1},{2,6},{6,2},{3,7},{7,3},{8,12},{12,8},{9,1... | collective-permute-start | bytes 786440 | tf_op jit(solution)/shard_map/weights/ppermute | solution.py:292
  83.4 3.4 %collective-permute-start.9 = (bf16[4,32,1024]{2,1,0:T(8,128)(2,1)S(1)}, bf16[4,32,1024]{2,1,0:T(8,128)(2,1)S(1)}, u32[]{:S(2)}, u32[]{:S(2)}) collective-permute-start(bf16[4,32,1024]{2,1,0:T(8,128)(2,1)S(1)} %collective-permute-done.5.refs_3_), channel_id=1, source_target_pairs={{0,4},{4,0},{1,5},{5,1},{2,6},{6,2},{3,7},{7,3},{8,12},{12,8},{9,1... | collective-permute-start | bytes 786440 | tf_op jit(solution)/shard_map/weights/ppermute | solution.py:292
